TPU v7x, 32 devices: a whole 2x2x4 slice. The times are simulated.
32 devices in a mesh: groups: 2 (over y), tm: 4 (over z), dp: 4 (over x, core).
Axes of the slice: x: 2, y: 2, z: 4, core: 2. Of those that a mesh axis runs over, the one named last changes fastest.
Arguments:
- clips: bfloat16 [8, 8, 8, 32, 384], P(('groups', 'dp'), 'tm'), parts along dimension 0, may hold values from -16 to 16
- cotangent: bfloat16 [8, 8, 8, 32, 384], P(('groups', 'dp'), 'tm'), parts along dimension 0, may hold values from -6 to 6
- spatial_kernel: float32 [7, 7, 384], replicated, may hold values from -0.875 to 0.875
- temporal_kernel: float32 [31, 384], replicated, may hold values from -1 to 1
- norm_gain: float32 [384], replicated, may hold values from 0.1 to 1.9
- w_expand: bfloat16 [384, 1536], replicated, may hold values from -0.3125 to 0.3125
- w_project: bfloat16 [1536, 384], replicated, may hold values from -0.15625 to 0.15625
Outputs:
- block_out: bfloat16 [8, 8, 8, 32, 384], P(('groups', 'dp'), 'tm'), parts along dimension 0
- grad_clips: bfloat16 [8, 8, 8, 32, 384], P(('groups', 'dp'), 'tm'), parts along dimension 0
- grad_expand: float32 [3072, 384], P(('groups', 'tm', 'dp')), parts along dimension 0
There are 2 independent parts, one for each index of `groups`. A program takes and returns all parts, laid end to end along the dimension named above; an argument that names none is the same for every part. Nothing has to cross between parts.
All inputs are finite; a program needn't handle non-finite values.
Results may differ from a plain program's by a relative error of at most 0.0077.
Values may be sent and summed in bfloat16 or wider, within the bound.
No kernel may reach another device: no remote copies, remote signals or barrier semaphores. Data moves between devices by JAX's collectives and lax.ppermute only.
A program may use at most 64 MiB of HBM per device.

v0:
```python
import jax
import jax.numpy as jnp
from jax import lax
from jax.sharding import PartitionSpec as P


def spatial_pass(values, kernel, flip):
    radius = kernel.shape[0] // 2
    height = values.shape[-3]
    width = values.shape[-2]
    row_axis = values.ndim - 3
    col_axis = values.ndim - 2
    pads = [(0, 0)] * (values.ndim - 3) + [(radius, radius), (radius, radius), (0, 0)]
    padded = jnp.pad(values, pads)
    summed = jnp.zeros(values.shape, jnp.float32)
    for row_off in range(kernel.shape[0]):
        for col_off in range(kernel.shape[1]):
            first_row = 2 * radius - row_off if flip else row_off
            first_col = 2 * radius - col_off if flip else col_off
            window = lax.slice_in_dim(padded, first_row, first_row + height, axis=row_axis)
            window = lax.slice_in_dim(window, first_col, first_col + width, axis=col_axis)
            summed = summed + kernel[row_off, col_off] * window
    return summed


def time_pass(values, kernel, time_axis, flip):
    radius = kernel.shape[0] // 2
    length = values.shape[time_axis]
    pads = [(0, 0)] * values.ndim
    pads[time_axis] = (radius, radius)
    padded = jnp.pad(values, pads)
    summed = jnp.zeros(values.shape, jnp.float32)
    for lag_index in range(kernel.shape[0]):
        first_pos = 2 * radius - lag_index if flip else lag_index
        summed = summed + kernel[lag_index] * lax.slice_in_dim(
            padded, first_pos, first_pos + length, axis=time_axis
        )
    return summed


def gelu_value(preact):
    return 0.5 * preact * (1.0 + lax.erf(preact * 0.7071067811865476))


def gelu_slope(preact):
    return (
        0.5 * (1.0 + lax.erf(preact * 0.7071067811865476))
        + preact * jnp.exp(-0.5 * preact * preact) * 0.3989422804014327
    )


def token_block(tokens, grads, norm_gain, w_expand, w_project):
    values = tokens.astype(jnp.float32)
    average = jnp.mean(values, axis=-1, keepdims=True)
    centred = values - average
    inv_std = lax.rsqrt(jnp.mean(centred * centred, axis=-1, keepdims=True) + 1e-06)
    normed = centred * inv_std
    scaled = (normed * norm_gain).astype(jnp.bfloat16)
    preact = jnp.dot(scaled, w_expand, preferred_element_type=jnp.float32)
    hidden = gelu_value(preact).astype(jnp.bfloat16)
    branch = jnp.dot(hidden, w_project, preferred_element_type=jnp.float32).astype(jnp.bfloat16)
    d_hidden = jnp.dot(grads, w_project.T, preferred_element_type=jnp.float32)
    d_pre = (d_hidden * gelu_slope(preact)).astype(jnp.bfloat16)
    d_scaled = jnp.dot(d_pre, w_expand.T, preferred_element_type=jnp.float32)
    contrib = lax.psum_scatter(
        lax.dot_general(
            d_pre, scaled, (((0,), (0,)), ((), ())), preferred_element_type=jnp.float32
        ),
        ("tm", "dp"),
        scatter_dimension=0,
        tiled=True,
    )
    d_normed = d_scaled * norm_gain
    d_tokens = inv_std * (
        d_normed
        - jnp.mean(d_normed, axis=-1, keepdims=True)
        - normed * jnp.mean(d_normed * normed, axis=-1, keepdims=True)
    )
    return (branch, d_tokens.astype(jnp.bfloat16), contrib)


def local(clips, cotangent, spatial_kernel, temporal_kernel, norm_gain, w_expand, w_project):
    shape = clips.shape
    channels = shape[4]
    pixels = shape[2] * shape[3]
    flat_shape = (shape[0], shape[1], pixels, channels)
    device_count = lax.axis_size("tm") * lax.axis_size("dp")
    scale_factor = float(shape[0] * shape[1] * pixels * device_count) ** (-0.5)
    first = (
        spatial_pass(clips.astype(jnp.float32), spatial_kernel, False)
        .astype(jnp.bfloat16)
        .reshape(flat_shape)
    )
    tiles = lax.all_to_all(first, "tm", split_axis=2, concat_axis=1, tiled=True)
    second_tiles = time_pass(tiles.astype(jnp.float32), temporal_kernel, 1, False).astype(
        jnp.bfloat16
    )
    second = lax.all_to_all(second_tiles, "tm", split_axis=1, concat_axis=2, tiled=True)
    branch, d_tokens, contrib = token_block(
        second.reshape(-1, channels),
        cotangent.reshape(-1, channels),
        norm_gain,
        w_expand,
        w_project,
    )
    branch_frames = branch.reshape(shape)
    d_second = lax.all_to_all(
        d_tokens.reshape(flat_shape), "tm", split_axis=2, concat_axis=1, tiled=True
    )
    d_first_tiles = time_pass(d_second.astype(jnp.float32), temporal_kernel, 1, True).astype(
        jnp.bfloat16
    )
    d_first = lax.all_to_all(d_first_tiles, "tm", split_axis=1, concat_axis=2, tiled=True)
    block_out = (clips.astype(jnp.float32) + branch_frames.astype(jnp.float32)).astype(jnp.bfloat16)
    grad_clips = (
        cotangent.astype(jnp.float32)
        + spatial_pass(d_first.reshape(shape).astype(jnp.float32), spatial_kernel, True)
    ).astype(jnp.bfloat16)
    return (block_out, grad_clips, contrib * scale_factor)


def solution(mesh):
    in_specs = (
        P(("groups", "dp"), "tm", None, None, None),
        P(("groups", "dp"), "tm", None, None, None),
        P(),
        P(),
        P(),
        P(),
        P(),
    )
    out_specs = (
        P(("groups", "dp"), "tm", None, None, None),
        P(("groups", "dp"), "tm", None, None, None),
        P(("groups", "tm", "dp"), None),
    )
    return jax.shard_map(local, mesh=mesh, in_specs=in_specs, out_specs=out_specs, check_vma=False)
```

profile of v0, /device:TPU:0, one launch (start us, length us, event | category | flops | bytes accessed | tf_op | source)
XLA Modules:
  0.0 130.2 jit_solution(12538282292803020163)
XLA Ops:
  7.2 0.0 copy-start
  7.2 1.0 slice_reduce_fusion.60
  8.2 1.3 slice_reduce_fusion.62
  9.7 1.8 %slice_reduce_fusion.61 = (f32[384]{0:T(512)S(1)}, f32[384]{0:T(512)S(1)}, f32[384]{0:T(512)S(1)}, f32[384]{0:T(512)S(1)}, f32[384]{0:T(512)S(1)}, /*index=5*/f3...) fusion(f32[7,7,384]{2,1,0:T(8,128)} %param.9), kind=kLoop, calls=%fused_computation.482 | loop fusion | bytes 58368 | tf_op jit(solution)/shard_map/slice | solution.py:22
  11.6 1.1 convert_element_type.146
  12.7 5.6 %fusion.101 = bf16[1,2,8,32,384]{4,3,2,1,0:T(8,128)(2,1)S(1)} fusion(f32[1,2,8,32,384]{4,3,2,1,0:T(8,128)S(1)} %convert_element_type.146, f32[384]{0:T(512)S(1)} %get-tuple-element.52, f32[384]{0:T(512)S(1)} %get-tuple-element.53, f32[384]{0:T(512)S(1)} %get-tuple-element.6, f32[384]{0:T(512)S(1)} %get-tuple-element.7, f32[384]{0:T(512)S(1)} %get-tuple-element.8, ...), kind=kLoop, calls=%fused_computation.230 | loop fusion | flops 19267584 | bytes 1254912 | tf_op jit(solution)/shard_map/convert_element_type | solution.py:91
  18.3 1.2 copy.30
  19.5 6.3 %all-to-all-start = ((bf16[1,2,256,384]{3,1,0,2:T(2,128)(2,1)}), bf16[1,2,256,384]{3,1,0,2:T(2,128)(2,1)S(1)}, u32[]{:S(2)}, u32[]{:S(2)}) async-start(bf16[1,2,256,384]{3,1,0,2:T(2,128)(2,1)} %copy.30), calls=%async_computation | async-start | bytes 786432 | tf_op jit(solution)/shard_map/all_to_all | solution.py:94
  25.8 0.7 slice_reduce_fusion.63
  26.5 0.7 multiply_reduce_fusion.2
  27.1 10.3 %all-to-all-done = bf16[1,2,256,384]{3,1,0,2:T(2,128)(2,1)S(1)} async-done(((bf16[1,2,256,384]{3,1,0,2:T(2,128)(2,1)}), bf16[1,2,256,384]{3,1,0,2:T(2,128)(2,1)S(1)}, u32[]{:S(2)}, u32[]{:S(2)}) %all-to-all-start) | async-done | bytes 393248 | tf_op jit(solution)/shard_map/all_to_all | solution.py:94
  37.5 0.1 convert_bitcast_fusion.2
  37.7 0.1 copy.32
  38.0 0.0 copy-start.87
  38.1 1.6 %fusion.264 = bf16[1,8,64,384]{3,2,0,1:T(8,128)(2,1)S(1)} fusion(f32[384]{0:T(512)} %get-tuple-element.76, f32[384]{0:T(512)} %get-tuple-element.77, f32[384]{0:T(512)} %get-tuple-element.69, f32[384]{0:T(512)} %get-tuple-element.70, f32[384]{0:T(512)} %get-tuple-element.71, f32[384]{0:T(512)} %get-tuple-element.72, f32[384]{0:T(512)} %get-tuple-element.73, ...), kind=kLoop, calls=%fused_computation.405 | loop fusion | flops 7667712 | bytes 1216512 | tf_op jit(solution)/shard_map/convert_element_type | solution.py:95
  39.7 13.3 %all_to_all.16 = bf16[1,8,64,384]{3,2,0,1:T(8,128)(2,1)S(1)} all-to-all(bf16[1,8,64,384]{3,2,0,1:T(8,128)(2,1)S(1)} %fusion.264), channel_id=1, replica_groups=mesh['groups'=2,'tm'=4,'dp'=4] {'tm'}, dimensions={1} | all-to-all | bytes 786432 | tf_op jit(solution)/shard_map/all_to_all | solution.py:98
  53.0 0.2 fusion.263
  53.1 0.1 div.15
  53.2 0.1 convert_bitcast_fusion.3
  53.3 0.3 multiply_reduce_fusion.1
  53.6 0.1 rsqrt.12
  53.7 0.1 copy.35
  53.8 0.2 multiply_convert_fusion.5
  54.0 0.0 copy-start.3
  54.0 0.0 copy-start.88
  54.0 1.0 fusion.270
  55.0 0.4 copy-done.88
  55.4 1.6 %fusion.4 = bf16[512,1536]{1,0:T(8,128)(2,1)S(1)} fusion(f32[512,1536]{1,0:T(8,128)S(1)} %fusion.270, bf16[512,384]{1,0:T(8,128)(2,1)S(1)} %bitcast.66, bf16[1536,384]{1,0:T(8,128)(2,1)S(1)} %copy-done.88), kind=kOutput, calls=%fused_computation.132 | convolution fusion | flops 611844096 | bytes 6291456 | tf_op jit(solution)/shard_map/dot_general | solution.py:62
  57.0 2.5 %fusion.271 = f32[1536,384]{1,0:T(8,128)} fusion(bf16[512,1536]{1,0:T(8,128)(2,1)S(1)} %fusion.4, bf16[512,384]{1,0:T(8,128)(2,1)S(1)} %multiply_convert_fusion.5), kind=kOutput, calls=%fused_computation.490 | convolution fusion | flops 603979776 | bytes 4325376 | tf_op jit(solution)/shard_map/dot_general | solution.py:66
  59.5 0.0 reduce-scatter.2.cloned.1.call-update
  59.5 0.0 copy-start.86
  59.6 1.9 %fusion.269 = (f32[512]{0:T(512)S(1)}, f32[512]{0:T(512)S(1)}, f32[512,384]{1,0:T(8,128)S(1)}) fusion(f32[512]{0:T(512)} %copy-done.85, f32[512]{0:T(512)} %copy-done.83, f32[1,2,4,64,384]{4,3,2,1,0:T(8,128)S(1)} %copy.35, f32[384]{0:T(512)} %param.11, bf16[512,1536]{1,0:T(8,128)(2,1)S(1)} %fusion.4, bf16[384,1536]{1,0:T(8,128)(2,1)S(1)} %copy-done), kind=kOutput, calls=%fused_computation.488 | convolution fusion | flops 605158400 | bytes 4335104 | tf_op jit(solution)/shard_map/dot_general | solution.py:64
  61.4 0.3 multiply_convert_fusion.4
  61.8 0.4 copy.39
  62.2 0.0 copy-start.89
  62.2 13.6 %all_to_all.17 = bf16[1,2,256,384]{3,1,0,2:T(2,128)(2,1)S(1)} all-to-all(bf16[1,2,256,384]{3,1,0,2:T(2,128)(2,1)S(1)} %copy.39), channel_id=1, replica_groups=mesh['groups'=2,'tm'=4,'dp'=4] {'tm'}, dimensions={2} | all-to-all | bytes 786432 | tf_op jit(solution)/shard_map/all_to_all | solution.py:107
  75.9 0.1 convert_bitcast_fusion.1
  76.0 0.1 copy.41
  76.0 2.4 %fusion.265 = bf16[1,8,64,384]{3,2,0,1:T(8,128)(2,1)} fusion(f32[384]{0:T(512)} %get-tuple-element.76, f32[384]{0:T(512)} %get-tuple-element.77, f32[384]{0:T(512)} %get-tuple-element.69, f32[384]{0:T(512)} %get-tuple-element.70, f32[384]{0:T(512)} %get-tuple-element.71, f32[384]{0:T(512)} %get-tuple-element.72, f32[384]{0:T(512)} %get-tuple-element.73, ...), kind=kLoop, calls=%fused_computation.406 | loop fusion | flops 7667712 | bytes 1216512 | tf_op jit(solution)/shard_map/convert_element_type | solution.py:110
  78.4 3.6 %all-to-all-start.3 = ((bf16[1,8,64,384]{3,2,0,1:T(8,128)(2,1)}), bf16[1,8,64,384]{3,2,0,1:T(8,128)(2,1)S(1)}, u32[]{:S(2)}, u32[]{:S(2)}) async-start(bf16[1,8,64,384]{3,2,0,1:T(8,128)(2,1)} %fusion.265), calls=%async_computation.3 | async-start | bytes 786432 | tf_op jit(solution)/shard_map/all_to_all | solution.py:113
  82.1 2.9 %fusion.7 = bf16[512,384]{1,0:T(8,128)(2,1)S(1)} fusion(bf16[1536,384]{1,0:T(8,128)(2,1)S(1)} %copy-done.89, f32[512,1536]{1,0:T(8,128)} %copy-done.1), kind=kOutput, calls=%fused_computation.136 | convolution fusion | flops 608108544 | bytes 4718592 | tf_op jit(solution)/shard_map/dot_general | solution.py:61
  85.4 0.8 fusion.261
  86.2 10.2 %all-to-all-done.3 = bf16[1,8,64,384]{3,2,0,1:T(8,128)(2,1)S(1)} async-done(((bf16[1,8,64,384]{3,2,0,1:T(8,128)(2,1)}), bf16[1,8,64,384]{3,2,0,1:T(8,128)(2,1)S(1)}, u32[]{:S(2)}, u32[]{:S(2)}) %all-to-all-start.3) | async-done | bytes 393248 | tf_op jit(solution)/shard_map/all_to_all | solution.py:113
  96.4 0.1 convert_bitcast_fusion
  96.5 0.1 copy.44
  96.9 6.1 %fusion.199 = bf16[1,2,8,32,384]{4,3,2,1,0:T(8,128)(2,1)} fusion(f32[1,2,8,32,384]{4,3,2,1,0:T(8,128)S(1)} %bitcast.58, bf16[1,2,8,32,384]{4,3,2,1,0:T(8,128)(2,1)S(1)} %copy-done.4, f32[384]{0:T(512)S(1)} %copy-done.17, f32[384]{0:T(512)S(1)} %copy-done.19, f32[384]{0:T(512)S(1)} %copy-done.23, f32[384]{0:T(512)S(1)} %copy-done.25, f32[384]{0:T(512)S(1)} %copy-done.27, ...), kind=kLoop, calls=%fused_computation.328 | loop fusion | flops 19660800 | bytes 1648128 | tf_op jit(solution)/shard_map/convert_element_type | solution.py:118
  103.1 18.7 %reduce-scatter.2.cloned.1.call-done = f32[96,384]{1,0:T(8,128)} async-done(((f32[1536,384]{1,0:T(8,128)}), f32[96,384]{1,0:T(8,128)}) %reduce-scatter.2.cloned.1.call-update) | async-done | bytes 147472 | tf_op jit(solution)/shard_map/reduce_scatter | solution.py:65
  121.7 1.6 %broadcast_multiply_fusion = f32[96,384]{1,0:T(8,128)} fusion(f32[96,384]{1,0:T(8,128)} %reduce-scatter.2.cloned.1.call-done), kind=kLoop, calls=%fused_computation.407 | loop fusion | flops 36864 | bytes 294912 | tf_op jit(solution)/shard_map/mul | solution.py:119
  (180 shorter events, 0.5 us)
Async XLA Ops:
  7.2 46.8 %copy-start = (bf16[384,1536]{1,0:T(8,128)(2,1)S(1)}, bf16[384,1536]{1,0:T(8,128)(2,1)}, u32[]{:S(2)}) copy-start(bf16[384,1536]{1,0:T(8,128)(2,1)} %param.12) | copy-start | bytes 3538948
  7.2 18.6 %copy-start.5 = (f32[31,384]{1,0:T(8,128)S(1)}, f32[31,384]{1,0:T(8,128)}, u32[]{:S(2)}) copy-start(f32[31,384]{1,0:T(8,128)} %param.10) | copy-start | bytes 142852
  8.2 29.4 %copy-start.6 = (f32[384]{0:T(512)}, f32[384]{0:T(512)S(1)}, u32[]{:S(2)}) copy-start(f32[384]{0:T(512)S(1)} %get-tuple-element.47) | copy-start | bytes 4612
  8.2 29.4 %copy-start.8 = (f32[384]{0:T(512)}, f32[384]{0:T(512)S(1)}, u32[]{:S(2)}) copy-start(f32[384]{0:T(512)S(1)} %get-tuple-element.48) | copy-start | bytes 4612
  8.2 29.4 %copy-start.10 = (f32[384]{0:T(512)}, f32[384]{0:T(512)S(1)}, u32[]{:S(2)}) copy-start(f32[384]{0:T(512)S(1)} %get-tuple-element.49) | copy-start | bytes 4612
  8.2 29.4 %copy-start.12 = (f32[384]{0:T(512)}, f32[384]{0:T(512)S(1)}, u32[]{:S(2)}) copy-start(f32[384]{0:T(512)S(1)} %get-tuple-element.50) | copy-start | bytes 4612
  8.2 29.4 %copy-start.14 = (f32[384]{0:T(512)}, f32[384]{0:T(512)S(1)}, u32[]{:S(2)}) copy-start(f32[384]{0:T(512)S(1)} %get-tuple-element.51) | copy-start | bytes 4612
  8.2 29.4 %copy-start.16 = (f32[384]{0:T(512)}, f32[384]{0:T(512)S(1)}, u32[]{:S(2)}) copy-start(f32[384]{0:T(512)S(1)} %get-tuple-element.52) | copy-start | bytes 4612
  8.2 29.4 %copy-start.18 = (f32[384]{0:T(512)}, f32[384]{0:T(512)S(1)}, u32[]{:S(2)}) copy-start(f32[384]{0:T(512)S(1)} %get-tuple-element.53) | copy-start | bytes 4612
  9.5 28.2 %copy-start.20 = (f32[384]{0:T(512)}, f32[384]{0:T(512)S(1)}, u32[]{:S(2)}) copy-start(f32[384]{0:T(512)S(1)} %get-tuple-element.5) | copy-start | bytes 4612
  9.5 28.2 %copy-start.22 = (f32[384]{0:T(512)}, f32[384]{0:T(512)S(1)}, u32[]{:S(2)}) copy-start(f32[384]{0:T(512)S(1)} %get-tuple-element.6) | copy-start | bytes 4612
  9.5 28.2 %copy-start.24 = (f32[384]{0:T(512)}, f32[384]{0:T(512)S(1)}, u32[]{:S(2)}) copy-start(f32[384]{0:T(512)S(1)} %get-tuple-element.7) | copy-start | bytes 4612
  9.6 28.2 %copy-start.26 = (f32[384]{0:T(512)}, f32[384]{0:T(512)S(1)}, u32[]{:S(2)}) copy-start(f32[384]{0:T(512)S(1)} %get-tuple-element.8) | copy-start | bytes 4612
  9.6 28.2 %copy-start.28 = (f32[384]{0:T(512)}, f32[384]{0:T(512)S(1)}, u32[]{:S(2)}) copy-start(f32[384]{0:T(512)S(1)} %get-tuple-element.9) | copy-start | bytes 4612
  9.6 28.2 %copy-start.30 = (f32[384]{0:T(512)}, f32[384]{0:T(512)S(1)}, u32[]{:S(2)}) copy-start(f32[384]{0:T(512)S(1)} %get-tuple-element.10) | copy-start | bytes 4612
  9.6 28.2 %copy-start.32 = (f32[384]{0:T(512)}, f32[384]{0:T(512)S(1)}, u32[]{:S(2)}) copy-start(f32[384]{0:T(512)S(1)} %get-tuple-element.11) | copy-start | bytes 4612
  9.6 28.2 %copy-start.34 = (f32[384]{0:T(512)}, f32[384]{0:T(512)S(1)}, u32[]{:S(2)}) copy-start(f32[384]{0:T(512)S(1)} %get-tuple-element.12) | copy-start | bytes 4612
  9.6 28.2 %copy-start.36 = (f32[384]{0:T(512)}, f32[384]{0:T(512)S(1)}, u32[]{:S(2)}) copy-start(f32[384]{0:T(512)S(1)} %get-tuple-element.13) | copy-start | bytes 4612
  9.6 28.2 %copy-start.38 = (f32[384]{0:T(512)}, f32[384]{0:T(512)S(1)}, u32[]{:S(2)}) copy-start(f32[384]{0:T(512)S(1)} %get-tuple-element.14) | copy-start | bytes 4612
  9.6 28.2 %copy-start.40 = (f32[384]{0:T(512)}, f32[384]{0:T(512)S(1)}, u32[]{:S(2)}) copy-start(f32[384]{0:T(512)S(1)} %get-tuple-element.15) | copy-start | bytes 4612
  9.6 28.2 %copy-start.42 = (f32[384]{0:T(512)}, f32[384]{0:T(512)S(1)}, u32[]{:S(2)}) copy-start(f32[384]{0:T(512)S(1)} %get-tuple-element.16) | copy-start | bytes 4612
  9.6 28.2 %copy-start.44 = (f32[384]{0:T(512)}, f32[384]{0:T(512)S(1)}, u32[]{:S(2)}) copy-start(f32[384]{0:T(512)S(1)} %get-tuple-element.17) | copy-start | bytes 4612
  9.7 28.2 %copy-start.46 = (f32[384]{0:T(512)}, f32[384]{0:T(512)S(1)}, u32[]{:S(2)}) copy-start(f32[384]{0:T(512)S(1)} %get-tuple-element.18) | copy-start | bytes 4612
  9.7 28.2 %copy-start.48 = (f32[384]{0:T(512)}, f32[384]{0:T(512)S(1)}, u32[]{:S(2)}) copy-start(f32[384]{0:T(512)S(1)} %get-tuple-element.19) | copy-start | bytes 4612
  9.7 28.2 %copy-start.50 = (f32[384]{0:T(512)}, f32[384]{0:T(512)S(1)}, u32[]{:S(2)}) copy-start(f32[384]{0:T(512)S(1)} %get-tuple-element.20) | copy-start | bytes 4612
  9.7 28.2 %copy-start.52 = (f32[384]{0:T(512)}, f32[384]{0:T(512)S(1)}, u32[]{:S(2)}) copy-start(f32[384]{0:T(512)S(1)} %get-tuple-element.21) | copy-start | bytes 4612
  9.7 28.2 %copy-start.54 = (f32[384]{0:T(512)}, f32[384]{0:T(512)S(1)}, u32[]{:S(2)}) copy-start(f32[384]{0:T(512)S(1)} %get-tuple-element.22) | copy-start | bytes 4612
  9.7 28.2 %copy-start.56 = (f32[384]{0:T(512)}, f32[384]{0:T(512)S(1)}, u32[]{:S(2)}) copy-start(f32[384]{0:T(512)S(1)} %get-tuple-element.23) | copy-start | bytes 4612
  11.5 26.4 %copy-start.58 = (f32[384]{0:T(512)}, f32[384]{0:T(512)S(1)}, u32[]{:S(2)}) copy-start(f32[384]{0:T(512)S(1)} %get-tuple-element.24) | copy-start | bytes 4612
  11.5 26.4 %copy-start.60 = (f32[384]{0:T(512)}, f32[384]{0:T(512)S(1)}, u32[]{:S(2)}) copy-start(f32[384]{0:T(512)S(1)} %get-tuple-element.25) | copy-start | bytes 4612
  11.5 26.4 %copy-start.62 = (f32[384]{0:T(512)}, f32[384]{0:T(512)S(1)}, u32[]{:S(2)}) copy-start(f32[384]{0:T(512)S(1)} %get-tuple-element.26) | copy-start | bytes 4612
  11.6 26.4 %copy-start.64 = (f32[384]{0:T(512)}, f32[384]{0:T(512)S(1)}, u32[]{:S(2)}) copy-start(f32[384]{0:T(512)S(1)} %get-tuple-element.27) | copy-start | bytes 4612
  11.6 26.4 %copy-start.66 = (f32[384]{0:T(512)}, f32[384]{0:T(512)S(1)}, u32[]{:S(2)}) copy-start(f32[384]{0:T(512)S(1)} %get-tuple-element.28) | copy-start | bytes 4612
  11.6 26.4 %copy-start.68 = (f32[384]{0:T(512)}, f32[384]{0:T(512)S(1)}, u32[]{:S(2)}) copy-start(f32[384]{0:T(512)S(1)} %get-tuple-element.29) | copy-start | bytes 4612
  11.6 26.4 %copy-start.70 = (f32[384]{0:T(512)}, f32[384]{0:T(512)S(1)}, u32[]{:S(2)}) copy-start(f32[384]{0:T(512)S(1)} %get-tuple-element.30) | copy-start | bytes 4612
  11.6 26.4 %copy-start.72 = (f32[384]{0:T(512)}, f32[384]{0:T(512)S(1)}, u32[]{:S(2)}) copy-start(f32[384]{0:T(512)S(1)} %get-tuple-element.31) | copy-start | bytes 4612
  11.6 26.4 %copy-start.74 = (f32[384]{0:T(512)}, f32[384]{0:T(512)S(1)}, u32[]{:S(2)}) copy-start(f32[384]{0:T(512)S(1)} %get-tuple-element.32) | copy-start | bytes 4612
  11.6 26.4 %copy-start.76 = (f32[384]{0:T(512)}, f32[384]{0:T(512)S(1)}, u32[]{:S(2)}) copy-start(f32[384]{0:T(512)S(1)} %get-tuple-element.33) | copy-start | bytes 4612
  11.6 26.4 %copy-start.78 = (f32[384]{0:T(512)}, f32[384]{0:T(512)S(1)}, u32[]{:S(2)}) copy-start(f32[384]{0:T(512)S(1)} %get-tuple-element.34) | copy-start | bytes 4612
  11.6 26.4 %copy-start.80 = (f32[384]{0:T(512)}, f32[384]{0:T(512)S(1)}, u32[]{:S(2)}) copy-start(f32[384]{0:T(512)S(1)} %get-tuple-element.35) | copy-start | bytes 4612
  11.6 41.6 %copy-start.82 = (f32[384]{0:T(512)}, f32[384]{0:T(512)S(1)}, u32[]{:S(2)}) copy-start(f32[384]{0:T(512)S(1)} %get-tuple-element.36) | copy-start | bytes 4612
  19.5 18.0 %all-to-all-start = ((bf16[1,2,256,384]{3,1,0,2:T(2,128)(2,1)}), bf16[1,2,256,384]{3,1,0,2:T(2,128)(2,1)S(1)}, u32[]{:S(2)}, u32[]{:S(2)}) async-start(bf16[1,2,256,384]{3,1,0,2:T(2,128)(2,1)} %copy.30), calls=%async_computation | async-start | bytes 786432 | tf_op jit(solution)/shard_map/all_to_all | solution.py:94
  25.8 95.9 %reduce-scatter.2.cloned.1.call-start = ((), (), s32[]{:S(2)}) async-start(), calls=%async_computation.5 | async-start | bytes 2506752 | tf_op jit(solution)/shard_map/reduce_scatter | solution.py:65
  38.0 15.7 %copy-start.87 = (f32[384]{0:T(512)S(1)}, f32[384]{0:T(512)}, u32[]{:S(2)}) copy-start(f32[384]{0:T(512)} %param.11) | copy-start | bytes 4612
  62.2 19.8 %copy-start.89 = (bf16[1536,384]{1,0:T(8,128)(2,1)S(1)}, bf16[1536,384]{1,0:T(8,128)(2,1)}, u32[]{:S(2)}) copy-start(bf16[1536,384]{1,0:T(8,128)(2,1)} %param.13) | copy-start | bytes 3538948
  78.4 18.0 %all-to-all-start.3 = ((bf16[1,8,64,384]{3,2,0,1:T(8,128)(2,1)}), bf16[1,8,64,384]{3,2,0,1:T(8,128)(2,1)S(1)}, u32[]{:S(2)}, u32[]{:S(2)}) async-start(bf16[1,8,64,384]{3,2,0,1:T(8,128)(2,1)} %fusion.265), calls=%async_computation.3 | async-start | bytes 786432 | tf_op jit(solution)/shard_map/all_to_all | solution.py:113
  85.0 11.6 %copy-start.4 = (bf16[1,2,8,32,384]{4,3,2,1,0:T(8,128)(2,1)S(1)}, bf16[1,2,8,32,384]{4,3,2,1,0:T(8,128)(2,1)}, u32[]{:S(2)}) copy-start(bf16[1,2,8,32,384]{4,3,2,1,0:T(8,128)(2,1)} %param.8) | copy-start | bytes 1179652
  85.0 11.6 %copy-start.7 = (f32[384]{0:T(512)S(1)}, f32[384]{0:T(512)}, u32[]{:S(2)}) copy-start(f32[384]{0:T(512)} %copy-done.6) | copy-start | bytes 4612
  (45 other events, 442.6 us)
Sparse Core Ops, SparseCore 0:
  59.6 62.0 reduce-scatter.1
where the time goes:
time: 131 us; the launch traced here: 130 us
  waiting for transfers between devices  39.2 us (30%)
  blocking collectives  26.9 us (21%)
  other arithmetic  21.8 us (17%)
  between operations  15.5 us (12%)
  starting transfers between devices  9.96 us (8%)
  matrix products  9.86 us (8%)
  local copies, waits for them, and re-layouts  6.89 us (5%)
    reduce_scatter x1, waiting for transfers between devices, token_block(): lax.psum_scatter(lax.dot_general(d_pre, scaled, (((0,), (0,)), ((), ())),...  18.7 us
    all_to_all x1, blocking collectives, local(): lax.all_to_all(d_tokens.reshape(flat_shape), 'tm', split_axis=2, concat_a...  13.6 us
    all_to_all x1, blocking collectives, local(): lax.all_to_all(second_tiles, 'tm', split_axis=1, concat_axis=2, tiled=True)  13.3 us
    all_to_all x1, waiting for transfers between devices, local(): tiles = lax.all_to_all(first, 'tm', split_axis=2, concat_axis=1, tiled=True)  10.3 us
    all_to_all x1, waiting for transfers between devices, local(): lax.all_to_all(d_first_tiles, 'tm', split_axis=1, concat_axis=2, tiled=True)  10.2 us
    all_to_all x1, starting transfers between devices, local(): tiles = lax.all_to_all(first, 'tm', split_axis=2, concat_axis=1, tiled=True)  6.32 us
    convert_element_type x1, other arithmetic, local(): grad_clips = (cotangent.astype(jnp.float32) + spatial_pass(d_first.reshap...  6.12 us
    convert_element_type x1, other arithmetic, local(): first = spatial_pass(clips.astype(jnp.float32), spatial_kernel, False).as...  5.61 us
  transfers between devices with their start and end apart: 3, of which 3 were waited for; matrix products, arithmetic and copies ran while one was open for 13% of the time, Pallas kernels for 0%

commit v1 on v0

v1 whole, which is shorter than its diff:
```python
import functools
import jax
import jax.numpy as jnp
from jax import lax
from jax.experimental import pallas as pl
from jax.experimental.pallas import tpu as pltpu
from jax.sharding import PartitionSpec as P

LANES = 128
PAD = 8
F32 = jnp.float32
BF16 = jnp.bfloat16
VMEM_LIMIT = 32 * 1024 * 1024


def call(body, outs, scratch, *args, flops=0, limit=VMEM_LIMIT):
    moved = sum(a.size * a.dtype.itemsize for a in args)
    moved += sum(o.size * o.dtype.itemsize for o in outs)
    return pl.pallas_call(
        body,
        out_shape=tuple(outs),
        in_specs=[pl.BlockSpec(memory_space=pltpu.VMEM)] * len(args),
        out_specs=tuple([pl.BlockSpec(memory_space=pltpu.VMEM)] * len(outs)),
        scratch_shapes=list(scratch),
        cost_estimate=pl.CostEstimate(flops=flops, bytes_accessed=moved, transcendentals=0),
        compiler_params=pltpu.CompilerParams(vmem_limit_bytes=limit),
    )(*args)


def struct(shape, dtype):
    return jax.ShapeDtypeStruct(tuple(shape), dtype)


def slot_to(step, count):
    if count == 1:
        return 0
    return lax.rem(lax.axis_index("tm") + step, count)


def slot_from(step, count):
    if count == 1:
        return 0
    return lax.rem(lax.axis_index("tm") + count - step, count)


def exchange(pieces):
    count = len(pieces)
    got = [pieces[0]]
    for step in range(1, count):
        pairs = [(i, (i + step) % count) for i in range(count)]
        got.append(lax.ppermute(pieces[step], "tm", pairs))
    return got


def conv_rows(pad_ref, kernel_ref, block, col, height, flip, emit):
    taps = kernel_ref.shape[1]
    radius = taps // 2
    acc = [None] * height
    for col_off in range(taps):
        shift = radius - col_off if flip else col_off - radius
        weights = [
            kernel_ref[block, row_off, pl.ds(col_off, 1), :] for row_off in range(taps)
        ]
        for row in range(height):
            values = pad_ref[block, :, row, pl.ds(PAD + col + shift, 8), :]
            for row_off in range(taps):
                out = row - radius + row_off if flip else row + radius - row_off
                if 0 <= out < height:
                    term = values * weights[row_off][None]
                    acc[out] = term if acc[out] is None else acc[out] + term
    for row in range(height):
        emit(row, acc[row])


def clear_pads(pad_ref, width):
    blocks, frames, height, _, lanes = pad_ref.shape
    zero = jnp.zeros((blocks, frames, height, PAD, lanes), F32)
    pad_ref[:, :, :, 0:PAD, :] = zero
    pad_ref[:, :, :, PAD + width : PAD + width + PAD, :] = zero


def spatial_fwd(count, *refs):
    clips, cot, kernel = refs[:3]
    firsts = refs[3 : 3 + count]
    cots = refs[3 + count : 3 + 2 * count]
    pad_ref, flat = refs[3 + 2 * count :]
    _, frames, height, width, channels = clips.shape
    blocks = channels // LANES
    pixels = height * width // count
    clear_pads(pad_ref, width)
    for block in range(blocks):
        lanes = slice(block * LANES, (block + 1) * LANES)
        pad_ref[block, :, :, PAD : PAD + width, :] = clips[0, :, :, :, lanes].astype(F32)

    for block in range(blocks):
        lanes = slice(block * LANES, (block + 1) * LANES)
        for col in range(0, width, 8):

            def emit(row, value):
                flat[:, row, pl.ds(col, 8), lanes] = value

            conv_rows(pad_ref, kernel, block, col, height, False, emit)
    rows = height // count
    for step in range(count):
        base = slot_to(step, count) * rows
        firsts[step][...] = (
            flat[:, pl.ds(base, rows), :, :].reshape(frames, pixels, channels).astype(BF16)
        )
        cots[step][...] = cot[0, :, pl.ds(base, rows), :, :].reshape(frames, pixels, channels)


def spatial_bwd(count, *refs):
    pieces = refs[:count]
    cot, kernel, out_ref, pad_ref = refs[count:]
    _, frames, height, width, channels = cot.shape
    blocks = channels // LANES
    rows = height // count
    clear_pads(pad_ref, width)
    for step in range(count):
        base = slot_from(step, count) * rows
        for block in range(blocks):
            lanes = slice(block * LANES, (block + 1) * LANES)
            piece = pieces[step][:, :, lanes].astype(F32).reshape(frames, rows, width, LANES)
            pad_ref[block, :, pl.ds(base, rows), PAD : PAD + width, :] = piece
    for block in range(blocks):
        lanes = slice(block * LANES, (block + 1) * LANES)
        for col in range(0, width, 16):
            halves = []
            for part in range(2):
                rows_out = []
                conv_rows(
                    pad_ref, kernel, block, col + 8 * part, height, True,
                    lambda row, value: rows_out.append(value),
                )
                halves.append(rows_out)
            for row in range(height):
                total = jnp.concatenate([halves[0][row], halves[1][row]], axis=1)
                total = total + cot[0, :, row, pl.ds(col, 16), lanes].astype(F32)
                out_ref[0, :, row, pl.ds(col, 16), lanes] = total.astype(BF16)


def mix_frames(source, target, kernel, flip):
    frames = source.shape[0]
    taps = kernel.shape[0]
    radius = taps // 2
    if frames <= 16:
        for out in range(frames):
            total = None
            for inp in range(frames):
                lag = (out - inp if flip else inp - out) + radius
                if 0 <= lag < taps:
                    term = kernel[pl.ds(lag, 1), :] * source[inp]
                    total = term if total is None else total + term
            target[out] = total.astype(BF16).astype(F32)
        return

    def one(out, carry):
        def tap(inp, total):
            lag = (out - inp if flip else inp - out) + radius
            return total + kernel[pl.ds(lag, 1), :] * source[inp]

        low = jnp.maximum(out - radius, 0)
        high = jnp.minimum(out + radius + 1, frames)
        total = lax.fori_loop(low, high, tap, jnp.zeros(source.shape[1:], F32))
        target[out] = total.astype(BF16).astype(F32)
        return carry

    lax.fori_loop(0, frames, one, 0)


def place_frames(count, pieces, target):
    for step in range(count):
        frames = pieces[step].shape[0]
        base = slot_from(step, count) * frames
        target[pl.ds(base, frames)] = pieces[step][...].astype(target.dtype)


def mlp_fwd(count, chunk, *refs):
    pieces = refs[:count]
    taps, gain, w_expand, w_project = refs[count : count + 4]
    branches = refs[count + 4 : 2 * count + 4]
    scaled, slope, normed, inv_std, mixed_in, mixed, hidden, branch = refs[2 * count + 4 :]
    frames, pixels, channels = mixed_in.shape
    tokens = frames * pixels
    place_frames(count, pieces, mixed_in)
    mix_frames(mixed_in, mixed, taps, False)
    values = mixed[...].reshape(tokens, channels)
    average = jnp.mean(values, axis=-1, keepdims=True)
    centred = values - average
    inverse = lax.rsqrt(jnp.mean(centred * centred, axis=-1, keepdims=True) + 1e-06)
    inv_std[...] = inverse
    norm = centred * inverse
    normed[...] = norm
    scaled[...] = (norm * gain[...]).astype(BF16)
    for start in range(0, w_expand.shape[1], chunk):
        part = slice(start, start + chunk)
        pre = jnp.dot(scaled[...], w_expand[:, part], preferred_element_type=F32)
        cdf = 0.5 + 0.5 * lax.erf(pre * 0.7071067811865476)
        hidden[:, part] = (pre * cdf).astype(BF16)
        slope[:, part] = (cdf + pre * jnp.exp(-0.5 * pre * pre) * 0.3989422804014327).astype(BF16)
    branch[...] = jnp.dot(hidden[...], w_project[...], preferred_element_type=F32).reshape(
        frames, pixels, channels
    )
    own = frames // count
    for step in range(count):
        base = slot_to(step, count) * own
        branches[step][...] = branch[pl.ds(base, own)].astype(BF16)


def mlp_bwd(count, chunk, *refs):
    pieces = refs[:count]
    slope, normed, inv_std, taps, gain, w_expand, w_project = refs[count : count + 7]
    outs = refs[count + 7 : 2 * count + 7]
    d_pre, grads, d_second, d_first = refs[2 * count + 7 :]
    frames, pixels, channels = grads.shape
    tokens = frames * pixels
    place_frames(count, pieces, grads)
    grad_rows = grads[...].reshape(tokens, channels).astype(BF16)
    last = (((1,), (1,)), ((), ()))
    for start in range(0, w_expand.shape[1], chunk):
        part = slice(start, start + chunk)
        d_hidden = lax.dot_general(grad_rows, w_project[part, :], last, preferred_element_type=F32)
        d_pre[:, part] = (d_hidden * slope[:, part].astype(F32)).astype(BF16)
    d_scaled = lax.dot_general(d_pre[...], w_expand[...], last, preferred_element_type=F32)
    d_normed = d_scaled * gain[...]
    norm = normed[...]
    d_tokens = inv_std[...] * (
        d_normed
        - jnp.mean(d_normed, axis=-1, keepdims=True)
        - norm * jnp.mean(d_normed * norm, axis=-1, keepdims=True)
    )
    d_second[...] = d_tokens.astype(BF16).astype(F32).reshape(frames, pixels, channels)
    mix_frames(d_second, d_first, taps, True)
    own = frames // count
    for step in range(count):
        base = slot_to(step, count) * own
        outs[step][...] = d_first[pl.ds(base, own)].astype(BF16)


def add_residual(count, *refs):
    pieces = refs[:count]
    clips, out_ref = refs[count:]
    _, frames, height, width, channels = clips.shape
    rows = height // count
    for step in range(count):
        base = slot_from(step, count) * rows
        piece = pieces[step][...].reshape(frames, rows, width, channels).astype(F32)
        here = (0, slice(None), pl.ds(base, rows))
        out_ref[here] = (clips[here].astype(F32) + piece).astype(BF16)


def weight_grad(d_pre, scaled, keep, send, full):
    block = keep.shape[1]
    full[...] = lax.dot_general(
        d_pre[...], scaled[...], (((0,), (0,)), ((), ())), preferred_element_type=F32
    ).reshape(full.shape)
    core = lax.rem(lax.axis_index("dp"), 2)
    for pair in range(full.shape[0] // 2):
        keep[pair] = full[2 * pair + core]
        send[pair] = full[2 * pair + 1 - core].astype(BF16)


def fold_pair(keep_in, got, keep, send):
    side = lax.div(lax.axis_index("dp"), 2)
    for slot in range(keep.shape[0]):
        mine, other = 2 * slot + side, 2 * slot + 1 - side
        keep[slot] = keep_in[mine] + got[mine].astype(F32)
        send[slot] = (keep_in[other] + got[other].astype(F32)).astype(BF16)


def fold_tm(count, keep_in, got, keep, *sends):
    for step in range(count):
        slot = slot_to(step, count)
        total = keep_in[slot] + got[slot].astype(F32)
        if step == 0:
            keep[...] = total
        else:
            sends[step - 1][...] = total.astype(BF16)


def fold_last(scale_factor, keep_in, *refs):
    total = keep_in[...]
    for got in refs[:-1]:
        total = total + got[...].astype(F32)
    refs[-1][...] = total * scale_factor


def scatter_grad(d_pre, scaled, count, scale_factor):
    hid, channels = d_pre.shape[1], scaled.shape[1]
    sides = lax.axis_size("dp")
    if count == 1 or sides != 4:
        whole = lax.dot_general(
            d_pre, scaled, (((0,), (0,)), ((), ())), preferred_element_type=F32
        )
        return (
            lax.psum_scatter(whole, ("tm", "dp"), scatter_dimension=0, tiled=True) * scale_factor
        )
    block = hid // (count * sides)
    half = (2 * count, block, channels)
    quarter = (count, block, channels)
    keep, send = call(
        weight_grad,
        [struct(half, F32), struct(half, BF16)],
        [pltpu.VMEM((4 * count, block, channels), F32)],
        d_pre,
        scaled,
        flops=2 * hid * channels * d_pre.shape[0],
    )
    got = lax.ppermute(send, "dp", [(i, i ^ 1) for i in range(4)])
    keep, send = call(fold_pair, [struct(quarter, F32), struct(quarter, BF16)], [], keep, got)
    got = lax.ppermute(send, "dp", [(i, i ^ 2) for i in range(4)])
    piece = (block, channels)
    keep, *sends = call(
        functools.partial(fold_tm, count),
        [struct(piece, F32)] + [struct(piece, BF16)] * (count - 1),
        [],
        keep,
        got,
    )
    got = exchange([keep] + list(sends))[1:]
    return call(
        functools.partial(fold_last, scale_factor), [struct(piece, F32)], [], keep, *got
    )[0]


def local(clips, cotangent, spatial_kernel, temporal_kernel, norm_gain, w_expand, w_project):
    _, frames, height, width, channels = clips.shape
    members = lax.axis_size("tm")
    device_count = members * lax.axis_size("dp")
    pixels = height * width
    scale_factor = float(clips.shape[0] * frames * pixels * device_count) ** (-0.5)
    hid = w_expand.shape[1]
    chunk = 256
    blocks = channels // LANES
    count = members if members <= 8 and height % members == 0 else 1
    all_frames = frames * members
    columns = pixels // members
    tokens = all_frames * columns

    def to_columns(pieces):
        if count > 1:
            return exchange(pieces)
        whole = pieces[0][None]
        return [lax.all_to_all(whole, "tm", split_axis=2, concat_axis=1, tiled=True)[0]]

    def to_frames(pieces):
        if count > 1:
            return exchange(pieces)
        whole = pieces[0][None]
        return [lax.all_to_all(whole, "tm", split_axis=1, concat_axis=2, tiled=True)[0]]

    kernel = spatial_kernel.reshape(spatial_kernel.shape[:2] + (blocks, LANES)).transpose(2, 0, 1, 3)
    gain = norm_gain.reshape(1, channels)
    pad = pltpu.VMEM((blocks, frames, height, width + 2 * PAD, LANES), F32)
    conv_flops = 2 * 49 * frames * pixels * channels
    mlp_flops = 2 * tokens * channels * hid

    piece = struct((frames, pixels // count, channels), BF16)
    outs = call(
        functools.partial(spatial_fwd, count),
        [piece] * (2 * count),
        [pad, pltpu.VMEM((frames, height, width, channels), F32)],
        clips,
        cotangent,
        kernel,
        flops=conv_flops,
    )
    firsts = to_columns(list(outs[:count]))
    cots = to_columns(list(outs[count:]))

    column = (all_frames, columns, channels)
    back = struct((all_frames // count, columns, channels), BF16)
    outs = call(
        functools.partial(mlp_fwd, count, chunk),
        [back] * count
        + [
            struct((tokens, channels), BF16),
            struct((tokens, hid), BF16),
            struct((tokens, channels), F32),
            struct((tokens, 1), F32),
        ],
        [
            pltpu.VMEM(column, F32),
            pltpu.VMEM(column, F32),
            pltpu.VMEM((tokens, hid), BF16),
            pltpu.VMEM(column, F32),
        ],
        *firsts,
        temporal_kernel,
        gain,
        w_expand,
        w_project,
        flops=2 * mlp_flops,
    )
    scaled, slope, normed, inv_std = outs[count:]
    branches = to_frames(list(outs[:count]))

    outs = call(
        functools.partial(mlp_bwd, count, chunk),
        [back] * count + [struct((tokens, hid), BF16)],
        [pltpu.VMEM(column, F32), pltpu.VMEM(column, F32), pltpu.VMEM(column, F32)],
        *cots,
        slope,
        normed,
        inv_std,
        temporal_kernel,
        gain,
        w_expand,
        w_project,
        flops=2 * mlp_flops,
    )
    d_pre = outs[count]
    d_firsts = to_frames(list(outs[:count]))

    grad_expand = scatter_grad(d_pre, scaled, count, scale_factor)

    grad_clips = call(
        functools.partial(spatial_bwd, count),
        [struct(clips.shape, BF16)],
        [pad],
        *d_firsts,
        cotangent,
        kernel,
        flops=conv_flops,
    )[0]
    block_out = call(
        functools.partial(add_residual, count), [struct(clips.shape, BF16)], [], *branches, clips
    )[0]
    return (block_out, grad_clips, grad_expand)


def solution(mesh):
    in_specs = (
        P(("groups", "dp"), "tm", None, None, None),
        P(("groups", "dp"), "tm", None, None, None),
        P(),
        P(),
        P(),
        P(),
        P(),
    )
    out_specs = (
        P(("groups", "dp"), "tm", None, None, None),
        P(("groups", "dp"), "tm", None, None, None),
        P(("groups", "tm", "dp"), None),
    )
    return jax.shard_map(local, mesh=mesh, in_specs=in_specs, out_specs=out_specs, check_vma=False)
```

time: 131 us -> 64.4 us (0.49)
  waiting for transfers between devices: 39.2 us -> 11.2 us
  blocking collectives: 26.9 us -> 0 us
  other arithmetic: 21.8 us -> 0 us
  starting transfers between devices: 9.96 us -> 31.5 us
  between operations: 15.5 us -> 0.75 us
  Pallas kernels: 0 us -> 13.5 us
  matrix products: 9.86 us -> 0 us
    ppermute x0 -> x17, starting transfers between devices: none -> 31.5 us  [the longest x15 29.9 us: exchange(): got.append(lax.ppermute(pieces[step], 'tm', pairs))]
    all_to_all x2 -> x0, blocking collectives: 26.9 us -> none  [the longest x1 13.6 us: local(): lax.all_to_all(d_tokens.reshape(flat_shape), 'tm', split_axis=2, concat_a...]
    all_to_all x2 -> x0, waiting for transfers between devices: 20.5 us -> none  [the longest x1 10.3 us: local(): tiles = lax.all_to_all(first, 'tm', split_axis=2, concat_axis=1, tiled=True)]
    reduce_scatter x1 -> x0, waiting for transfers between devices: 18.7 us -> none  [token_block(): lax.psum_scatter(lax.dot_general(d_pre, scaled, (((0,), (0,)), ((), ())),...]
    convert_element_type x12 -> x0, other arithmetic: 18.4 us -> none  [the longest x1 6.12 us: local(): grad_clips = (cotangent.astype(jnp.float32) + spatial_pass(d_first.reshap...]
    pallas_call x0 -> x9, Pallas kernels: none -> 13.5 us  [call(): pl.pallas_call(body, out_shape=tuple(outs), in_specs=[pl.BlockSpec(memory...]
    ppermute x0 -> x17, waiting for transfers between devices: none -> 11.2 us  [the longest x15 9.25 us: exchange(): got.append(lax.ppermute(pieces[step], 'tm', pairs))]
    all_to_all x2 -> x0, starting transfers between devices: 9.96 us -> none  [the longest x1 6.32 us: local(): tiles = lax.all_to_all(first, 'tm', split_axis=2, concat_axis=1, tiled=True)]
  transfers between devices with their start and end apart: 3 -> 17, of which waited for: 3 -> 5; matrix products, arithmetic and copies ran while one was open for 13% -> 1% of each run, Pallas kernels for 0% -> 10%
where the time goes in v1:
time: 64.4 us; the launch traced here: 64 us
  starting transfers between devices  31.5 us (49%)
  Pallas kernels  13.5 us (21%)
  waiting for transfers between devices  11.2 us (17%)
  local copies, waits for them, and re-layouts  6.91 us (11%)
  between operations  0.75 us (1%)
    ppermute x15, starting transfers between devices, exchange(): got.append(lax.ppermute(pieces[step], 'tm', pairs))  29.9 us
    pallas_call x9, Pallas kernels, call(): pl.pallas_call(body, out_shape=tuple(outs), in_specs=[pl.BlockSpec(memory...  13.5 us
    ppermute x15, waiting for transfers between devices, exchange(): got.append(lax.ppermute(pieces[step], 'tm', pairs))  9.25 us
    unnamed x18, local copies, waits for them, and re-layouts  6.23 us
    ppermute x1, waiting for transfers between devices, scatter_grad(): got = lax.ppermute(send, 'dp', [(i, i ^ 1) for i in range(4)])  1.99 us
    ppermute x1, starting transfers between devices, scatter_grad(): got = lax.ppermute(send, 'dp', [(i, i ^ 2) for i in range(4)])  1.56 us
  transfers between devices with their start and end apart: 17, of which 5 were waited for; matrix products, arithmetic and copies ran while one was open for 1% of the time, Pallas kernels for 10%

profile of v1, /device:TPU:0, one launch (start us, length us, event | category | flops | bytes accessed | tf_op | source)
XLA Modules:
  0.0 64.0 jit_solution(5566480441763764475)
XLA Ops:
  0.6 0.0 copy-start
  0.6 0.9 %copy-done = f32[7,7,384]{2,1,0:T(8,128)S(1)} copy-done((f32[7,7,384]{2,1,0:T(8,128)S(1)}, f32[7,7,384]{2,1,0:T(8,128)}, u32[]{:S(2)}) %copy-start) | copy-done | bytes 75288
  1.5 1.0 %copy-done.1 = bf16[1,2,8,32,384]{4,3,2,1,0:T(8,128)(2,1)S(1)} copy-done((bf16[1,2,8,32,384]{4,3,2,1,0:T(8,128)(2,1)S(1)}, bf16[1,2,8,32,384]{4,3,2,1,0:T(8,128)(2,1)}, u32[]{:S(2)}) %copy-start.1) | copy-done | bytes 393240
  2.5 1.0 %copy-done.3 = bf16[1,2,8,32,384]{4,3,2,1,0:T(8,128)(2,1)S(1)} copy-done((bf16[1,2,8,32,384]{4,3,2,1,0:T(8,128)(2,1)S(1)}, bf16[1,2,8,32,384]{4,3,2,1,0:T(8,128)(2,1)}, u32[]{:S(2)}) %copy-start.3) | copy-done | bytes 393240
  3.5 2.1 %shard_map.94 = (bf16[2,64,384]{2,1,0:T(8,128)(2,1)S(1)}, bf16[2,64,384]{2,1,0:T(8,128)(2,1)S(1)}, bf16[2,64,384]{2,1,0:T(8,128)(2,1)S(1)}, bf16[2,64,384]{2,1,0...) custom-call(bf16[1,2,8,32,384]{4,3,2,1,0:T(8,128)(2,1)S(1)} %copy-do, ...), custom_call_target="tpu_custom_call" | custom-call | flops 19267584 | bytes 1648128 | tf_op jit(solution)/shard_map/pallas_call | solution.py:19
  5.6 3.1 %collective-permute-start = (bf16[2,64,384]{2,1,0:T(8,128)(2,1)S(1)}, bf16[2,64,384]{2,1,0:T(8,128)(2,1)S(1)}, u32[]{:S(2)}, u32[]{:S(2)}) collective-permute-start(bf16[2,64,384]{2,1,0:T(8,128)(2,1)S(1)} %get-tuple-element.33), channel_id=1, source_target_pairs={{0,4},{4,8},{8,12},{12,0},{1,5},{5,9},{9,13},{13,1},{2,6},{6,10},{... | collective-permute-start | bytes 294920 | tf_op jit(solution)/shard_map/ppermute | solution.py:51
  8.7 2.6 %collective-permute-start.1 = (bf16[2,64,384]{2,1,0:T(8,128)(2,1)S(1)}, bf16[2,64,384]{2,1,0:T(8,128)(2,1)S(1)}, u32[]{:S(2)}, u32[]{:S(2)}) collective-permute-start(bf16[2,64,384]{2,1,0:T(8,128)(2,1)S(1)} %get-tuple-element.34), channel_id=1, source_target_pairs={{0,8},{4,12},{8,0},{12,4},{1,9},{5,13},{9,1},{13,5},{2,10},{6,14},... | collective-permute-start | bytes 294920 | tf_op jit(solution)/shard_map/ppermute | solution.py:51
  11.3 1.3 %collective-permute-start.2 = (bf16[2,64,384]{2,1,0:T(8,128)(2,1)S(1)}, bf16[2,64,384]{2,1,0:T(8,128)(2,1)S(1)}, u32[]{:S(2)}, u32[]{:S(2)}) collective-permute-start(bf16[2,64,384]{2,1,0:T(8,128)(2,1)S(1)} %get-tuple-element.35), channel_id=1, source_target_pairs={{0,12},{4,0},{8,4},{12,8},{1,13},{5,1},{9,5},{13,9},{2,14},{6,2},{... | collective-permute-start | bytes 294920 | tf_op jit(solution)/shard_map/ppermute | solution.py:51
  12.7 0.7 %collective-permute-start.6 = (bf16[2,64,384]{2,1,0:T(8,128)(2,1)S(1)}, bf16[2,64,384]{2,1,0:T(8,128)(2,1)S(1)}, u32[]{:S(2)}, u32[]{:S(2)}) collective-permute-start(bf16[2,64,384]{2,1,0:T(8,128)(2,1)S(1)} %get-tuple-element.41), channel_id=1, source_target_pairs={{0,4},{4,8},{8,12},{12,0},{1,5},{5,9},{9,13},{13,1},{2,6},{6,10},{... | collective-permute-start | bytes 294920 | tf_op jit(solution)/shard_map/ppermute | solution.py:51
  13.3 0.3 collective-permute-start.7
  13.7 0.7 %reshape.13.refs_5_.refs_8_ = f32[1,384]{1,0:T(1,128)S(1)} reshape(f32[384]{0:T(512)} %param.11) | data formatting | bytes 3072 | tf_op jit(solution)/shard_map/reshape | solution.py:353
  14.4 0.0 collective-permute-done.refs_1_
  14.4 3.1 %collective-permute-start.8 = (bf16[2,64,384]{2,1,0:T(8,128)(2,1)S(1)}, bf16[2,64,384]{2,1,0:T(8,128)(2,1)S(1)}, u32[]{:S(2)}, u32[]{:S(2)}) collective-permute-start(bf16[2,64,384]{2,1,0:T(8,128)(2,1)S(1)} %get-tuple-element.43), channel_id=1, source_target_pairs={{0,12},{4,0},{8,4},{12,8},{1,13},{5,1},{9,5},{13,9},{2,14},{6,2},{... | collective-permute-start | bytes 294920 | tf_op jit(solution)/shard_map/ppermute | solution.py:51
  17.5 3.9 %collective-permute-done.1.refs_2_ = bf16[2,64,384]{2,1,0:T(8,128)(2,1)S(1)} collective-permute-done((bf16[2,64,384]{2,1,0:T(8,128)(2,1)S(1)}, bf16[2,64,384]{2,1,0:T(8,128)(2,1)S(1)}, u32[]{:S(2)}, u32[]{:S(2)}) %collective-permute-start.1) | collective-permute-done | bytes 98336 | tf_op jit(solution)/shard_map/ppermute | solution.py:51
  21.4 1.3 %copy-done.5 = bf16[384,1536]{1,0:T(8,128)(2,1)S(1)} copy-done((bf16[384,1536]{1,0:T(8,128)(2,1)S(1)}, bf16[384,1536]{1,0:T(8,128)(2,1)}, u32[]{:S(2)}) %copy-start.5) | copy-done | bytes 1179672
  22.7 1.3 %copy-done.7 = bf16[1536,384]{1,0:T(8,128)(2,1)S(1)} copy-done((bf16[1536,384]{1,0:T(8,128)(2,1)S(1)}, bf16[1536,384]{1,0:T(8,128)(2,1)}, u32[]{:S(2)}) %copy-start.7) | copy-done | bytes 1179672
  24.0 0.8 %copy-done.8 = f32[31,384]{1,0:T(8,128)S(1)} copy-done((f32[31,384]{1,0:T(8,128)S(1)}, f32[31,384]{1,0:T(8,128)}, u32[]{:S(2)}) %copy-start.8) | copy-done | bytes 47640
  24.8 2.9 %shard_map.95 = (bf16[2,64,384]{2,1,0:T(8,128)(2,1)S(1)}, bf16[2,64,384]{2,1,0:T(8,128)(2,1)S(1)}, bf16[2,64,384]{2,1,0:T(8,128)(2,1)S(1)}, bf16[2,64,384]{2,1,0...) custom-call(bf16[2,64,384]{2,1,0:T(8,128)(2,1)S(1)} %get-tuple-eleme, ...), custom_call_target="tpu_custom_call" | custom-call | flops 1207959552 | bytes 5949440 | tf_op jit(solution)/shard_map/pallas_call | solution.py:19
  27.7 0.0 collective-permute-done.7.refs_2_
  27.7 0.0 collective-permute-done.8.refs_3_
  27.7 2.6 %shard_map.97 = (bf16[2,64,384]{2,1,0:T(8,128)(2,1)S(1)}, bf16[2,64,384]{2,1,0:T(8,128)(2,1)S(1)}, bf16[2,64,384]{2,1,0:T(8,128)(2,1)S(1)}, bf16[2,64,384]{2,1,0:T(8,128)(2,1)S(1)}, bf16[512,1536]{1,0:T(8,128)(2,1)S(1)}) custom-call(bf16[2,64,384]{2,1,0:T(8,128)(2,1)S(1)} %get-tuple-element.40.refs_0_, ...), custom_call_target="tpu_custom_call" | custom-call | flops 1207959552 | bytes 7129088 | tf_op jit(solution)/shard_map/pallas_call | solution.py:19
  30.3 1.3 %shard_map.99 = (f32[8,96,384]{2,1,0:T(8,128)S(1)}, bf16[8,96,384]{2,1,0:T(8,128)(2,1)S(1)}) custom-call(bf16[512,1536]{1,0:T(8,128)(2,1)S(1)} %get-tuple-element.51.d_pre, bf16[512,384]{1,0:T(8,128)(2,1)S(1)} %get-tuple-element.52.scaled), custom_call_target="tpu_custom_call" | custom-call | flops 603979776 | bytes 3735552 | tf_op jit(solution)/shard_map/pallas_call | solution.py:19
  31.7 0.1 collective-permute-start.12
  31.8 2.0 %collective-permute-done.12.got = bf16[8,96,384]{2,1,0:T(8,128)(2,1)S(1)} collective-permute-done((bf16[8,96,384]{2,1,0:T(8,128)(2,1)S(1)}, bf16[8,96,384]{2,1,0:T(8,128)(2,1)S(1)}, u32[]{:S(2)}, u32[]{:S(2)}) %collective-permute-start.12) | collective-permute-done | bytes 589856 | tf_op jit(solution)/shard_map/ppermute | solution.py:309
  33.8 0.1 shard_map.100
  33.9 0.0 copy-start.2
  33.9 1.6 %collective-permute-start.13 = (bf16[4,96,384]{2,1,0:T(8,128)(2,1)S(1)}, bf16[4,96,384]{2,1,0:T(8,128)(2,1)S(1)}, u32[]{:S(2)}, u32[]{:S(2)}) collective-permute-start(bf16[4,96,384]{2,1,0:T(8,128)(2,1)S(1)} %get-tuple-element.56), channel_id=1, source_target_pairs={{0,2},{1,3},{2,0},{3,1},{4,6},{5,7},{6,4},{7,5},{8,10},{9,11},{10,... | collective-permute-start | bytes 884744 | tf_op jit(solution)/shard_map/ppermute | solution.py:311
  35.4 3.3 %collective-permute-start.3 = (bf16[2,64,384]{2,1,0:T(8,128)(2,1)S(1)}, bf16[2,64,384]{2,1,0:T(8,128)(2,1)S(1)}, u32[]{:S(2)}, u32[]{:S(2)}) collective-permute-start(bf16[2,64,384]{2,1,0:T(8,128)(2,1)S(1)} %get-tuple-element.37), channel_id=1, source_target_pairs={{0,4},{4,8},{8,12},{12,0},{1,5},{5,9},{9,13},{13,1},{2,6},{6,10},{... | collective-permute-start | bytes 294920 | tf_op jit(solution)/shard_map/ppermute | solution.py:51
  38.8 2.6 %collective-permute-start.4 = (bf16[2,64,384]{2,1,0:T(8,128)(2,1)S(1)}, bf16[2,64,384]{2,1,0:T(8,128)(2,1)S(1)}, u32[]{:S(2)}, u32[]{:S(2)}) collective-permute-start(bf16[2,64,384]{2,1,0:T(8,128)(2,1)S(1)} %get-tuple-element.38), channel_id=1, source_target_pairs={{0,8},{4,12},{8,0},{12,4},{1,9},{5,13},{9,1},{13,5},{2,10},{6,14},... | collective-permute-start | bytes 294920 | tf_op jit(solution)/shard_map/ppermute | solution.py:51
  41.4 2.0 %collective-permute-start.9 = (bf16[2,64,384]{2,1,0:T(8,128)(2,1)S(1)}, bf16[2,64,384]{2,1,0:T(8,128)(2,1)S(1)}, u32[]{:S(2)}, u32[]{:S(2)}) collective-permute-start(bf16[2,64,384]{2,1,0:T(8,128)(2,1)S(1)} %get-tuple-element.48), channel_id=1, source_target_pairs={{0,4},{4,8},{8,12},{12,0},{1,5},{5,9},{9,13},{13,1},{2,6},{6,10},{... | collective-permute-start | bytes 294920 | tf_op jit(solution)/shard_map/ppermute | solution.py:51
  43.4 1.1 %collective-permute-done.3.refs_1_ = bf16[2,64,384]{2,1,0:T(8,128)(2,1)S(1)} collective-permute-done((bf16[2,64,384]{2,1,0:T(8,128)(2,1)S(1)}, bf16[2,64,384]{2,1,0:T(8,128)(2,1)S(1)}, u32[]{:S(2)}, u32[]{:S(2)}) %collective-permute-start.3) | collective-permute-done | bytes 98336 | tf_op jit(solution)/shard_map/ppermute | solution.py:51
  44.6 2.1 %collective-permute-start.10 = (bf16[2,64,384]{2,1,0:T(8,128)(2,1)S(1)}, bf16[2,64,384]{2,1,0:T(8,128)(2,1)S(1)}, u32[]{:S(2)}, u32[]{:S(2)}) collective-permute-start(bf16[2,64,384]{2,1,0:T(8,128)(2,1)S(1)} %get-tuple-element.49), channel_id=1, source_target_pairs={{0,8},{4,12},{8,0},{12,4},{1,9},{5,13},{9,1},{13,5},{2,10},{6,14},... | collective-permute-start | bytes 294920 | tf_op jit(solution)/shard_map/ppermute | solution.py:51
  46.6 0.0 collective-permute-done.13.got
  46.6 2.2 %collective-permute-start.11 = (bf16[2,64,384]{2,1,0:T(8,128)(2,1)S(1)}, bf16[2,64,384]{2,1,0:T(8,128)(2,1)S(1)}, u32[]{:S(2)}, u32[]{:S(2)}) collective-permute-start(bf16[2,64,384]{2,1,0:T(8,128)(2,1)S(1)} %get-tuple-element.50), channel_id=1, source_target_pairs={{0,12},{4,0},{8,4},{12,8},{1,13},{5,1},{9,5},{13,9},{2,14},{6,2},{... | collective-permute-start | bytes 294920 | tf_op jit(solution)/shard_map/ppermute | solution.py:51
  48.8 0.1 shard_map.101
  48.9 2.6 %collective-permute-done.4.refs_2_ = bf16[2,64,384]{2,1,0:T(8,128)(2,1)S(1)} collective-permute-done((bf16[2,64,384]{2,1,0:T(8,128)(2,1)S(1)}, bf16[2,64,384]{2,1,0:T(8,128)(2,1)S(1)}, u32[]{:S(2)}, u32[]{:S(2)}) %collective-permute-start.4) | collective-permute-done | bytes 98336 | tf_op jit(solution)/shard_map/ppermute | solution.py:51
  51.5 0.0 collective-permute-start.14
  51.5 0.0 collective-permute-done.5.refs_3_
  51.5 2.9 %collective-permute-start.15 = (bf16[96,384]{1,0:T(8,128)(2,1)S(1)}, bf16[96,384]{1,0:T(8,128)(2,1)S(1)}, u32[]{:S(2)}, u32[]{:S(2)}) collective-permute-start(bf16[96,384]{1,0:T(8,128)(2,1)S(1)} %get-tuple-element.59), channel_id=1, source_target_pairs={{0,8},{4,12},{8,0},{12,4},{1,9},{5,13},{9,1},{13,5},{2,10},{6,14},... | collective-permute-start | bytes 221192 | tf_op jit(solution)/shard_map/ppermute | solution.py:51
  54.4 0.0 collective-permute-done.9.refs_1_
  54.4 3.6 %collective-permute-start.16 = (bf16[96,384]{1,0:T(8,128)(2,1)S(1)}, bf16[96,384]{1,0:T(8,128)(2,1)S(1)}, u32[]{:S(2)}, u32[]{:S(2)}) collective-permute-start(bf16[96,384]{1,0:T(8,128)(2,1)S(1)} %get-tuple-element.60), channel_id=1, source_target_pairs={{0,12},{4,0},{8,4},{12,8},{1,13},{5,1},{9,5},{13,9},{2,14},{6,2},{... | collective-permute-start | bytes 221192 | tf_op jit(solution)/shard_map/ppermute | solution.py:51
  58.1 0.9 %shard_map.96 = bf16[1,2,8,32,384]{4,3,2,1,0:T(8,128)(2,1)} custom-call(bf16[2,64,384]{2,1,0:T(8,128)(2,1)S(1)} %get-tuple-element.36.refs_0_, bf16[2,64,384]{2,1,0:T(8,128)(2,1)S(1)} %collective-permute-done.3.refs_1_, bf16[2,64,384]{2,1,0:T(8,128)(2,1)S(1)} %collective-permute-done.4.refs_2_, bf16[2,64,384]{2,1,0:T(8,128)(2,1)S(1)} %collective-permute-done.5.refs_3_, ...), custom_call_target="tpu_custom_call" | custom-call | bytes 1179648 | tf_op jit(solution)/shard_map/pallas_call | solution.py:19
  58.9 0.0 collective-permute-done.10.refs_2_
  58.9 0.0 collective-permute-done.11.refs_3_
  58.9 2.9 %shard_map.98 = bf16[1,2,8,32,384]{4,3,2,1,0:T(8,128)(2,1)} custom-call(bf16[2,64,384]{2,1,0:T(8,128)(2,1)S(1)} %get-tuple-element.47.refs_0_, bf16[2,64,384]{2,1,0:T(8,128)(2,1)S(1)} %collective-permute-done.9.refs_1_, bf16[2,64,384]{2,1,0:T(8,128)(2,1)S(1)} %collective-permute-done.10.refs_2_, bf16[2,64,384]{2,1,0:T(8,128)(2,1)S(1)} %collective-permute-done.11.refs_3_, ...), custom_call_target="tpu_custom_call" | custom-call | flops 19267584 | bytes 1254912 | tf_op jit(solution)/shard_map/pallas_call | solution.py:19
  61.8 0.0 collective-permute-done.14.refs_0_
  61.8 1.5 %collective-permute-done.15.refs_1_ = bf16[96,384]{1,0:T(8,128)(2,1)S(1)} collective-permute-done((bf16[96,384]{1,0:T(8,128)(2,1)S(1)}, bf16[96,384]{1,0:T(8,128)(2,1)S(1)}, u32[]{:S(2)}, u32[]{:S(2)}) %collective-permute-start.15) | collective-permute-done | bytes 73760 | tf_op jit(solution)/shard_map/ppermute | solution.py:51
  63.3 0.7 %shard_map.102 = f32[96,384]{1,0:T(8,128)} custom-call(f32[96,384]{1,0:T(8,128)S(1)} %get-tuple-element.57.keep_in, bf16[96,384]{1,0:T(8,128)(2,1)S(1)} %collective-permute-done.14.refs_0_, bf16[96,384]{1,0:T(8,128)(2,1)S(1)} %collective-permute-done.15.refs_1_, bf16[96,384]{1,0:T(8,128)(2,1)S(1)} %collective-permute-done.16.refs_2_), custom_call_target="tpu_custom_call" | custom-call | bytes 516096 | tf_op jit(solution)/shard_map/pallas_call | solution.py:19
  (15 shorter events, 0.0 us)
Async XLA Ops:
  0.6 0.9 %copy-start = (f32[7,7,384]{2,1,0:T(8,128)S(1)}, f32[7,7,384]{2,1,0:T(8,128)}, u32[]{:S(2)}) copy-start(f32[7,7,384]{2,1,0:T(8,128)} %param.9) | copy-start | bytes 225796
  1.5 1.0 %copy-start.1 = (bf16[1,2,8,32,384]{4,3,2,1,0:T(8,128)(2,1)S(1)}, bf16[1,2,8,32,384]{4,3,2,1,0:T(8,128)(2,1)}, u32[]{:S(2)}) copy-start(bf16[1,2,8,32,384]{4,3,2,1,0:T(8,128)(2,1)} %refs_4_.5) | copy-start | bytes 1179652
  2.5 1.0 %copy-start.3 = (bf16[1,2,8,32,384]{4,3,2,1,0:T(8,128)(2,1)S(1)}, bf16[1,2,8,32,384]{4,3,2,1,0:T(8,128)(2,1)}, u32[]{:S(2)}) copy-start(bf16[1,2,8,32,384]{4,3,2,1,0:T(8,128)(2,1)} %refs_4_.4) | copy-start | bytes 1179652
  5.6 8.8 %collective-permute-start = (bf16[2,64,384]{2,1,0:T(8,128)(2,1)S(1)}, bf16[2,64,384]{2,1,0:T(8,128)(2,1)S(1)}, u32[]{:S(2)}, u32[]{:S(2)}) collective-permute-start(bf16[2,64,384]{2,1,0:T(8,128)(2,1)S(1)} %get-tuple-element.33), channel_id=1, source_target_pairs={{0,4},{4,8},{8,12},{12,0},{1,5},{5,9},{9,13},{13,1},{2,6},{6,10},{... | collective-permute-start | bytes 294920 | tf_op jit(solution)/shard_map/ppermute | solution.py:51
  8.7 12.7 %collective-permute-start.1 = (bf16[2,64,384]{2,1,0:T(8,128)(2,1)S(1)}, bf16[2,64,384]{2,1,0:T(8,128)(2,1)S(1)}, u32[]{:S(2)}, u32[]{:S(2)}) collective-permute-start(bf16[2,64,384]{2,1,0:T(8,128)(2,1)S(1)} %get-tuple-element.34), channel_id=1, source_target_pairs={{0,8},{4,12},{8,0},{12,4},{1,9},{5,13},{9,1},{13,5},{2,10},{6,14},... | collective-permute-start | bytes 294920 | tf_op jit(solution)/shard_map/ppermute | solution.py:51
  11.3 10.1 %collective-permute-start.2 = (bf16[2,64,384]{2,1,0:T(8,128)(2,1)S(1)}, bf16[2,64,384]{2,1,0:T(8,128)(2,1)S(1)}, u32[]{:S(2)}, u32[]{:S(2)}) collective-permute-start(bf16[2,64,384]{2,1,0:T(8,128)(2,1)S(1)} %get-tuple-element.35), channel_id=1, source_target_pairs={{0,12},{4,0},{8,4},{12,8},{1,13},{5,1},{9,5},{13,9},{2,14},{6,2},{... | collective-permute-start | bytes 294920 | tf_op jit(solution)/shard_map/ppermute | solution.py:51
  12.7 15.0 %collective-permute-start.6 = (bf16[2,64,384]{2,1,0:T(8,128)(2,1)S(1)}, bf16[2,64,384]{2,1,0:T(8,128)(2,1)S(1)}, u32[]{:S(2)}, u32[]{:S(2)}) collective-permute-start(bf16[2,64,384]{2,1,0:T(8,128)(2,1)S(1)} %get-tuple-element.41), channel_id=1, source_target_pairs={{0,4},{4,8},{8,12},{12,0},{1,5},{5,9},{9,13},{13,1},{2,6},{6,10},{... | collective-permute-start | bytes 294920 | tf_op jit(solution)/shard_map/ppermute | solution.py:51
  13.3 14.4 %collective-permute-start.7 = (bf16[2,64,384]{2,1,0:T(8,128)(2,1)S(1)}, bf16[2,64,384]{2,1,0:T(8,128)(2,1)S(1)}, u32[]{:S(2)}, u32[]{:S(2)}) collective-permute-start(bf16[2,64,384]{2,1,0:T(8,128)(2,1)S(1)} %get-tuple-element.42), channel_id=1, source_target_pairs={{0,8},{4,12},{8,0},{12,4},{1,9},{5,13},{9,1},{13,5},{2,10},{6,14},... | collective-permute-start | bytes 294920 | tf_op jit(solution)/shard_map/ppermute | solution.py:51
  14.4 13.3 %collective-permute-start.8 = (bf16[2,64,384]{2,1,0:T(8,128)(2,1)S(1)}, bf16[2,64,384]{2,1,0:T(8,128)(2,1)S(1)}, u32[]{:S(2)}, u32[]{:S(2)}) collective-permute-start(bf16[2,64,384]{2,1,0:T(8,128)(2,1)S(1)} %get-tuple-element.43), channel_id=1, source_target_pairs={{0,12},{4,0},{8,4},{12,8},{1,13},{5,1},{9,5},{13,9},{2,14},{6,2},{... | collective-permute-start | bytes 294920 | tf_op jit(solution)/shard_map/ppermute | solution.py:51
  21.4 1.3 %copy-start.5 = (bf16[384,1536]{1,0:T(8,128)(2,1)S(1)}, bf16[384,1536]{1,0:T(8,128)(2,1)}, u32[]{:S(2)}) copy-start(bf16[384,1536]{1,0:T(8,128)(2,1)} %refs_9_.1) | copy-start | bytes 3538948
  22.7 1.3 %copy-start.7 = (bf16[1536,384]{1,0:T(8,128)(2,1)S(1)}, bf16[1536,384]{1,0:T(8,128)(2,1)}, u32[]{:S(2)}) copy-start(bf16[1536,384]{1,0:T(8,128)(2,1)} %refs_10_.1) | copy-start | bytes 3538948
  24.0 0.8 %copy-start.8 = (f32[31,384]{1,0:T(8,128)S(1)}, f32[31,384]{1,0:T(8,128)}, u32[]{:S(2)}) copy-start(f32[31,384]{1,0:T(8,128)} %refs_7_.3) | copy-start | bytes 142852
  24.8 2.9 %copy-start.6 = (bf16[384,1536]{1,0:T(8,128)(2,1)S(1)}, bf16[384,1536]{1,0:T(8,128)(2,1)}, u32[]{:S(2)}) copy-start(bf16[384,1536]{1,0:T(8,128)(2,1)} %refs_9_.1) | copy-start | bytes 3538948
  31.7 2.1 %collective-permute-start.12 = (bf16[8,96,384]{2,1,0:T(8,128)(2,1)S(1)}, bf16[8,96,384]{2,1,0:T(8,128)(2,1)S(1)}, u32[]{:S(2)}, u32[]{:S(2)}) collective-permute-start(bf16[8,96,384]{2,1,0:T(8,128)(2,1)S(1)} %get-tuple-element.54), channel_id=1, source_target_pairs={{0,1},{1,0},{2,3},{3,2},{4,5},{5,4},{6,7},{7,6},{8,9},{9,8},{10,11... | collective-permute-start | bytes 1769480 | tf_op jit(solution)/shard_map/ppermute | solution.py:309
  33.8 24.3 %copy-start.4 = (bf16[1,2,8,32,384]{4,3,2,1,0:T(8,128)(2,1)S(1)}, bf16[1,2,8,32,384]{4,3,2,1,0:T(8,128)(2,1)}, u32[]{:S(2)}) copy-start(bf16[1,2,8,32,384]{4,3,2,1,0:T(8,128)(2,1)} %refs_4_.4) | copy-start | bytes 1179652
  33.9 25.0 %copy-start.2 = (bf16[1,2,8,32,384]{4,3,2,1,0:T(8,128)(2,1)S(1)}, bf16[1,2,8,32,384]{4,3,2,1,0:T(8,128)(2,1)}, u32[]{:S(2)}) copy-start(bf16[1,2,8,32,384]{4,3,2,1,0:T(8,128)(2,1)} %refs_4_.5) | copy-start | bytes 1179652
  33.9 12.7 %collective-permute-start.13 = (bf16[4,96,384]{2,1,0:T(8,128)(2,1)S(1)}, bf16[4,96,384]{2,1,0:T(8,128)(2,1)S(1)}, u32[]{:S(2)}, u32[]{:S(2)}) collective-permute-start(bf16[4,96,384]{2,1,0:T(8,128)(2,1)S(1)} %get-tuple-element.56), channel_id=1, source_target_pairs={{0,2},{1,3},{2,0},{3,1},{4,6},{5,7},{6,4},{7,5},{8,10},{9,11},{10,... | collective-permute-start | bytes 884744 | tf_op jit(solution)/shard_map/ppermute | solution.py:311
  35.4 9.1 %collective-permute-start.3 = (bf16[2,64,384]{2,1,0:T(8,128)(2,1)S(1)}, bf16[2,64,384]{2,1,0:T(8,128)(2,1)S(1)}, u32[]{:S(2)}, u32[]{:S(2)}) collective-permute-start(bf16[2,64,384]{2,1,0:T(8,128)(2,1)S(1)} %get-tuple-element.37), channel_id=1, source_target_pairs={{0,4},{4,8},{8,12},{12,0},{1,5},{5,9},{9,13},{13,1},{2,6},{6,10},{... | collective-permute-start | bytes 294920 | tf_op jit(solution)/shard_map/ppermute | solution.py:51
  38.8 12.7 %collective-permute-start.4 = (bf16[2,64,384]{2,1,0:T(8,128)(2,1)S(1)}, bf16[2,64,384]{2,1,0:T(8,128)(2,1)S(1)}, u32[]{:S(2)}, u32[]{:S(2)}) collective-permute-start(bf16[2,64,384]{2,1,0:T(8,128)(2,1)S(1)} %get-tuple-element.38), channel_id=1, source_target_pairs={{0,8},{4,12},{8,0},{12,4},{1,9},{5,13},{9,1},{13,5},{2,10},{6,14},... | collective-permute-start | bytes 294920 | tf_op jit(solution)/shard_map/ppermute | solution.py:51
  41.4 10.1 %collective-permute-start.5 = (bf16[2,64,384]{2,1,0:T(8,128)(2,1)S(1)}, bf16[2,64,384]{2,1,0:T(8,128)(2,1)S(1)}, u32[]{:S(2)}, u32[]{:S(2)}) collective-permute-start(bf16[2,64,384]{2,1,0:T(8,128)(2,1)S(1)} %get-tuple-element.39), channel_id=1, source_target_pairs={{0,12},{4,0},{8,4},{12,8},{1,13},{5,1},{9,5},{13,9},{2,14},{6,2},{... | collective-permute-start | bytes 294920 | tf_op jit(solution)/shard_map/ppermute | solution.py:51
  41.4 13.0 %collective-permute-start.9 = (bf16[2,64,384]{2,1,0:T(8,128)(2,1)S(1)}, bf16[2,64,384]{2,1,0:T(8,128)(2,1)S(1)}, u32[]{:S(2)}, u32[]{:S(2)}) collective-permute-start(bf16[2,64,384]{2,1,0:T(8,128)(2,1)S(1)} %get-tuple-element.48), channel_id=1, source_target_pairs={{0,4},{4,8},{8,12},{12,0},{1,5},{5,9},{9,13},{13,1},{2,6},{6,10},{... | collective-permute-start | bytes 294920 | tf_op jit(solution)/shard_map/ppermute | solution.py:51
  44.6 14.3 %collective-permute-start.10 = (bf16[2,64,384]{2,1,0:T(8,128)(2,1)S(1)}, bf16[2,64,384]{2,1,0:T(8,128)(2,1)S(1)}, u32[]{:S(2)}, u32[]{:S(2)}) collective-permute-start(bf16[2,64,384]{2,1,0:T(8,128)(2,1)S(1)} %get-tuple-element.49), channel_id=1, source_target_pairs={{0,8},{4,12},{8,0},{12,4},{1,9},{5,13},{9,1},{13,5},{2,10},{6,14},... | collective-permute-start | bytes 294920 | tf_op jit(solution)/shard_map/ppermute | solution.py:51
  46.6 12.3 %collective-permute-start.11 = (bf16[2,64,384]{2,1,0:T(8,128)(2,1)S(1)}, bf16[2,64,384]{2,1,0:T(8,128)(2,1)S(1)}, u32[]{:S(2)}, u32[]{:S(2)}) collective-permute-start(bf16[2,64,384]{2,1,0:T(8,128)(2,1)S(1)} %get-tuple-element.50), channel_id=1, source_target_pairs={{0,12},{4,0},{8,4},{12,8},{1,13},{5,1},{9,5},{13,9},{2,14},{6,2},{... | collective-permute-start | bytes 294920 | tf_op jit(solution)/shard_map/ppermute | solution.py:51
  51.5 10.3 %collective-permute-start.14 = (bf16[96,384]{1,0:T(8,128)(2,1)S(1)}, bf16[96,384]{1,0:T(8,128)(2,1)S(1)}, u32[]{:S(2)}, u32[]{:S(2)}) collective-permute-start(bf16[96,384]{1,0:T(8,128)(2,1)S(1)} %get-tuple-element.58), channel_id=1, source_target_pairs={{0,4},{4,8},{8,12},{12,0},{1,5},{5,9},{9,13},{13,1},{2,6},{6,10},{... | collective-permute-start | bytes 221192 | tf_op jit(solution)/shard_map/ppermute | solution.py:51
  51.5 11.8 %collective-permute-start.15 = (bf16[96,384]{1,0:T(8,128)(2,1)S(1)}, bf16[96,384]{1,0:T(8,128)(2,1)S(1)}, u32[]{:S(2)}, u32[]{:S(2)}) collective-permute-start(bf16[96,384]{1,0:T(8,128)(2,1)S(1)} %get-tuple-element.59), channel_id=1, source_target_pairs={{0,8},{4,12},{8,0},{12,4},{1,9},{5,13},{9,1},{13,5},{2,10},{6,14},... | collective-permute-start | bytes 221192 | tf_op jit(solution)/shard_map/ppermute | solution.py:51
  54.4 8.8 %collective-permute-start.16 = (bf16[96,384]{1,0:T(8,128)(2,1)S(1)}, bf16[96,384]{1,0:T(8,128)(2,1)S(1)}, u32[]{:S(2)}, u32[]{:S(2)}) collective-permute-start(bf16[96,384]{1,0:T(8,128)(2,1)S(1)} %get-tuple-element.60), channel_id=1, source_target_pairs={{0,12},{4,0},{8,4},{12,8},{1,13},{5,1},{9,5},{13,9},{2,14},{6,2},{... | collective-permute-start | bytes 221192 | tf_op jit(solution)/shard_map/ppermute | solution.py:51

commit v2 on v1

--- a/solution.py
+++ b/solution.py
@@ -13,16 +13,28 @@
 VMEM_LIMIT = 32 * 1024 * 1024
 
 
-def call(body, outs, scratch, *args, flops=0, limit=VMEM_LIMIT):
-    moved = sum(a.size * a.dtype.itemsize for a in args)
-    moved += sum(o.size * o.dtype.itemsize for o in outs)
+def call(body, outs, scratch, *args, cost=0, far=0, wait=(), limit=VMEM_LIMIT):
+    specs = [pl.BlockSpec(memory_space=pltpu.HBM)] * far
+    specs += [pl.BlockSpec(memory_space=pltpu.VMEM)] * (len(args) - far)
+    args = [
+        pltpu.with_memory_space_constraint(a, pltpu.HBM) if i < far else a
+        for i, a in enumerate(args)
+    ]
+    given = len(args)
+    for a in wait:
+        specs.append(pl.BlockSpec(memory_space=pl.ANY))
+        args.append(pltpu.with_memory_space_constraint(a, pltpu.HBM) if a.ndim == 5 else a)
+
+    def kernel(*refs):
+        body(*refs[:given], *refs[given + len(wait) :])
+
     return pl.pallas_call(
-        body,
+        kernel,
         out_shape=tuple(outs),
-        in_specs=[pl.BlockSpec(memory_space=pltpu.VMEM)] * len(args),
+        in_specs=specs,
         out_specs=tuple([pl.BlockSpec(memory_space=pltpu.VMEM)] * len(outs)),
         scratch_shapes=list(scratch),
-        cost_estimate=pl.CostEstimate(flops=flops, bytes_accessed=moved, transcendentals=0),
+        cost_estimate=pl.CostEstimate(flops=cost, bytes_accessed=cost, transcendentals=0),
         compiler_params=pltpu.CompilerParams(vmem_limit_bytes=limit),
     )(*args)
 
@@ -53,13 +65,14 @@
 
 
 def conv_rows(pad_ref, kernel_ref, block, col, height, flip, emit):
-    taps = kernel_ref.shape[1]
+    taps = kernel_ref.shape[0]
+    lanes = slice(block * LANES, (block + 1) * LANES)
     radius = taps // 2
     acc = [None] * height
     for col_off in range(taps):
         shift = radius - col_off if flip else col_off - radius
         weights = [
-            kernel_ref[block, row_off, pl.ds(col_off, 1), :] for row_off in range(taps)
+            kernel_ref[row_off, pl.ds(col_off, 1), lanes] for row_off in range(taps)
         ]
         for row in range(height):
             values = pad_ref[block, :, row, pl.ds(PAD + col + shift, 8), :]
@@ -80,18 +93,41 @@
 
 
 def spatial_fwd(count, *refs):
-    clips, cot, kernel = refs[:3]
-    firsts = refs[3 : 3 + count]
-    cots = refs[3 + count : 3 + 2 * count]
-    pad_ref, flat = refs[3 + 2 * count :]
-    _, frames, height, width, channels = clips.shape
+    clips_far, cot_far, kernel_far = refs[:3]
+    held = (len(refs) - 3 - 2 * count - 5) // 2
+    fars = refs[3 : 3 + held]
+    refs = refs[3 + held :]
+    firsts = refs[:count]
+    cots = refs[count : 2 * count]
+    nears = refs[2 * count : 2 * count + held]
+    clips, kernel, pad_ref, flat, sems = refs[2 * count + held :]
+    frames, height, width, channels = clips.shape
     blocks = channels // LANES
     pixels = height * width // count
+    rows = height // count
+    copies = [
+        pltpu.make_async_copy(clips_far.at[0], clips, sems.at[0]),
+        pltpu.make_async_copy(kernel_far, kernel, sems.at[1]),
+    ]
+    for step in range(count):
+        base = slot_to(step, count) * rows
+        copies.append(
+            pltpu.make_async_copy(
+                cot_far.at[0, :, pl.ds(base, rows)], cots[step], sems.at[2 + step]
+            )
+        )
+    for index in range(held):
+        copies.append(
+            pltpu.make_async_copy(fars[index], nears[index], sems.at[2 + count + index])
+        )
+    for copy in copies:
+        copy.start()
     clear_pads(pad_ref, width)
+    copies[0].wait()
     for block in range(blocks):
         lanes = slice(block * LANES, (block + 1) * LANES)
-        pad_ref[block, :, :, PAD : PAD + width, :] = clips[0, :, :, :, lanes].astype(F32)
-
+        pad_ref[block, :, :, PAD : PAD + width, :] = clips[:, :, :, lanes].astype(F32)
+    copies[1].wait()
     for block in range(blocks):
         lanes = slice(block * LANES, (block + 1) * LANES)
         for col in range(0, width, 8):
@@ -100,13 +136,13 @@
                 flat[:, row, pl.ds(col, 8), lanes] = value
 
             conv_rows(pad_ref, kernel, block, col, height, False, emit)
-    rows = height // count
     for step in range(count):
         base = slot_to(step, count) * rows
         firsts[step][...] = (
             flat[:, pl.ds(base, rows), :, :].reshape(frames, pixels, channels).astype(BF16)
         )
-        cots[step][...] = cot[0, :, pl.ds(base, rows), :, :].reshape(frames, pixels, channels)
+    for copy in copies[2:]:
+        copy.wait()
 
 
 def spatial_bwd(count, *refs):
@@ -172,7 +208,8 @@
     for step in range(count):
         frames = pieces[step].shape[0]
         base = slot_from(step, count) * frames
-        target[pl.ds(base, frames)] = pieces[step][...].astype(target.dtype)
+        piece = pieces[step][...].reshape((frames,) + target.shape[1:])
+        target[pl.ds(base, frames)] = piece.astype(target.dtype)
 
 
 def mlp_fwd(count, chunk, *refs):
@@ -191,7 +228,7 @@
     inv_std[...] = inverse
     norm = centred * inverse
     normed[...] = norm
-    scaled[...] = (norm * gain[...]).astype(BF16)
+    scaled[...] = (norm * gain[...].reshape(1, channels)).astype(BF16)
     for start in range(0, w_expand.shape[1], chunk):
         part = slice(start, start + chunk)
         pre = jnp.dot(scaled[...], w_expand[:, part], preferred_element_type=F32)
@@ -207,22 +244,38 @@
         branches[step][...] = branch[pl.ds(base, own)].astype(BF16)
 
 
-def mlp_bwd(count, chunk, *refs):
+def hidden_bwd(count, chunk, with_grad, *refs):
     pieces = refs[:count]
-    slope, normed, inv_std, taps, gain, w_expand, w_project = refs[count : count + 7]
-    outs = refs[count + 7 : 2 * count + 7]
-    d_pre, grads, d_second, d_first = refs[2 * count + 7 :]
+    slope, w_project, scaled, d_pre = refs[count : count + 4]
+    grads = refs[-1]
     frames, pixels, channels = grads.shape
     tokens = frames * pixels
     place_frames(count, pieces, grads)
     grad_rows = grads[...].reshape(tokens, channels).astype(BF16)
     last = (((1,), (1,)), ((), ()))
-    for start in range(0, w_expand.shape[1], chunk):
+    for start in range(0, w_project.shape[0], chunk):
         part = slice(start, start + chunk)
         d_hidden = lax.dot_general(grad_rows, w_project[part, :], last, preferred_element_type=F32)
         d_pre[:, part] = (d_hidden * slope[:, part].astype(F32)).astype(BF16)
+    if with_grad:
+        keep, send, full = refs[count + 4 : count + 7]
+        full[...] = lax.dot_general(
+            d_pre[...], scaled[...], (((0,), (0,)), ((), ())), preferred_element_type=F32
+        ).reshape(full.shape)
+        core = lax.rem(lax.axis_index("dp"), 2)
+        for pair in range(full.shape[0] // 2):
+            keep[pair] = full[2 * pair + core]
+            send[pair] = full[2 * pair + 1 - core].astype(BF16)
+
+
+def token_bwd(count, *refs):
+    d_pre, normed, inv_std, taps, gain, w_expand = refs[:6]
+    outs = refs[6 : count + 6]
+    d_second, d_first = refs[count + 6 :]
+    frames, pixels, channels = d_second.shape
+    last = (((1,), (1,)), ((), ()))
     d_scaled = lax.dot_general(d_pre[...], w_expand[...], last, preferred_element_type=F32)
-    d_normed = d_scaled * gain[...]
+    d_normed = d_scaled * gain[...].reshape(1, channels)
     norm = normed[...]
     d_tokens = inv_std[...] * (
         d_normed
@@ -247,17 +300,6 @@
         piece = pieces[step][...].reshape(frames, rows, width, channels).astype(F32)
         here = (0, slice(None), pl.ds(base, rows))
         out_ref[here] = (clips[here].astype(F32) + piece).astype(BF16)
-
-
-def weight_grad(d_pre, scaled, keep, send, full):
-    block = keep.shape[1]
-    full[...] = lax.dot_general(
-        d_pre[...], scaled[...], (((0,), (0,)), ((), ())), preferred_element_type=F32
-    ).reshape(full.shape)
-    core = lax.rem(lax.axis_index("dp"), 2)
-    for pair in range(full.shape[0] // 2):
-        keep[pair] = full[2 * pair + core]
-        send[pair] = full[2 * pair + 1 - core].astype(BF16)
 
 
 def fold_pair(keep_in, got, keep, send):
@@ -268,14 +310,18 @@
         send[slot] = (keep_in[other] + got[other].astype(F32)).astype(BF16)
 
 
-def fold_tm(count, keep_in, got, keep, *sends):
-    for step in range(count):
-        slot = slot_to(step, count)
-        total = keep_in[slot] + got[slot].astype(F32)
-        if step == 0:
-            keep[...] = total
-        else:
-            sends[step - 1][...] = total.astype(BF16)
+def fold_near(keep_in, got, keep, *sends):
+    me = lax.axis_index("tm")
+    for far in range(2):
+        mine = lax.bitwise_xor(me, 2 * far)
+        other = lax.bitwise_xor(me, 2 * far + 1)
+        keep[far] = keep_in[mine] + got[mine].astype(F32)
+        sends[far][...] = (keep_in[other] + got[other].astype(F32)).astype(BF16)
+
+
+def fold_far(keep_in, got, got_far, keep, send):
+    keep[...] = keep_in[0] + got[...].astype(F32)
+    send[...] = (keep_in[1] + got_far[...].astype(F32)).astype(BF16)
 
 
 def fold_last(scale_factor, keep_in, *refs):
@@ -285,42 +331,26 @@
     refs[-1][...] = total * scale_factor
 
 
-def scatter_grad(d_pre, scaled, count, scale_factor):
-    hid, channels = d_pre.shape[1], scaled.shape[1]
-    sides = lax.axis_size("dp")
-    if count == 1 or sides != 4:
-        whole = lax.dot_general(
-            d_pre, scaled, (((0,), (0,)), ((), ())), preferred_element_type=F32
-        )
-        return (
-            lax.psum_scatter(whole, ("tm", "dp"), scatter_dimension=0, tiled=True) * scale_factor
-        )
-    block = hid // (count * sides)
-    half = (2 * count, block, channels)
+def scatter_grad(keep, send, count, scale_factor, d_first, grad_clips):
+    channels = keep.shape[-1]
+    block = keep.shape[1]
     quarter = (count, block, channels)
+    piece = (block, channels)
+    got = lax.ppermute(send, "dp", [(i, i ^ 1) for i in range(4)])
     keep, send = call(
-        weight_grad,
-        [struct(half, F32), struct(half, BF16)],
-        [pltpu.VMEM((4 * count, block, channels), F32)],
-        d_pre,
-        scaled,
-        flops=2 * hid * channels * d_pre.shape[0],
-    )
-    got = lax.ppermute(send, "dp", [(i, i ^ 1) for i in range(4)])
-    keep, send = call(fold_pair, [struct(quarter, F32), struct(quarter, BF16)], [], keep, got)
+        fold_pair, [struct(quarter, F32), struct(quarter, BF16)], [], keep, got, wait=[d_first]
+    )
     got = lax.ppermute(send, "dp", [(i, i ^ 2) for i in range(4)])
-    piece = (block, channels)
+    pair = (2,) + piece
     keep, *sends = call(
-        functools.partial(fold_tm, count),
-        [struct(piece, F32)] + [struct(piece, BF16)] * (count - 1),
-        [],
-        keep,
-        got,
-    )
-    got = exchange([keep] + list(sends))[1:]
-    return call(
-        functools.partial(fold_last, scale_factor), [struct(piece, F32)], [], keep, *got
-    )[0]
+        fold_near, [struct(pair, F32), struct(piece, BF16), struct(piece, BF16)], [], keep, got
+    )
+    near = [lax.ppermute(send, "tm", [(i, i ^ 1) for i in range(4)]) for send in sends]
+    keep, send = call(
+        fold_far, [struct(piece, F32), struct(piece, BF16)], [], keep, *near, wait=[grad_clips]
+    )
+    got = lax.ppermute(send, "tm", [(i, i ^ 2) for i in range(4)])
+    return call(functools.partial(fold_last, scale_factor), [struct(piece, F32)], [], keep, got)[0]
 
 
 def local(clips, cotangent, spatial_kernel, temporal_kernel, norm_gain, w_expand, w_project):
@@ -340,7 +370,7 @@
     def to_columns(pieces):
         if count > 1:
             return exchange(pieces)
-        whole = pieces[0][None]
+        whole = pieces[0].reshape(1, frames, pixels, channels)
         return [lax.all_to_all(whole, "tm", split_axis=2, concat_axis=1, tiled=True)[0]]
 
     def to_frames(pieces):
@@ -349,24 +379,29 @@
         whole = pieces[0][None]
         return [lax.all_to_all(whole, "tm", split_axis=1, concat_axis=2, tiled=True)[0]]
 
-    kernel = spatial_kernel.reshape(spatial_kernel.shape[:2] + (blocks, LANES)).transpose(2, 0, 1, 3)
-    gain = norm_gain.reshape(1, channels)
     pad = pltpu.VMEM((blocks, frames, height, width + 2 * PAD, LANES), F32)
-    conv_flops = 2 * 49 * frames * pixels * channels
-    mlp_flops = 2 * tokens * channels * hid
-
     piece = struct((frames, pixels // count, channels), BF16)
+    cot_piece = struct((frames, height // count, width, channels), BF16)
+    held = [temporal_kernel, w_expand, w_project]
     outs = call(
         functools.partial(spatial_fwd, count),
-        [piece] * (2 * count),
-        [pad, pltpu.VMEM((frames, height, width, channels), F32)],
+        [piece] * count + [cot_piece] * count + [struct(a.shape, a.dtype) for a in held],
+        [
+            pltpu.VMEM(clips.shape[1:], BF16),
+            pltpu.VMEM(spatial_kernel.shape, F32),
+            pad,
+            pltpu.VMEM((frames, height, width, channels), F32),
+            pltpu.SemaphoreType.DMA((2 + count + len(held),)),
+        ],
         clips,
         cotangent,
-        kernel,
-        flops=conv_flops,
+        spatial_kernel,
+        *held,
+        far=3 + len(held),
     )
     firsts = to_columns(list(outs[:count]))
-    cots = to_columns(list(outs[count:]))
+    cots = to_columns(list(outs[count : 2 * count]))
+    temporal_kernel, w_expand, w_project = outs[2 * count :]
 
     column = (all_frames, columns, channels)
     back = struct((all_frames // count, columns, channels), BF16)
@@ -387,45 +422,59 @@
         ],
         *firsts,
         temporal_kernel,
-        gain,
+        norm_gain,
         w_expand,
         w_project,
-        flops=2 * mlp_flops,
     )
     scaled, slope, normed, inv_std = outs[count:]
     branches = to_frames(list(outs[:count]))
 
+    sides = lax.axis_size("dp")
+    staged = count == 4 and sides == 4
+    half = (2 * count, hid // (sides * count), channels)
     outs = call(
-        functools.partial(mlp_bwd, count, chunk),
-        [back] * count + [struct((tokens, hid), BF16)],
-        [pltpu.VMEM(column, F32), pltpu.VMEM(column, F32), pltpu.VMEM(column, F32)],
+        functools.partial(hidden_bwd, count, chunk, staged),
+        [struct((tokens, hid), BF16)] + [struct(half, F32), struct(half, BF16)] * staged,
+        [pltpu.VMEM((2 * half[0],) + half[1:], F32)] * staged + [pltpu.VMEM(column, F32)],
         *cots,
         slope,
+        w_project,
+        scaled,
+    )
+    d_pre = outs[0]
+    shares = outs[1:]
+    outs = call(
+        functools.partial(token_bwd, count),
+        [back] * count,
+        [pltpu.VMEM(column, F32), pltpu.VMEM(column, F32)],
+        d_pre,
         normed,
         inv_std,
         temporal_kernel,
-        gain,
+        norm_gain,
         w_expand,
-        w_project,
-        flops=2 * mlp_flops,
-    )
-    d_pre = outs[count]
-    d_firsts = to_frames(list(outs[:count]))
-
-    grad_expand = scatter_grad(d_pre, scaled, count, scale_factor)
-
+    )
+    d_firsts = to_frames(list(outs))
+
+    block_out = call(
+        functools.partial(add_residual, count), [struct(clips.shape, BF16)], [], *branches, clips
+    )[0]
     grad_clips = call(
         functools.partial(spatial_bwd, count),
         [struct(clips.shape, BF16)],
         [pad],
         *d_firsts,
         cotangent,
-        kernel,
-        flops=conv_flops,
+        spatial_kernel,
     )[0]
-    block_out = call(
-        functools.partial(add_residual, count), [struct(clips.shape, BF16)], [], *branches, clips
-    )[0]
+    if staged:
+        grad_expand = scatter_grad(*shares, count, scale_factor, outs[0], grad_clips)
+    else:
+        whole = lax.dot_general(
+            d_pre, scaled, (((0,), (0,)), ((), ())), preferred_element_type=F32
+        )
+        whole = lax.psum_scatter(whole, ("tm", "dp"), scatter_dimension=0, tiled=True)
+        grad_expand = whole * scale_factor
     return (block_out, grad_clips, grad_expand)
 
 

time: 64.4 us -> 57.4 us (0.89)
  local copies, waits for them, and re-layouts: 6.91 us -> 0.02 us
  starting transfers between devices: 31.5 us -> 26.3 us
  waiting for transfers between devices: 11.2 us -> 15.7 us
  Pallas kernels: 13.5 us -> 14.5 us
    ppermute x15 -> x12, starting transfers between devices: 29.9 us -> 20.6 us  [exchange(): got.append(lax.ppermute(pieces[step], 'tm', pairs))]
    unnamed x18 -> x8, local copies, waits for them, and re-layouts: 6.23 us -> 0.02 us
    ppermute x0 -> x3, starting transfers between devices: none -> 4.08 us  [the longest x2 2.72 us: scatter_grad(): lax.ppermute(send, 'tm', [(i, i ^ 1) for i in range(4)])]
    ppermute x0 -> x3, waiting for transfers between devices: none -> 2.78 us  [the longest x1 2.78 us: scatter_grad(): got = lax.ppermute(send, 'tm', [(i, i ^ 2) for i in range(4)])]
    ppermute x1, waiting for transfers between devices: 0.01 us -> 2.78 us  [scatter_grad(): got = lax.ppermute(send, 'dp', [(i, i ^ 2) for i in range(4)])]
    ppermute x1, waiting for transfers between devices: 1.99 us -> 0.25 us  [scatter_grad(): got = lax.ppermute(send, 'dp', [(i, i ^ 1) for i in range(4)])]
    pallas_call x9 -> x10, Pallas kernels: 13.5 us -> 14.5 us  [call(): pl.pallas_call(kernel, out_shape=tuple(outs), in_specs=specs, out_specs=t...]
    reshape x1 -> x0, local copies, waits for them, and re-layouts: 0.68 us -> none  [local(): gain = norm_gain.reshape(1, channels)]
  transfers between devices with their start and end apart: 17 -> 17, of which waited for: 5 -> 7; matrix products, arithmetic and copies ran while one was open for 1% -> 0% of each run, Pallas kernels for 10% -> 15%
where the time goes in v2:
time: 57.4 us; the launch traced here: 57.3 us
  starting transfers between devices  26.3 us (46%)
  waiting for transfers between devices  15.7 us (27%)
  Pallas kernels  14.5 us (25%)
  between operations  0.71 us (1%)
    ppermute x12, starting transfers between devices, exchange(): got.append(lax.ppermute(pieces[step], 'tm', pairs))  20.6 us
    pallas_call x10, Pallas kernels, call(): pl.pallas_call(kernel, out_shape=tuple(outs), in_specs=specs, out_specs=t...  14.5 us
    ppermute x12, waiting for transfers between devices, exchange(): got.append(lax.ppermute(pieces[step], 'tm', pairs))  9.86 us
    ppermute x1, waiting for transfers between devices, scatter_grad(): got = lax.ppermute(send, 'dp', [(i, i ^ 2) for i in range(4)])  2.78 us
    ppermute x1, waiting for transfers between devices, scatter_grad(): got = lax.ppermute(send, 'tm', [(i, i ^ 2) for i in range(4)])  2.78 us
    ppermute x2, starting transfers between devices, scatter_grad(): lax.ppermute(send, 'tm', [(i, i ^ 1) for i in range(4)])  2.72 us
    ppermute x1, starting transfers between devices, scatter_grad(): got = lax.ppermute(send, 'dp', [(i, i ^ 2) for i in range(4)])  1.55 us
    ppermute x1, starting transfers between devices, scatter_grad(): got = lax.ppermute(send, 'tm', [(i, i ^ 2) for i in range(4)])  1.37 us
  transfers between devices with their start and end apart: 17, of which 7 were waited for; matrix products, arithmetic and copies ran while one was open for 0% of the time, Pallas kernels for 15%

profile of v2, /device:TPU:0, one launch (start us, length us, event | category | flops | bytes accessed | tf_op | source)
XLA Modules:
  0.0 57.3 jit_solution(14418734324327319562)
XLA Ops:
  0.6 0.0 copy-start.3
  0.6 3.1 %shard_map.94 = (bf16[2,64,384]{2,1,0:T(8,128)(2,1)S(1)}, bf16[2,64,384]{2,1,0:T(8,128)(2,1)S(1)}, bf16[2,64,384]{2,1,0:T(8,128)(2,1)S(1)}, bf16[2,64,384]{2,1,0...) custom-call(bf16[1,2,8,32,384]{4,3,2,1,0:T(8,128)(2,1)} %refs_4_.5, ...), custom_call_target="tpu_custom_call" | custom-call | tf_op jit(solution)/shard_map/pallas_call | solution.py:31
  3.8 3.1 %collective-permute-start = (bf16[2,64,384]{2,1,0:T(8,128)(2,1)S(1)}, bf16[2,64,384]{2,1,0:T(8,128)(2,1)S(1)}, u32[]{:S(2)}, u32[]{:S(2)}) collective-permute-start(bf16[2,64,384]{2,1,0:T(8,128)(2,1)S(1)} %get-tuple-element.37), channel_id=1, source_target_pairs={{0,4},{4,8},{8,12},{12,0},{1,5},{5,9},{9,13},{13,1},{2,6},{6,10},{... | collective-permute-start | bytes 294920 | tf_op jit(solution)/shard_map/ppermute | solution.py:63
  6.9 2.6 %collective-permute-start.1 = (bf16[2,64,384]{2,1,0:T(8,128)(2,1)S(1)}, bf16[2,64,384]{2,1,0:T(8,128)(2,1)S(1)}, u32[]{:S(2)}, u32[]{:S(2)}) collective-permute-start(bf16[2,64,384]{2,1,0:T(8,128)(2,1)S(1)} %get-tuple-element.38), channel_id=1, source_target_pairs={{0,8},{4,12},{8,0},{12,4},{1,9},{5,13},{9,1},{13,5},{2,10},{6,14},... | collective-permute-start | bytes 294920 | tf_op jit(solution)/shard_map/ppermute | solution.py:63
  9.5 1.3 %collective-permute-start.2 = (bf16[2,64,384]{2,1,0:T(8,128)(2,1)S(1)}, bf16[2,64,384]{2,1,0:T(8,128)(2,1)S(1)}, u32[]{:S(2)}, u32[]{:S(2)}) collective-permute-start(bf16[2,64,384]{2,1,0:T(8,128)(2,1)S(1)} %get-tuple-element.39), channel_id=1, source_target_pairs={{0,12},{4,0},{8,4},{12,8},{1,13},{5,1},{9,5},{13,9},{2,14},{6,2},{... | collective-permute-start | bytes 294920 | tf_op jit(solution)/shard_map/ppermute | solution.py:63
  10.8 0.7 %collective-permute-start.6 = (bf16[2,2,32,384]{3,2,1,0:T(8,128)(2,1)S(1)}, bf16[2,2,32,384]{3,2,1,0:T(8,128)(2,1)S(1)}, u32[]{:S(2)}, u32[]{:S(2)}) collective-permute-start(bf16[2,2,32,384]{3,2,1,0:T(8,128)(2,1)S(1)} %get-tuple-element.48), channel_id=1, source_target_pairs={{0,4},{4,8},{8,12},{12,0},{1,5},{5,9},{9,13},{13,1},{2,6},{6,10},{... | collective-permute-start | bytes 294920 | tf_op jit(solution)/shard_map/ppermute | solution.py:63
  11.5 0.3 collective-permute-start.7
  11.8 0.7 %collective-permute-done.refs_1_ = bf16[2,64,384]{2,1,0:T(8,128)(2,1)S(1)} collective-permute-done((bf16[2,64,384]{2,1,0:T(8,128)(2,1)S(1)}, bf16[2,64,384]{2,1,0:T(8,128)(2,1)S(1)}, u32[]{:S(2)}, u32[]{:S(2)}) %collective-permute-start) | collective-permute-done | bytes 98336 | tf_op jit(solution)/shard_map/ppermute | solution.py:63
  12.5 3.1 %collective-permute-start.8 = (bf16[2,2,32,384]{3,2,1,0:T(8,128)(2,1)S(1)}, bf16[2,2,32,384]{3,2,1,0:T(8,128)(2,1)S(1)}, u32[]{:S(2)}, u32[]{:S(2)}) collective-permute-start(bf16[2,2,32,384]{3,2,1,0:T(8,128)(2,1)S(1)} %get-tuple-element.50), channel_id=1, source_target_pairs={{0,12},{4,0},{8,4},{12,8},{1,13},{5,1},{9,5},{13,9},{2,14},{6,2},{... | collective-permute-start | bytes 294920 | tf_op jit(solution)/shard_map/ppermute | solution.py:63
  15.6 3.9 %collective-permute-done.1.refs_2_ = bf16[2,64,384]{2,1,0:T(8,128)(2,1)S(1)} collective-permute-done((bf16[2,64,384]{2,1,0:T(8,128)(2,1)S(1)}, bf16[2,64,384]{2,1,0:T(8,128)(2,1)S(1)}, u32[]{:S(2)}, u32[]{:S(2)}) %collective-permute-start.1) | collective-permute-done | bytes 98336 | tf_op jit(solution)/shard_map/ppermute | solution.py:63
  19.6 0.0 collective-permute-done.2.refs_3_
  19.6 0.0 copy-done.3
  19.6 2.9 %shard_map.95 = (bf16[2,64,384]{2,1,0:T(8,128)(2,1)S(1)}, bf16[2,64,384]{2,1,0:T(8,128)(2,1)S(1)}, bf16[2,64,384]{2,1,0:T(8,128)(2,1)S(1)}, bf16[2,64,384]{2,1,0...) custom-call(bf16[2,64,384]{2,1,0:T(8,128)(2,1)S(1)} %get-tuple-eleme, ...), custom_call_target="tpu_custom_call" | custom-call | tf_op jit(solution)/shard_map/pallas_call | solution.py:31
  22.5 0.0 collective-permute-done.6.refs_1_
  22.5 1.9 %collective-permute-done.7.refs_2_ = bf16[2,2,32,384]{3,2,1,0:T(8,128)(2,1)S(1)} collective-permute-done((bf16[2,2,32,384]{3,2,1,0:T(8,128)(2,1)S(1)}, bf16[2,2,32,384]{3,2,1,0:T(8,128)(2,1)S(1)}, u32[]{:S(2)}, u32[]{:S(2)}) %collective-permute-start.7) | collective-permute-done | bytes 98336 | tf_op jit(solution)/shard_map/ppermute | solution.py:63
  24.5 0.0 collective-permute-done.8.refs_3_
  24.5 2.2 %shard_map.97 = (bf16[512,1536]{1,0:T(8,128)(2,1)S(1)}, f32[8,96,384]{2,1,0:T(8,128)S(1)}, bf16[8,96,384]{2,1,0:T(8,128)(2,1)S(1)}) custom-call(bf16[2,2,32,384]{3,2,1,0:T(8,128)(2,1)S(1)} %get-tuple-element.47.refs_0_, bf16[2,2,32,384]{3,2,1,0:T(8,128)(2,1)S(1)} %collective-permute-done.6.refs_1_, ...), custom_call_target="tpu_custom_call" | custom-call | tf_op jit(solution)/shard_map/pallas_call | solution.py:31
  26.6 0.1 collective-permute-start.12
  26.7 1.7 %shard_map.98 = (bf16[2,64,384]{2,1,0:T(8,128)(2,1)S(1)}, bf16[2,64,384]{2,1,0:T(8,128)(2,1)S(1)}, bf16[2,64,384]{2,1,0:T(8,128)(2,1)S(1)}, bf16[2,64,384]{2,1,0:T(8,128)(2,1)S(1)}) custom-call(bf16[512,1536]{1,0:T(8,128)(2,1)S(1)} %get-tuple-element.53.refs_0_, f32[512,384]{1,0:T(8,128)S(1)} %get-tuple-element.54.refs_1_, ...), custom_call_target="tpu_custom_call" | custom-call | tf_op jit(solution)/shard_map/pallas_call | solution.py:31
  28.5 0.2 collective-permute-done.12.refs_1_
  28.7 0.1 shard_map.100
  28.8 1.6 %collective-permute-start.13 = (bf16[4,96,384]{2,1,0:T(8,128)(2,1)S(1)}, bf16[4,96,384]{2,1,0:T(8,128)(2,1)S(1)}, u32[]{:S(2)}, u32[]{:S(2)}) collective-permute-start(bf16[4,96,384]{2,1,0:T(8,128)(2,1)S(1)} %get-tuple-element.63), channel_id=1, source_target_pairs={{0,2},{1,3},{2,0},{3,1},{4,6},{5,7},{6,4},{7,5},{8,10},{9,11},{10,... | collective-permute-start | bytes 884744 | tf_op jit(solution)/shard_map/ppermute | solution.py:343
  30.4 2.6 %collective-permute-start.9 = (bf16[2,64,384]{2,1,0:T(8,128)(2,1)S(1)}, bf16[2,64,384]{2,1,0:T(8,128)(2,1)S(1)}, u32[]{:S(2)}, u32[]{:S(2)}) collective-permute-start(bf16[2,64,384]{2,1,0:T(8,128)(2,1)S(1)} %get-tuple-element.57), channel_id=1, source_target_pairs={{0,4},{4,8},{8,12},{12,0},{1,5},{5,9},{9,13},{13,1},{2,6},{6,10},{... | collective-permute-start | bytes 294920 | tf_op jit(solution)/shard_map/ppermute | solution.py:63
  33.0 1.6 %collective-permute-start.10 = (bf16[2,64,384]{2,1,0:T(8,128)(2,1)S(1)}, bf16[2,64,384]{2,1,0:T(8,128)(2,1)S(1)}, u32[]{:S(2)}, u32[]{:S(2)}) collective-permute-start(bf16[2,64,384]{2,1,0:T(8,128)(2,1)S(1)} %get-tuple-element.58), channel_id=1, source_target_pairs={{0,8},{4,12},{8,0},{12,4},{1,9},{5,13},{9,1},{13,5},{2,10},{6,14},... | collective-permute-start | bytes 294920 | tf_op jit(solution)/shard_map/ppermute | solution.py:63
  34.6 0.7 %collective-permute-start.11 = (bf16[2,64,384]{2,1,0:T(8,128)(2,1)S(1)}, bf16[2,64,384]{2,1,0:T(8,128)(2,1)S(1)}, u32[]{:S(2)}, u32[]{:S(2)}) collective-permute-start(bf16[2,64,384]{2,1,0:T(8,128)(2,1)S(1)} %get-tuple-element.59), channel_id=1, source_target_pairs={{0,12},{4,0},{8,4},{12,8},{1,13},{5,1},{9,5},{13,9},{2,14},{6,2},{... | collective-permute-start | bytes 294920 | tf_op jit(solution)/shard_map/ppermute | solution.py:63
  35.3 2.8 %collective-permute-done.13.refs_1_ = bf16[4,96,384]{2,1,0:T(8,128)(2,1)S(1)} collective-permute-done((bf16[4,96,384]{2,1,0:T(8,128)(2,1)S(1)}, bf16[4,96,384]{2,1,0:T(8,128)(2,1)S(1)}, u32[]{:S(2)}, u32[]{:S(2)}) %collective-permute-start.13) | collective-permute-done | bytes 294944 | tf_op jit(solution)/shard_map/ppermute | solution.py:343
  38.1 0.1 shard_map.101
  38.2 0.0 copy-start.1
  38.2 2.6 %collective-permute-start.14 = (bf16[96,384]{1,0:T(8,128)(2,1)S(1)}, bf16[96,384]{1,0:T(8,128)(2,1)S(1)}, u32[]{:S(2)}, u32[]{:S(2)}) collective-permute-start(bf16[96,384]{1,0:T(8,128)(2,1)S(1)} %get-tuple-element.65), channel_id=1, source_target_pairs={{0,4},{4,0},{8,12},{12,8},{1,5},{5,1},{9,13},{13,9},{2,6},{6,2},{1... | collective-permute-start | bytes 221192 | tf_op jit(solution)/shard_map/ppermute | solution.py:348
  40.8 0.1 collective-permute-start.15
  40.9 0.0 collective-permute-done.9.refs_1_
  40.9 1.9 %collective-permute-start.3 = (bf16[2,64,384]{2,1,0:T(8,128)(2,1)S(1)}, bf16[2,64,384]{2,1,0:T(8,128)(2,1)S(1)}, u32[]{:S(2)}, u32[]{:S(2)}) collective-permute-start(bf16[2,64,384]{2,1,0:T(8,128)(2,1)S(1)} %get-tuple-element.44), channel_id=1, source_target_pairs={{0,4},{4,8},{8,12},{12,0},{1,5},{5,9},{9,13},{13,1},{2,6},{6,10},{... | collective-permute-start | bytes 294920 | tf_op jit(solution)/shard_map/ppermute | solution.py:63
  42.8 0.0 collective-permute-done.10.refs_2_
  42.8 1.6 %collective-permute-start.4 = (bf16[2,64,384]{2,1,0:T(8,128)(2,1)S(1)}, bf16[2,64,384]{2,1,0:T(8,128)(2,1)S(1)}, u32[]{:S(2)}, u32[]{:S(2)}) collective-permute-start(bf16[2,64,384]{2,1,0:T(8,128)(2,1)S(1)} %get-tuple-element.45), channel_id=1, source_target_pairs={{0,8},{4,12},{8,0},{12,4},{1,9},{5,13},{9,1},{13,5},{2,10},{6,14},... | collective-permute-start | bytes 294920 | tf_op jit(solution)/shard_map/ppermute | solution.py:63
  44.5 0.0 collective-permute-done.11.refs_3_
  44.5 1.0 %collective-permute-start.5 = (bf16[2,64,384]{2,1,0:T(8,128)(2,1)S(1)}, bf16[2,64,384]{2,1,0:T(8,128)(2,1)S(1)}, u32[]{:S(2)}, u32[]{:S(2)}) collective-permute-start(bf16[2,64,384]{2,1,0:T(8,128)(2,1)S(1)} %get-tuple-element.46), channel_id=1, source_target_pairs={{0,12},{4,0},{8,4},{12,8},{1,13},{5,1},{9,5},{13,9},{2,14},{6,2},{... | collective-permute-start | bytes 294920 | tf_op jit(solution)/shard_map/ppermute | solution.py:63
  45.5 0.0 copy-done
  45.5 2.8 %shard_map.99.refs_3_ = bf16[1,2,8,32,384]{4,3,2,1,0:T(8,128)(2,1)} custom-call(bf16[2,64,384]{2,1,0:T(8,128)(2,1)S(1)} %get-tuple-element.56.refs_0_.refs_2_, bf16[2,64,384]{2,1,0:T(8,128)(2,1)S(1)} %collective-permute-done.9.refs_1_, bf16[2,64,384]{2,1,0:T(8,128)(2,1)S(1)} %collective-permute-done.10.refs_2_, ...), custom_call_target="tpu_custom_call" | custom-call | tf_op jit(solution)/shard_map/pallas_call | solution.py:31
  48.3 0.0 collective-permute-done.14.refs_1_
  48.3 0.0 collective-permute-done.15.refs_2_
  48.3 1.4 %collective-permute-start.16 = (bf16[96,384]{1,0:T(8,128)(2,1)S(1)}, bf16[96,384]{1,0:T(8,128)(2,1)S(1)}, u32[]{:S(2)}, u32[]{:S(2)}) collective-permute-start(bf16[96,384]{1,0:T(8,128)(2,1)S(1)} %get-tuple-element.68), channel_id=1, source_target_pairs={{0,8},{4,12},{8,0},{12,4},{1,9},{5,13},{9,1},{13,5},{2,10},{6,14},... | collective-permute-start | bytes 221192 | tf_op jit(solution)/shard_map/ppermute | solution.py:352
  49.7 0.0 collective-permute-done.3.refs_1_
  49.7 3.3 %collective-permute-done.4.refs_2_ = bf16[2,64,384]{2,1,0:T(8,128)(2,1)S(1)} collective-permute-done((bf16[2,64,384]{2,1,0:T(8,128)(2,1)S(1)}, bf16[2,64,384]{2,1,0:T(8,128)(2,1)S(1)}, u32[]{:S(2)}, u32[]{:S(2)}) %collective-permute-start.4) | collective-permute-done | bytes 98336 | tf_op jit(solution)/shard_map/ppermute | solution.py:63
  53.0 0.0 collective-permute-done.5.refs_3_
  53.0 0.0 copy-done.1
  53.0 0.9 %shard_map.96 = bf16[1,2,8,32,384]{4,3,2,1,0:T(8,128)(2,1)} custom-call(bf16[2,64,384]{2,1,0:T(8,128)(2,1)S(1)} %get-tuple-element.43.refs_0_, bf16[2,64,384]{2,1,0:T(8,128)(2,1)S(1)} %collective-permute-done.3.refs_1_, bf16[2,64,384]{2,1,0:T(8,128)(2,1)S(1)} %collective-permute-done.4.refs_2_, bf16[2,64,384]{2,1,0:T(8,128)(2,1)S(1)} %collective-permute-done.5.refs_3_, ...), custom_call_target="tpu_custom_call" | custom-call | tf_op jit(solution)/shard_map/pallas_call | solution.py:31
  53.8 2.8 %collective-permute-done.16.refs_1_ = bf16[96,384]{1,0:T(8,128)(2,1)S(1)} collective-permute-done((bf16[96,384]{1,0:T(8,128)(2,1)S(1)}, bf16[96,384]{1,0:T(8,128)(2,1)S(1)}, u32[]{:S(2)}, u32[]{:S(2)}) %collective-permute-start.16) | collective-permute-done | bytes 73760 | tf_op jit(solution)/shard_map/ppermute | solution.py:352
  56.6 0.7 %shard_map.103 = f32[96,384]{1,0:T(8,128)} custom-call(f32[96,384]{1,0:T(8,128)S(1)} %get-tuple-element.67.refs_0_, bf16[96,384]{1,0:T(8,128)(2,1)S(1)} %collective-permute-done.16.refs_1_), custom_call_target="tpu_custom_call" | custom-call | tf_op jit(solution)/shard_map/pallas_call | solution.py:31
  (4 shorter events, 0.0 us)
Async XLA Ops:
  0.6 19.0 %copy-start.3 = (f32[384]{0:T(512)S(1)}, f32[384]{0:T(512)}, u32[]{:S(2)}) copy-start(f32[384]{0:T(512)} %refs_4_.6) | copy-start | bytes 4612
  3.8 8.8 %collective-permute-start = (bf16[2,64,384]{2,1,0:T(8,128)(2,1)S(1)}, bf16[2,64,384]{2,1,0:T(8,128)(2,1)S(1)}, u32[]{:S(2)}, u32[]{:S(2)}) collective-permute-start(bf16[2,64,384]{2,1,0:T(8,128)(2,1)S(1)} %get-tuple-element.37), channel_id=1, source_target_pairs={{0,4},{4,8},{8,12},{12,0},{1,5},{5,9},{9,13},{13,1},{2,6},{6,10},{... | collective-permute-start | bytes 294920 | tf_op jit(solution)/shard_map/ppermute | solution.py:63
  6.9 12.7 %collective-permute-start.1 = (bf16[2,64,384]{2,1,0:T(8,128)(2,1)S(1)}, bf16[2,64,384]{2,1,0:T(8,128)(2,1)S(1)}, u32[]{:S(2)}, u32[]{:S(2)}) collective-permute-start(bf16[2,64,384]{2,1,0:T(8,128)(2,1)S(1)} %get-tuple-element.38), channel_id=1, source_target_pairs={{0,8},{4,12},{8,0},{12,4},{1,9},{5,13},{9,1},{13,5},{2,10},{6,14},... | collective-permute-start | bytes 294920 | tf_op jit(solution)/shard_map/ppermute | solution.py:63
  9.5 10.1 %collective-permute-start.2 = (bf16[2,64,384]{2,1,0:T(8,128)(2,1)S(1)}, bf16[2,64,384]{2,1,0:T(8,128)(2,1)S(1)}, u32[]{:S(2)}, u32[]{:S(2)}) collective-permute-start(bf16[2,64,384]{2,1,0:T(8,128)(2,1)S(1)} %get-tuple-element.39), channel_id=1, source_target_pairs={{0,12},{4,0},{8,4},{12,8},{1,13},{5,1},{9,5},{13,9},{2,14},{6,2},{... | collective-permute-start | bytes 294920 | tf_op jit(solution)/shard_map/ppermute | solution.py:63
  10.8 11.7 %collective-permute-start.6 = (bf16[2,2,32,384]{3,2,1,0:T(8,128)(2,1)S(1)}, bf16[2,2,32,384]{3,2,1,0:T(8,128)(2,1)S(1)}, u32[]{:S(2)}, u32[]{:S(2)}) collective-permute-start(bf16[2,2,32,384]{3,2,1,0:T(8,128)(2,1)S(1)} %get-tuple-element.48), channel_id=1, source_target_pairs={{0,4},{4,8},{8,12},{12,0},{1,5},{5,9},{9,13},{13,1},{2,6},{6,10},{... | collective-permute-start | bytes 294920 | tf_op jit(solution)/shard_map/ppermute | solution.py:63
  11.5 13.0 %collective-permute-start.7 = (bf16[2,2,32,384]{3,2,1,0:T(8,128)(2,1)S(1)}, bf16[2,2,32,384]{3,2,1,0:T(8,128)(2,1)S(1)}, u32[]{:S(2)}, u32[]{:S(2)}) collective-permute-start(bf16[2,2,32,384]{3,2,1,0:T(8,128)(2,1)S(1)} %get-tuple-element.49), channel_id=1, source_target_pairs={{0,8},{4,12},{8,0},{12,4},{1,9},{5,13},{9,1},{13,5},{2,10},{6,14},... | collective-permute-start | bytes 294920 | tf_op jit(solution)/shard_map/ppermute | solution.py:63
  12.5 11.9 %collective-permute-start.8 = (bf16[2,2,32,384]{3,2,1,0:T(8,128)(2,1)S(1)}, bf16[2,2,32,384]{3,2,1,0:T(8,128)(2,1)S(1)}, u32[]{:S(2)}, u32[]{:S(2)}) collective-permute-start(bf16[2,2,32,384]{3,2,1,0:T(8,128)(2,1)S(1)} %get-tuple-element.50), channel_id=1, source_target_pairs={{0,12},{4,0},{8,4},{12,8},{1,13},{5,1},{9,5},{13,9},{2,14},{6,2},{... | collective-permute-start | bytes 294920 | tf_op jit(solution)/shard_map/ppermute | solution.py:63
  26.6 2.1 %collective-permute-start.12 = (bf16[8,96,384]{2,1,0:T(8,128)(2,1)S(1)}, bf16[8,96,384]{2,1,0:T(8,128)(2,1)S(1)}, u32[]{:S(2)}, u32[]{:S(2)}) collective-permute-start(bf16[8,96,384]{2,1,0:T(8,128)(2,1)S(1)} %get-tuple-element.61), channel_id=1, source_target_pairs={{0,1},{1,0},{2,3},{3,2},{4,5},{5,4},{6,7},{7,6},{8,9},{9,8},{10,11... | collective-permute-start | bytes 1769480 | tf_op jit(solution)/shard_map/ppermute | solution.py:339
  28.7 16.8 %copy-start = (bf16[1,2,8,32,384]{4,3,2,1,0:T(8,128)(2,1)S(1)}, bf16[1,2,8,32,384]{4,3,2,1,0:T(8,128)(2,1)}, u32[]{:S(2)}) copy-start(bf16[1,2,8,32,384]{4,3,2,1,0:T(8,128)(2,1)} %refs_4_.7) | copy-start | bytes 1179652
  28.7 16.8 %copy-start.2 = (f32[7,7,384]{2,1,0:T(8,128)S(1)}, f32[7,7,384]{2,1,0:T(8,128)}, u32[]{:S(2)}) copy-start(f32[7,7,384]{2,1,0:T(8,128)} %refs_5_.5) | copy-start | bytes 225796
  28.8 9.3 %collective-permute-start.13 = (bf16[4,96,384]{2,1,0:T(8,128)(2,1)S(1)}, bf16[4,96,384]{2,1,0:T(8,128)(2,1)S(1)}, u32[]{:S(2)}, u32[]{:S(2)}) collective-permute-start(bf16[4,96,384]{2,1,0:T(8,128)(2,1)S(1)} %get-tuple-element.63), channel_id=1, source_target_pairs={{0,2},{1,3},{2,0},{3,1},{4,6},{5,7},{6,4},{7,5},{8,10},{9,11},{10,... | collective-permute-start | bytes 884744 | tf_op jit(solution)/shard_map/ppermute | solution.py:343
  30.4 10.5 %collective-permute-start.9 = (bf16[2,64,384]{2,1,0:T(8,128)(2,1)S(1)}, bf16[2,64,384]{2,1,0:T(8,128)(2,1)S(1)}, u32[]{:S(2)}, u32[]{:S(2)}) collective-permute-start(bf16[2,64,384]{2,1,0:T(8,128)(2,1)S(1)} %get-tuple-element.57), channel_id=1, source_target_pairs={{0,4},{4,8},{8,12},{12,0},{1,5},{5,9},{9,13},{13,1},{2,6},{6,10},{... | collective-permute-start | bytes 294920 | tf_op jit(solution)/shard_map/ppermute | solution.py:63
  33.0 9.9 %collective-permute-start.10 = (bf16[2,64,384]{2,1,0:T(8,128)(2,1)S(1)}, bf16[2,64,384]{2,1,0:T(8,128)(2,1)S(1)}, u32[]{:S(2)}, u32[]{:S(2)}) collective-permute-start(bf16[2,64,384]{2,1,0:T(8,128)(2,1)S(1)} %get-tuple-element.58), channel_id=1, source_target_pairs={{0,8},{4,12},{8,0},{12,4},{1,9},{5,13},{9,1},{13,5},{2,10},{6,14},... | collective-permute-start | bytes 294920 | tf_op jit(solution)/shard_map/ppermute | solution.py:63
  34.6 9.9 %collective-permute-start.11 = (bf16[2,64,384]{2,1,0:T(8,128)(2,1)S(1)}, bf16[2,64,384]{2,1,0:T(8,128)(2,1)S(1)}, u32[]{:S(2)}, u32[]{:S(2)}) collective-permute-start(bf16[2,64,384]{2,1,0:T(8,128)(2,1)S(1)} %get-tuple-element.59), channel_id=1, source_target_pairs={{0,12},{4,0},{8,4},{12,8},{1,13},{5,1},{9,5},{13,9},{2,14},{6,2},{... | collective-permute-start | bytes 294920 | tf_op jit(solution)/shard_map/ppermute | solution.py:63
  38.2 14.8 %copy-start.1 = (bf16[1,2,8,32,384]{4,3,2,1,0:T(8,128)(2,1)S(1)}, bf16[1,2,8,32,384]{4,3,2,1,0:T(8,128)(2,1)}, u32[]{:S(2)}) copy-start(bf16[1,2,8,32,384]{4,3,2,1,0:T(8,128)(2,1)} %refs_4_.5) | copy-start | bytes 1179652
  38.2 10.1 %collective-permute-start.14 = (bf16[96,384]{1,0:T(8,128)(2,1)S(1)}, bf16[96,384]{1,0:T(8,128)(2,1)S(1)}, u32[]{:S(2)}, u32[]{:S(2)}) collective-permute-start(bf16[96,384]{1,0:T(8,128)(2,1)S(1)} %get-tuple-element.65), channel_id=1, source_target_pairs={{0,4},{4,0},{8,12},{12,8},{1,5},{5,1},{9,13},{13,9},{2,6},{6,2},{1... | collective-permute-start | bytes 221192 | tf_op jit(solution)/shard_map/ppermute | solution.py:348
  40.8 7.5 %collective-permute-start.15 = (bf16[96,384]{1,0:T(8,128)(2,1)S(1)}, bf16[96,384]{1,0:T(8,128)(2,1)S(1)}, u32[]{:S(2)}, u32[]{:S(2)}) collective-permute-start(bf16[96,384]{1,0:T(8,128)(2,1)S(1)} %get-tuple-element.66), channel_id=1, source_target_pairs={{0,4},{4,0},{8,12},{12,8},{1,5},{5,1},{9,13},{13,9},{2,6},{6,2},{1... | collective-permute-start | bytes 221192 | tf_op jit(solution)/shard_map/ppermute | solution.py:348
  40.9 8.8 %collective-permute-start.3 = (bf16[2,64,384]{2,1,0:T(8,128)(2,1)S(1)}, bf16[2,64,384]{2,1,0:T(8,128)(2,1)S(1)}, u32[]{:S(2)}, u32[]{:S(2)}) collective-permute-start(bf16[2,64,384]{2,1,0:T(8,128)(2,1)S(1)} %get-tuple-element.44), channel_id=1, source_target_pairs={{0,4},{4,8},{8,12},{12,0},{1,5},{5,9},{9,13},{13,1},{2,6},{6,10},{... | collective-permute-start | bytes 294920 | tf_op jit(solution)/shard_map/ppermute | solution.py:63
  42.8 10.1 %collective-permute-start.4 = (bf16[2,64,384]{2,1,0:T(8,128)(2,1)S(1)}, bf16[2,64,384]{2,1,0:T(8,128)(2,1)S(1)}, u32[]{:S(2)}, u32[]{:S(2)}) collective-permute-start(bf16[2,64,384]{2,1,0:T(8,128)(2,1)S(1)} %get-tuple-element.45), channel_id=1, source_target_pairs={{0,8},{4,12},{8,0},{12,4},{1,9},{5,13},{9,1},{13,5},{2,10},{6,14},... | collective-permute-start | bytes 294920 | tf_op jit(solution)/shard_map/ppermute | solution.py:63
  44.5 8.5 %collective-permute-start.5 = (bf16[2,64,384]{2,1,0:T(8,128)(2,1)S(1)}, bf16[2,64,384]{2,1,0:T(8,128)(2,1)S(1)}, u32[]{:S(2)}, u32[]{:S(2)}) collective-permute-start(bf16[2,64,384]{2,1,0:T(8,128)(2,1)S(1)} %get-tuple-element.46), channel_id=1, source_target_pairs={{0,12},{4,0},{8,4},{12,8},{1,13},{5,1},{9,5},{13,9},{2,14},{6,2},{... | collective-permute-start | bytes 294920 | tf_op jit(solution)/shard_map/ppermute | solution.py:63
  48.3 8.3 %collective-permute-start.16 = (bf16[96,384]{1,0:T(8,128)(2,1)S(1)}, bf16[96,384]{1,0:T(8,128)(2,1)S(1)}, u32[]{:S(2)}, u32[]{:S(2)}) collective-permute-start(bf16[96,384]{1,0:T(8,128)(2,1)S(1)} %get-tuple-element.68), channel_id=1, source_target_pairs={{0,8},{4,12},{8,0},{12,4},{1,9},{5,13},{9,1},{13,5},{2,10},{6,14},... | collective-permute-start | bytes 221192 | tf_op jit(solution)/shard_map/ppermute | solution.py:352

commit v3 on v2

--- a/solution.py
+++ b/solution.py
@@ -53,6 +53,20 @@
     if count == 1:
         return 0
     return lax.rem(lax.axis_index("tm") + count - step, count)
+
+
+def partner(step, count):
+    if count == 1:
+        return 0
+    return lax.bitwise_xor(lax.axis_index("tm"), step)
+
+
+def swap(pieces):
+    got = [pieces[0]]
+    for step in range(1, len(pieces)):
+        pairs = [(i, i ^ step) for i in range(len(pieces))]
+        got.append(lax.ppermute(pieces[step], "tm", pairs))
+    return got
 
 
 def exchange(pieces):
@@ -147,17 +161,20 @@
 
 def spatial_bwd(count, *refs):
     pieces = refs[:count]
-    cot, kernel, out_ref, pad_ref = refs[count:]
+    clips, cot, kernel, block_out, out_ref, pad_ref = refs[count:]
     _, frames, height, width, channels = cot.shape
     blocks = channels // LANES
     rows = height // count
     clear_pads(pad_ref, width)
     for step in range(count):
-        base = slot_from(step, count) * rows
+        base = partner(step, count) * rows
         for block in range(blocks):
             lanes = slice(block * LANES, (block + 1) * LANES)
-            piece = pieces[step][:, :, lanes].astype(F32).reshape(frames, rows, width, LANES)
+            piece = pieces[step][1, :, :, lanes].astype(F32).reshape(frames, rows, width, LANES)
             pad_ref[block, :, pl.ds(base, rows), PAD : PAD + width, :] = piece
+        here = (0, slice(None), pl.ds(base, rows))
+        branch = pieces[step][0].reshape(frames, rows, width, channels).astype(F32)
+        block_out[here] = (clips[here].astype(F32) + branch).astype(BF16)
     for block in range(blocks):
         lanes = slice(block * LANES, (block + 1) * LANES)
         for col in range(0, width, 16):
@@ -215,8 +232,7 @@
 def mlp_fwd(count, chunk, *refs):
     pieces = refs[:count]
     taps, gain, w_expand, w_project = refs[count : count + 4]
-    branches = refs[count + 4 : 2 * count + 4]
-    scaled, slope, normed, inv_std, mixed_in, mixed, hidden, branch = refs[2 * count + 4 :]
+    branch, scaled, slope, normed, inv_std, mixed_in, mixed, hidden = refs[count + 4 :]
     frames, pixels, channels = mixed_in.shape
     tokens = frames * pixels
     place_frames(count, pieces, mixed_in)
@@ -235,13 +251,8 @@
         cdf = 0.5 + 0.5 * lax.erf(pre * 0.7071067811865476)
         hidden[:, part] = (pre * cdf).astype(BF16)
         slope[:, part] = (cdf + pre * jnp.exp(-0.5 * pre * pre) * 0.3989422804014327).astype(BF16)
-    branch[...] = jnp.dot(hidden[...], w_project[...], preferred_element_type=F32).reshape(
-        frames, pixels, channels
-    )
-    own = frames // count
-    for step in range(count):
-        base = slot_to(step, count) * own
-        branches[step][...] = branch[pl.ds(base, own)].astype(BF16)
+    out = jnp.dot(hidden[...], w_project[...], preferred_element_type=F32).astype(BF16)
+    branch[...] = out.reshape(branch.shape)
 
 
 def hidden_bwd(count, chunk, with_grad, *refs):
@@ -269,9 +280,9 @@
 
 
 def token_bwd(count, *refs):
-    d_pre, normed, inv_std, taps, gain, w_expand = refs[:6]
-    outs = refs[6 : count + 6]
-    d_second, d_first = refs[count + 6 :]
+    d_pre, normed, inv_std, taps, gain, w_expand, branch = refs[:7]
+    outs = refs[7 : count + 7]
+    d_second, d_first = refs[count + 7 :]
     frames, pixels, channels = d_second.shape
     last = (((1,), (1,)), ((), ()))
     d_scaled = lax.dot_general(d_pre[...], w_expand[...], last, preferred_element_type=F32)
@@ -286,20 +297,9 @@
     mix_frames(d_second, d_first, taps, True)
     own = frames // count
     for step in range(count):
-        base = slot_to(step, count) * own
-        outs[step][...] = d_first[pl.ds(base, own)].astype(BF16)
-
-
-def add_residual(count, *refs):
-    pieces = refs[:count]
-    clips, out_ref = refs[count:]
-    _, frames, height, width, channels = clips.shape
-    rows = height // count
-    for step in range(count):
-        base = slot_from(step, count) * rows
-        piece = pieces[step][...].reshape(frames, rows, width, channels).astype(F32)
-        here = (0, slice(None), pl.ds(base, rows))
-        out_ref[here] = (clips[here].astype(F32) + piece).astype(BF16)
+        base = partner(step, count) * own
+        outs[step][0] = branch[pl.ds(base, own)]
+        outs[step][1] = d_first[pl.ds(base, own)].astype(BF16)
 
 
 def fold_pair(keep_in, got, keep, send):
@@ -331,7 +331,7 @@
     refs[-1][...] = total * scale_factor
 
 
-def scatter_grad(keep, send, count, scale_factor, d_first, grad_clips):
+def scatter_grad(keep, send, count, scale_factor, d_first):
     channels = keep.shape[-1]
     block = keep.shape[1]
     quarter = (count, block, channels)
@@ -347,7 +347,7 @@
     )
     near = [lax.ppermute(send, "tm", [(i, i ^ 1) for i in range(4)]) for send in sends]
     keep, send = call(
-        fold_far, [struct(piece, F32), struct(piece, BF16)], [], keep, *near, wait=[grad_clips]
+        fold_far, [struct(piece, F32), struct(piece, BF16)], [], keep, *near
     )
     got = lax.ppermute(send, "tm", [(i, i ^ 2) for i in range(4)])
     return call(functools.partial(fold_last, scale_factor), [struct(piece, F32)], [], keep, got)[0]
@@ -362,7 +362,7 @@
     hid = w_expand.shape[1]
     chunk = 256
     blocks = channels // LANES
-    count = members if members <= 8 and height % members == 0 else 1
+    count = members if members in (2, 4, 8) and height % members == 0 else 1
     all_frames = frames * members
     columns = pixels // members
     tokens = all_frames * columns
@@ -375,9 +375,8 @@
 
     def to_frames(pieces):
         if count > 1:
-            return exchange(pieces)
-        whole = pieces[0][None]
-        return [lax.all_to_all(whole, "tm", split_axis=1, concat_axis=2, tiled=True)[0]]
+            return swap(pieces)
+        return [lax.all_to_all(pieces[0], "tm", split_axis=1, concat_axis=2, tiled=True)]
 
     pad = pltpu.VMEM((blocks, frames, height, width + 2 * PAD, LANES), F32)
     piece = struct((frames, pixels // count, channels), BF16)
@@ -407,8 +406,8 @@
     back = struct((all_frames // count, columns, channels), BF16)
     outs = call(
         functools.partial(mlp_fwd, count, chunk),
-        [back] * count
-        + [
+        [
+            struct(column, BF16),
             struct((tokens, channels), BF16),
             struct((tokens, hid), BF16),
             struct((tokens, channels), F32),
@@ -418,7 +417,6 @@
             pltpu.VMEM(column, F32),
             pltpu.VMEM(column, F32),
             pltpu.VMEM((tokens, hid), BF16),
-            pltpu.VMEM(column, F32),
         ],
         *firsts,
         temporal_kernel,
@@ -426,8 +424,7 @@
         w_expand,
         w_project,
     )
-    scaled, slope, normed, inv_std = outs[count:]
-    branches = to_frames(list(outs[:count]))
+    branch, scaled, slope, normed, inv_std = outs
 
     sides = lax.axis_size("dp")
     staged = count == 4 and sides == 4
@@ -445,7 +442,7 @@
     shares = outs[1:]
     outs = call(
         functools.partial(token_bwd, count),
-        [back] * count,
+        [struct((2,) + back.shape, BF16)] * count,
         [pltpu.VMEM(column, F32), pltpu.VMEM(column, F32)],
         d_pre,
         normed,
@@ -453,22 +450,21 @@
         temporal_kernel,
         norm_gain,
         w_expand,
-    )
-    d_firsts = to_frames(list(outs))
-
-    block_out = call(
-        functools.partial(add_residual, count), [struct(clips.shape, BF16)], [], *branches, clips
-    )[0]
-    grad_clips = call(
+        branch,
+    )
+    arrived = to_frames(list(outs))
+
+    block_out, grad_clips = call(
         functools.partial(spatial_bwd, count),
-        [struct(clips.shape, BF16)],
+        [struct(clips.shape, BF16)] * 2,
         [pad],
-        *d_firsts,
+        *arrived,
+        clips,
         cotangent,
         spatial_kernel,
-    )[0]
+    )
     if staged:
-        grad_expand = scatter_grad(*shares, count, scale_factor, outs[0], grad_clips)
+        grad_expand = scatter_grad(*shares, count, scale_factor, outs[0])
     else:
         whole = lax.dot_general(
             d_pre, scaled, (((0,), (0,)), ((), ())), preferred_element_type=F32

time: 57.4 us -> 56.4 us (0.983)
  starting transfers between devices: 26.3 us -> 21.7 us
  waiting for transfers between devices: 15.7 us -> 20.1 us
  Pallas kernels: 14.5 us -> 13.7 us
    ppermute x12 -> x6, starting transfers between devices: 20.6 us -> 11.1 us  [exchange(): got.append(lax.ppermute(pieces[step], 'tm', pairs))]
    ppermute x2, waiting for transfers between devices: 0.01 us -> 9.29 us  [scatter_grad(): lax.ppermute(send, 'tm', [(i, i ^ 1) for i in range(4)])]
    ppermute x0 -> x3, starting transfers between devices: none -> 4.93 us  [swap(): got.append(lax.ppermute(pieces[step], 'tm', pairs))]
    ppermute x12 -> x6, waiting for transfers between devices: 9.86 us -> 6.69 us  [exchange(): got.append(lax.ppermute(pieces[step], 'tm', pairs))]
    ppermute x1, waiting for transfers between devices: 2.78 us -> 1.13 us  [scatter_grad(): got = lax.ppermute(send, 'tm', [(i, i ^ 2) for i in range(4)])]
    pallas_call x10 -> x9, Pallas kernels: 14.5 us -> 13.7 us  [call(): pl.pallas_call(kernel, out_shape=tuple(outs), in_specs=specs, out_specs=t...]
  transfers between devices with their start and end apart: 17 -> 14, of which waited for: 7 -> 8; matrix products, arithmetic and copies ran while one was open for 0% -> 0% of each run, Pallas kernels for 15% -> 14%
where the time goes in v3:
time: 56.4 us; the launch traced here: 56.3 us
  starting transfers between devices  21.7 us (38%)
  waiting for transfers between devices  20.1 us (36%)
  Pallas kernels  13.7 us (24%)
  between operations  0.72 us (1%)
    pallas_call x9, Pallas kernels, call(): pl.pallas_call(kernel, out_shape=tuple(outs), in_specs=specs, out_specs=t...  13.7 us
    ppermute x6, starting transfers between devices, exchange(): got.append(lax.ppermute(pieces[step], 'tm', pairs))  11.1 us
    ppermute x2, waiting for transfers between devices, scatter_grad(): lax.ppermute(send, 'tm', [(i, i ^ 1) for i in range(4)])  9.29 us
    ppermute x6, waiting for transfers between devices, exchange(): got.append(lax.ppermute(pieces[step], 'tm', pairs))  6.69 us
    ppermute x3, starting transfers between devices, swap(): got.append(lax.ppermute(pieces[step], 'tm', pairs))  4.93 us
    ppermute x1, waiting for transfers between devices, scatter_grad(): got = lax.ppermute(send, 'dp', [(i, i ^ 2) for i in range(4)])  2.82 us
    ppermute x2, starting transfers between devices, scatter_grad(): lax.ppermute(send, 'tm', [(i, i ^ 1) for i in range(4)])  2.73 us
    ppermute x1, starting transfers between devices, scatter_grad(): got = lax.ppermute(send, 'dp', [(i, i ^ 2) for i in range(4)])  1.56 us
  transfers between devices with their start and end apart: 14, of which 8 were waited for; matrix products, arithmetic and copies ran while one was open for 0% of the time, Pallas kernels for 14%

profile of v3, /device:TPU:0, one launch (start us, length us, event | category | flops | bytes accessed | tf_op | source)
XLA Modules:
  0.0 56.3 jit_solution(13322689184949420309)
XLA Ops:
  0.6 0.0 copy-start.3
  0.6 3.1 %shard_map.94 = (bf16[2,64,384]{2,1,0:T(8,128)(2,1)S(1)}, bf16[2,64,384]{2,1,0:T(8,128)(2,1)S(1)}, bf16[2,64,384]{2,1,0:T(8,128)(2,1)S(1)}, bf16[2,64,384]{2,1,0...) custom-call(bf16[1,2,8,32,384]{4,3,2,1,0:T(8,128)(2,1)} %refs_4_.5, ...), custom_call_target="tpu_custom_call" | custom-call | tf_op jit(solution)/shard_map/pallas_call | solution.py:31
  3.8 3.1 %collective-permute-start.3 = (bf16[2,64,384]{2,1,0:T(8,128)(2,1)S(1)}, bf16[2,64,384]{2,1,0:T(8,128)(2,1)S(1)}, u32[]{:S(2)}, u32[]{:S(2)}) collective-permute-start(bf16[2,64,384]{2,1,0:T(8,128)(2,1)S(1)} %get-tuple-element.40), channel_id=1, source_target_pairs={{0,4},{4,8},{8,12},{12,0},{1,5},{5,9},{9,13},{13,1},{2,6},{6,10},{... | collective-permute-start | bytes 294920 | tf_op jit(solution)/shard_map/ppermute | solution.py:77
  6.9 2.6 %collective-permute-start.4 = (bf16[2,64,384]{2,1,0:T(8,128)(2,1)S(1)}, bf16[2,64,384]{2,1,0:T(8,128)(2,1)S(1)}, u32[]{:S(2)}, u32[]{:S(2)}) collective-permute-start(bf16[2,64,384]{2,1,0:T(8,128)(2,1)S(1)} %get-tuple-element.41), channel_id=1, source_target_pairs={{0,8},{4,12},{8,0},{12,4},{1,9},{5,13},{9,1},{13,5},{2,10},{6,14},... | collective-permute-start | bytes 294920 | tf_op jit(solution)/shard_map/ppermute | solution.py:77
  9.5 1.3 %collective-permute-start.5 = (bf16[2,64,384]{2,1,0:T(8,128)(2,1)S(1)}, bf16[2,64,384]{2,1,0:T(8,128)(2,1)S(1)}, u32[]{:S(2)}, u32[]{:S(2)}) collective-permute-start(bf16[2,64,384]{2,1,0:T(8,128)(2,1)S(1)} %get-tuple-element.42), channel_id=1, source_target_pairs={{0,12},{4,0},{8,4},{12,8},{1,13},{5,1},{9,5},{13,9},{2,14},{6,2},{... | collective-permute-start | bytes 294920 | tf_op jit(solution)/shard_map/ppermute | solution.py:77
  10.8 0.7 %collective-permute-start = (bf16[2,2,32,384]{3,2,1,0:T(8,128)(2,1)S(1)}, bf16[2,2,32,384]{3,2,1,0:T(8,128)(2,1)S(1)}, u32[]{:S(2)}, u32[]{:S(2)}) collective-permute-start(bf16[2,2,32,384]{3,2,1,0:T(8,128)(2,1)S(1)} %get-tuple-element.36), channel_id=1, source_target_pairs={{0,4},{4,8},{8,12},{12,0},{1,5},{5,9},{9,13},{13,1},{2,6},{6,10},{... | collective-permute-start | bytes 294920 | tf_op jit(solution)/shard_map/ppermute | solution.py:77
  11.5 0.3 collective-permute-start.1
  11.8 0.7 %collective-permute-done.3.refs_1_ = bf16[2,64,384]{2,1,0:T(8,128)(2,1)S(1)} collective-permute-done((bf16[2,64,384]{2,1,0:T(8,128)(2,1)S(1)}, bf16[2,64,384]{2,1,0:T(8,128)(2,1)S(1)}, u32[]{:S(2)}, u32[]{:S(2)}) %collective-permute-start.3) | collective-permute-done | bytes 98336 | tf_op jit(solution)/shard_map/ppermute | solution.py:77
  12.5 3.1 %collective-permute-start.2 = (bf16[2,2,32,384]{3,2,1,0:T(8,128)(2,1)S(1)}, bf16[2,2,32,384]{3,2,1,0:T(8,128)(2,1)S(1)}, u32[]{:S(2)}, u32[]{:S(2)}) collective-permute-start(bf16[2,2,32,384]{3,2,1,0:T(8,128)(2,1)S(1)} %get-tuple-element.38), channel_id=1, source_target_pairs={{0,12},{4,0},{8,4},{12,8},{1,13},{5,1},{9,5},{13,9},{2,14},{6,2},{... | collective-permute-start | bytes 294920 | tf_op jit(solution)/shard_map/ppermute | solution.py:77
  15.7 3.9 %collective-permute-done.4.refs_2_ = bf16[2,64,384]{2,1,0:T(8,128)(2,1)S(1)} collective-permute-done((bf16[2,64,384]{2,1,0:T(8,128)(2,1)S(1)}, bf16[2,64,384]{2,1,0:T(8,128)(2,1)S(1)}, u32[]{:S(2)}, u32[]{:S(2)}) %collective-permute-start.4) | collective-permute-done | bytes 98336 | tf_op jit(solution)/shard_map/ppermute | solution.py:77
  19.6 0.0 collective-permute-done.5.refs_3_
  19.6 0.0 copy-done.3
  19.6 2.8 %shard_map.95 = (bf16[8,64,384]{2,1,0:T(8,128)(2,1)S(1)}, bf16[512,384]{1,0:T(8,128)(2,1)S(1)}, bf16[512,1536]{1,0:T(8,128)(2,1)S(1)}, f32[512,384]{1,0:T(8,128)S(1)}, f32[512,1]{1,0:T(8,128)S(1)}) custom-call(bf16[2,64,384]{2,1,0:T(8,128)(2,1)S(1)} %get-tuple-element.39.refs_0_, bf16[2,64,384]{2,1,0:T(8,128)(2,1)S(1)} %collective-permute-done.3.refs_1_, ...), custom_call_target="tpu_custom_call" | custom-call | tf_op jit(solution)/shard_map/pallas_call | solution.py:31
  22.4 0.0 collective-permute-done.refs_1_
  22.4 2.0 %collective-permute-done.1.refs_2_ = bf16[2,2,32,384]{3,2,1,0:T(8,128)(2,1)S(1)} collective-permute-done((bf16[2,2,32,384]{3,2,1,0:T(8,128)(2,1)S(1)}, bf16[2,2,32,384]{3,2,1,0:T(8,128)(2,1)S(1)}, u32[]{:S(2)}, u32[]{:S(2)}) %collective-permute-start.1) | collective-permute-done | bytes 98336 | tf_op jit(solution)/shard_map/ppermute | solution.py:77
  24.5 0.0 collective-permute-done.2.refs_3_
  24.5 2.2 %shard_map.96 = (bf16[512,1536]{1,0:T(8,128)(2,1)S(1)}, f32[8,96,384]{2,1,0:T(8,128)S(1)}, bf16[8,96,384]{2,1,0:T(8,128)(2,1)S(1)}) custom-call(bf16[2,2,32,384]{3,2,1,0:T(8,128)(2,1)S(1)} %get-tuple-element.35.refs_0_, bf16[2,2,32,384]{3,2,1,0:T(8,128)(2,1)S(1)} %collective-permute-done.refs_1_, bf16[2,2,32,384]{3,2,1,0:T(8,128)(2,1)S(1)} %collective-permute-done.1.refs_2_, ...), custom_call_target="tpu_custom_call" | custom-call | tf_op jit(solution)/shard_map/pallas_call | solution.py:31
  26.6 0.1 collective-permute-start.9
  26.7 1.8 %shard_map.97 = (bf16[2,2,64,384]{3,2,1,0:T(8,128)(2,1)S(1)}, bf16[2,2,64,384]{3,2,1,0:T(8,128)(2,1)S(1)}, bf16[2,2,64,384]{3,2,1,0:T(8,128)(2,1)S(1)}, bf16[2,2,64,384]{3,2,1,0:T(8,128)(2,1)S(1)}) custom-call(bf16[512,1536]{1,0:T(8,128)(2,1)S(1)} %get-tuple-element.48.refs_0_, f32[512,384]{1,0:T(8,128)S(1)} %get-tuple-element.49.refs_1_, ...), custom_call_target="tpu_custom_call" | custom-call | tf_op jit(solution)/shard_map/pallas_call | solution.py:31
  28.5 0.2 collective-permute-done.9.refs_1_
  28.7 0.0 copy-start
  28.7 0.0 copy-start.1
  28.7 0.0 copy-start.2
  28.7 0.1 shard_map.99
  28.8 1.6 %collective-permute-start.10 = (bf16[4,96,384]{2,1,0:T(8,128)(2,1)S(1)}, bf16[4,96,384]{2,1,0:T(8,128)(2,1)S(1)}, u32[]{:S(2)}, u32[]{:S(2)}) collective-permute-start(bf16[4,96,384]{2,1,0:T(8,128)(2,1)S(1)} %get-tuple-element.61), channel_id=1, source_target_pairs={{0,2},{1,3},{2,0},{3,1},{4,6},{5,7},{6,4},{7,5},{8,10},{9,11},{10,... | collective-permute-start | bytes 884744 | tf_op jit(solution)/shard_map/ppermute | solution.py:343
  30.4 2.6 %collective-permute-start.6 = (bf16[2,2,64,384]{3,2,1,0:T(8,128)(2,1)S(1)}, bf16[2,2,64,384]{3,2,1,0:T(8,128)(2,1)S(1)}, u32[]{:S(2)}, u32[]{:S(2)}) collective-permute-start(bf16[2,2,64,384]{3,2,1,0:T(8,128)(2,1)S(1)} %get-tuple-element.53), channel_id=1, source_target_pairs={{0,4},{4,0},{8,12},{12,8},{1,5},{5,1},{9,13},{13,9},{2,6},{6,2},{1... | collective-permute-start | bytes 589832 | tf_op jit(solution)/shard_map/ppermute | solution.py:68
  33.0 1.6 %collective-permute-start.7 = (bf16[2,2,64,384]{3,2,1,0:T(8,128)(2,1)S(1)}, bf16[2,2,64,384]{3,2,1,0:T(8,128)(2,1)S(1)}, u32[]{:S(2)}, u32[]{:S(2)}) collective-permute-start(bf16[2,2,64,384]{3,2,1,0:T(8,128)(2,1)S(1)} %get-tuple-element.54), channel_id=1, source_target_pairs={{0,8},{4,12},{8,0},{12,4},{1,9},{5,13},{9,1},{13,5},{2,10},{6,14},... | collective-permute-start | bytes 589832 | tf_op jit(solution)/shard_map/ppermute | solution.py:68
  34.6 0.7 %collective-permute-start.8 = (bf16[2,2,64,384]{3,2,1,0:T(8,128)(2,1)S(1)}, bf16[2,2,64,384]{3,2,1,0:T(8,128)(2,1)S(1)}, u32[]{:S(2)}, u32[]{:S(2)}) collective-permute-start(bf16[2,2,64,384]{3,2,1,0:T(8,128)(2,1)S(1)} %get-tuple-element.55), channel_id=1, source_target_pairs={{0,12},{4,8},{8,4},{12,0},{1,13},{5,9},{9,5},{13,1},{2,14},{6,10},... | collective-permute-start | bytes 589832 | tf_op jit(solution)/shard_map/ppermute | solution.py:68
  35.3 2.8 %collective-permute-done.10.refs_1_ = bf16[4,96,384]{2,1,0:T(8,128)(2,1)S(1)} collective-permute-done((bf16[4,96,384]{2,1,0:T(8,128)(2,1)S(1)}, bf16[4,96,384]{2,1,0:T(8,128)(2,1)S(1)}, u32[]{:S(2)}, u32[]{:S(2)}) %collective-permute-start.10) | collective-permute-done | bytes 294944 | tf_op jit(solution)/shard_map/ppermute | solution.py:343
  38.1 0.1 shard_map.100
  38.2 2.6 %collective-permute-start.11 = (bf16[96,384]{1,0:T(8,128)(2,1)S(1)}, bf16[96,384]{1,0:T(8,128)(2,1)S(1)}, u32[]{:S(2)}, u32[]{:S(2)}) collective-permute-start(bf16[96,384]{1,0:T(8,128)(2,1)S(1)} %get-tuple-element.63), channel_id=1, source_target_pairs={{0,4},{4,0},{8,12},{12,8},{1,5},{5,1},{9,13},{13,9},{2,6},{6,2},{1... | collective-permute-start | bytes 221192 | tf_op jit(solution)/shard_map/ppermute | solution.py:348
  40.8 0.1 collective-permute-start.12
  40.9 7.3 %collective-permute-done.11.refs_1_ = bf16[96,384]{1,0:T(8,128)(2,1)S(1)} collective-permute-done((bf16[96,384]{1,0:T(8,128)(2,1)S(1)}, bf16[96,384]{1,0:T(8,128)(2,1)S(1)}, u32[]{:S(2)}, u32[]{:S(2)}) %collective-permute-start.11) | collective-permute-done | bytes 73760 | tf_op jit(solution)/shard_map/ppermute | solution.py:348
  48.2 2.0 %collective-permute-done.12.refs_2_ = bf16[96,384]{1,0:T(8,128)(2,1)S(1)} collective-permute-done((bf16[96,384]{1,0:T(8,128)(2,1)S(1)}, bf16[96,384]{1,0:T(8,128)(2,1)S(1)}, u32[]{:S(2)}, u32[]{:S(2)}) %collective-permute-start.12) | collective-permute-done | bytes 73760 | tf_op jit(solution)/shard_map/ppermute | solution.py:348
  50.2 1.2 %collective-permute-start.13 = (bf16[96,384]{1,0:T(8,128)(2,1)S(1)}, bf16[96,384]{1,0:T(8,128)(2,1)S(1)}, u32[]{:S(2)}, u32[]{:S(2)}) collective-permute-start(bf16[96,384]{1,0:T(8,128)(2,1)S(1)} %get-tuple-element.66), channel_id=1, source_target_pairs={{0,8},{4,12},{8,0},{12,4},{1,9},{5,13},{9,1},{13,5},{2,10},{6,14},... | collective-permute-start | bytes 221192 | tf_op jit(solution)/shard_map/ppermute | solution.py:352
  51.5 0.0 collective-permute-done.6.refs_1_
  51.5 0.0 collective-permute-done.7.refs_2_
  51.5 0.0 collective-permute-done.8.refs_3_
  51.5 0.0 copy-done
  51.5 0.0 copy-done.1
  51.5 0.0 copy-done.2
  51.5 2.9 %shard_map.98 = (bf16[1,2,8,32,384]{4,3,2,1,0:T(8,128)(2,1)}, bf16[1,2,8,32,384]{4,3,2,1,0:T(8,128)(2,1)}) custom-call(bf16[2,2,64,384]{3,2,1,0:T(8,128)(2,1)S(1)} %get-tuple-element.52.refs_0_.refs_2_, bf16[2,2,64,384]{3,2,1,0:T(8,128)(2,1)S(1)} %collective-permute-done.6.refs_1_, bf16[2,2,64,384]{3,2,1,0:T(8,128)(2,1)S(1)} %collective-permute-done.7.refs_2_, ...), custom_call_target="tpu_custom_call" | custom-call | tf_op jit(solution)/shard_map/pallas_call | solution.py:31
  54.4 1.1 %collective-permute-done.13.refs_1_ = bf16[96,384]{1,0:T(8,128)(2,1)S(1)} collective-permute-done((bf16[96,384]{1,0:T(8,128)(2,1)S(1)}, bf16[96,384]{1,0:T(8,128)(2,1)S(1)}, u32[]{:S(2)}, u32[]{:S(2)}) %collective-permute-start.13) | collective-permute-done | bytes 73760 | tf_op jit(solution)/shard_map/ppermute | solution.py:352
  55.6 0.7 %shard_map.102 = f32[96,384]{1,0:T(8,128)} custom-call(f32[96,384]{1,0:T(8,128)S(1)} %get-tuple-element.65.refs_0_, bf16[96,384]{1,0:T(8,128)(2,1)S(1)} %collective-permute-done.13.refs_1_), custom_call_target="tpu_custom_call" | custom-call | tf_op jit(solution)/shard_map/pallas_call | solution.py:31
  (1 shorter events, 0.0 us)
Async XLA Ops:
  0.6 19.0 %copy-start.3 = (f32[384]{0:T(512)S(1)}, f32[384]{0:T(512)}, u32[]{:S(2)}) copy-start(f32[384]{0:T(512)} %refs_4_.4) | copy-start | bytes 4612
  3.8 8.8 %collective-permute-start.3 = (bf16[2,64,384]{2,1,0:T(8,128)(2,1)S(1)}, bf16[2,64,384]{2,1,0:T(8,128)(2,1)S(1)}, u32[]{:S(2)}, u32[]{:S(2)}) collective-permute-start(bf16[2,64,384]{2,1,0:T(8,128)(2,1)S(1)} %get-tuple-element.40), channel_id=1, source_target_pairs={{0,4},{4,8},{8,12},{12,0},{1,5},{5,9},{9,13},{13,1},{2,6},{6,10},{... | collective-permute-start | bytes 294920 | tf_op jit(solution)/shard_map/ppermute | solution.py:77
  6.9 12.7 %collective-permute-start.4 = (bf16[2,64,384]{2,1,0:T(8,128)(2,1)S(1)}, bf16[2,64,384]{2,1,0:T(8,128)(2,1)S(1)}, u32[]{:S(2)}, u32[]{:S(2)}) collective-permute-start(bf16[2,64,384]{2,1,0:T(8,128)(2,1)S(1)} %get-tuple-element.41), channel_id=1, source_target_pairs={{0,8},{4,12},{8,0},{12,4},{1,9},{5,13},{9,1},{13,5},{2,10},{6,14},... | collective-permute-start | bytes 294920 | tf_op jit(solution)/shard_map/ppermute | solution.py:77
  9.5 10.1 %collective-permute-start.5 = (bf16[2,64,384]{2,1,0:T(8,128)(2,1)S(1)}, bf16[2,64,384]{2,1,0:T(8,128)(2,1)S(1)}, u32[]{:S(2)}, u32[]{:S(2)}) collective-permute-start(bf16[2,64,384]{2,1,0:T(8,128)(2,1)S(1)} %get-tuple-element.42), channel_id=1, source_target_pairs={{0,12},{4,0},{8,4},{12,8},{1,13},{5,1},{9,5},{13,9},{2,14},{6,2},{... | collective-permute-start | bytes 294920 | tf_op jit(solution)/shard_map/ppermute | solution.py:77
  10.8 11.6 %collective-permute-start = (bf16[2,2,32,384]{3,2,1,0:T(8,128)(2,1)S(1)}, bf16[2,2,32,384]{3,2,1,0:T(8,128)(2,1)S(1)}, u32[]{:S(2)}, u32[]{:S(2)}) collective-permute-start(bf16[2,2,32,384]{3,2,1,0:T(8,128)(2,1)S(1)} %get-tuple-element.36), channel_id=1, source_target_pairs={{0,4},{4,8},{8,12},{12,0},{1,5},{5,9},{9,13},{13,1},{2,6},{6,10},{... | collective-permute-start | bytes 294920 | tf_op jit(solution)/shard_map/ppermute | solution.py:77
  11.5 13.0 %collective-permute-start.1 = (bf16[2,2,32,384]{3,2,1,0:T(8,128)(2,1)S(1)}, bf16[2,2,32,384]{3,2,1,0:T(8,128)(2,1)S(1)}, u32[]{:S(2)}, u32[]{:S(2)}) collective-permute-start(bf16[2,2,32,384]{3,2,1,0:T(8,128)(2,1)S(1)} %get-tuple-element.37), channel_id=1, source_target_pairs={{0,8},{4,12},{8,0},{12,4},{1,9},{5,13},{9,1},{13,5},{2,10},{6,14},... | collective-permute-start | bytes 294920 | tf_op jit(solution)/shard_map/ppermute | solution.py:77
  12.5 11.9 %collective-permute-start.2 = (bf16[2,2,32,384]{3,2,1,0:T(8,128)(2,1)S(1)}, bf16[2,2,32,384]{3,2,1,0:T(8,128)(2,1)S(1)}, u32[]{:S(2)}, u32[]{:S(2)}) collective-permute-start(bf16[2,2,32,384]{3,2,1,0:T(8,128)(2,1)S(1)} %get-tuple-element.38), channel_id=1, source_target_pairs={{0,12},{4,0},{8,4},{12,8},{1,13},{5,1},{9,5},{13,9},{2,14},{6,2},{... | collective-permute-start | bytes 294920 | tf_op jit(solution)/shard_map/ppermute | solution.py:77
  26.6 2.1 %collective-permute-start.9 = (bf16[8,96,384]{2,1,0:T(8,128)(2,1)S(1)}, bf16[8,96,384]{2,1,0:T(8,128)(2,1)S(1)}, u32[]{:S(2)}, u32[]{:S(2)}) collective-permute-start(bf16[8,96,384]{2,1,0:T(8,128)(2,1)S(1)} %get-tuple-element.59), channel_id=1, source_target_pairs={{0,1},{1,0},{2,3},{3,2},{4,5},{5,4},{6,7},{7,6},{8,9},{9,8},{10,11... | collective-permute-start | bytes 1769480 | tf_op jit(solution)/shard_map/ppermute | solution.py:339
  28.7 22.8 %copy-start = (bf16[1,2,8,32,384]{4,3,2,1,0:T(8,128)(2,1)S(1)}, bf16[1,2,8,32,384]{4,3,2,1,0:T(8,128)(2,1)}, u32[]{:S(2)}) copy-start(bf16[1,2,8,32,384]{4,3,2,1,0:T(8,128)(2,1)} %refs_4_.5) | copy-start | bytes 1179652
  28.7 22.8 %copy-start.1 = (bf16[1,2,8,32,384]{4,3,2,1,0:T(8,128)(2,1)S(1)}, bf16[1,2,8,32,384]{4,3,2,1,0:T(8,128)(2,1)}, u32[]{:S(2)}) copy-start(bf16[1,2,8,32,384]{4,3,2,1,0:T(8,128)(2,1)} %refs_5_.5) | copy-start | bytes 1179652
  28.7 22.8 %copy-start.2 = (f32[7,7,384]{2,1,0:T(8,128)S(1)}, f32[7,7,384]{2,1,0:T(8,128)}, u32[]{:S(2)}) copy-start(f32[7,7,384]{2,1,0:T(8,128)} %refs_6_.1) | copy-start | bytes 225796
  28.8 9.3 %collective-permute-start.10 = (bf16[4,96,384]{2,1,0:T(8,128)(2,1)S(1)}, bf16[4,96,384]{2,1,0:T(8,128)(2,1)S(1)}, u32[]{:S(2)}, u32[]{:S(2)}) collective-permute-start(bf16[4,96,384]{2,1,0:T(8,128)(2,1)S(1)} %get-tuple-element.61), channel_id=1, source_target_pairs={{0,2},{1,3},{2,0},{3,1},{4,6},{5,7},{6,4},{7,5},{8,10},{9,11},{10,... | collective-permute-start | bytes 884744 | tf_op jit(solution)/shard_map/ppermute | solution.py:343
  30.4 21.1 %collective-permute-start.6 = (bf16[2,2,64,384]{3,2,1,0:T(8,128)(2,1)S(1)}, bf16[2,2,64,384]{3,2,1,0:T(8,128)(2,1)S(1)}, u32[]{:S(2)}, u32[]{:S(2)}) collective-permute-start(bf16[2,2,64,384]{3,2,1,0:T(8,128)(2,1)S(1)} %get-tuple-element.53), channel_id=1, source_target_pairs={{0,4},{4,0},{8,12},{12,8},{1,5},{5,1},{9,13},{13,9},{2,6},{6,2},{1... | collective-permute-start | bytes 589832 | tf_op jit(solution)/shard_map/ppermute | solution.py:68
  33.0 18.5 %collective-permute-start.7 = (bf16[2,2,64,384]{3,2,1,0:T(8,128)(2,1)S(1)}, bf16[2,2,64,384]{3,2,1,0:T(8,128)(2,1)S(1)}, u32[]{:S(2)}, u32[]{:S(2)}) collective-permute-start(bf16[2,2,64,384]{3,2,1,0:T(8,128)(2,1)S(1)} %get-tuple-element.54), channel_id=1, source_target_pairs={{0,8},{4,12},{8,0},{12,4},{1,9},{5,13},{9,1},{13,5},{2,10},{6,14},... | collective-permute-start | bytes 589832 | tf_op jit(solution)/shard_map/ppermute | solution.py:68
  34.6 16.9 %collective-permute-start.8 = (bf16[2,2,64,384]{3,2,1,0:T(8,128)(2,1)S(1)}, bf16[2,2,64,384]{3,2,1,0:T(8,128)(2,1)S(1)}, u32[]{:S(2)}, u32[]{:S(2)}) collective-permute-start(bf16[2,2,64,384]{3,2,1,0:T(8,128)(2,1)S(1)} %get-tuple-element.55), channel_id=1, source_target_pairs={{0,12},{4,8},{8,4},{12,0},{1,13},{5,9},{9,5},{13,1},{2,14},{6,10},... | collective-permute-start | bytes 589832 | tf_op jit(solution)/shard_map/ppermute | solution.py:68
  38.2 10.0 %collective-permute-start.11 = (bf16[96,384]{1,0:T(8,128)(2,1)S(1)}, bf16[96,384]{1,0:T(8,128)(2,1)S(1)}, u32[]{:S(2)}, u32[]{:S(2)}) collective-permute-start(bf16[96,384]{1,0:T(8,128)(2,1)S(1)} %get-tuple-element.63), channel_id=1, source_target_pairs={{0,4},{4,0},{8,12},{12,8},{1,5},{5,1},{9,13},{13,9},{2,6},{6,2},{1... | collective-permute-start | bytes 221192 | tf_op jit(solution)/shard_map/ppermute | solution.py:348
  40.8 9.4 %collective-permute-start.12 = (bf16[96,384]{1,0:T(8,128)(2,1)S(1)}, bf16[96,384]{1,0:T(8,128)(2,1)S(1)}, u32[]{:S(2)}, u32[]{:S(2)}) collective-permute-start(bf16[96,384]{1,0:T(8,128)(2,1)S(1)} %get-tuple-element.64), channel_id=1, source_target_pairs={{0,4},{4,0},{8,12},{12,8},{1,5},{5,1},{9,13},{13,9},{2,6},{6,2},{1... | collective-permute-start | bytes 221192 | tf_op jit(solution)/shard_map/ppermute | solution.py:348
  50.2 5.3 %collective-permute-start.13 = (bf16[96,384]{1,0:T(8,128)(2,1)S(1)}, bf16[96,384]{1,0:T(8,128)(2,1)S(1)}, u32[]{:S(2)}, u32[]{:S(2)}) collective-permute-start(bf16[96,384]{1,0:T(8,128)(2,1)S(1)} %get-tuple-element.66), channel_id=1, source_target_pairs={{0,8},{4,12},{8,0},{12,4},{1,9},{5,13},{9,1},{13,5},{2,10},{6,14},... | collective-permute-start | bytes 221192 | tf_op jit(solution)/shard_map/ppermute | solution.py:352

commit v4 on v3

--- a/solution.py
+++ b/solution.py
@@ -255,38 +255,53 @@
     branch[...] = out.reshape(branch.shape)
 
 
-def hidden_bwd(count, chunk, with_grad, *refs):
-    pieces = refs[:count]
-    slope, w_project, scaled, d_pre = refs[count : count + 4]
-    grads = refs[-1]
-    frames, pixels, channels = grads.shape
-    tokens = frames * pixels
-    place_frames(count, pieces, grads)
-    grad_rows = grads[...].reshape(tokens, channels).astype(BF16)
+def hidden_bwd(count, steps, with_grad, final, *refs):
+    pieces = refs[: len(steps)]
+    slope, w_project, scaled = refs[len(steps) : len(steps) + 3]
+    refs = refs[len(steps) + 3 :]
+    channels = scaled.shape[1]
+    rows = scaled.shape[0] // count
+    sources = [pl.multiple_of(slot_from(step, count) * rows, rows) for step in steps]
+    grads = jnp.concatenate([p[...].reshape(rows, channels) for p in pieces], axis=0)
+    d_hidden = lax.dot_general(
+        grads, w_project[...], (((1,), (1,)), ((), ())), preferred_element_type=F32
+    )
+    steep = jnp.concatenate([slope[pl.ds(source, rows), :] for source in sources], axis=0)
+    result = (d_hidden * steep.astype(F32)).astype(BF16)
+    if not with_grad:
+        refs[-1][...] = result
+        return
+    inputs = jnp.concatenate([scaled[pl.ds(source, rows), :] for source in sources], axis=0)
+    share = lax.dot_general(result, inputs, (((0,), (0,)), ((), ())), preferred_element_type=F32)
+    if not final:
+        d_pre, full = refs
+        d_pre[...] = result
+        full[...] = share.reshape(full.shape)
+        return
+    before, d_pre, keep, send, full = refs
+    d_pre[...] = result
+    full[...] = share.reshape(full.shape)
+    core = lax.rem(lax.axis_index("dp"), 2)
+    for pair in range(full.shape[0] // 2):
+        mine, other = 2 * pair + core, 2 * pair + 1 - core
+        keep[pair] = full[mine] + before[mine]
+        send[pair] = (full[other] + before[other]).astype(BF16)
+
+
+def token_bwd(count, groups, *refs):
+    parts, refs = refs[: len(groups)], refs[len(groups) :]
+    normed, inv_std, taps, gain, w_expand, branch = refs[:6]
+    outs = refs[6 : count + 6]
+    d_second, d_first = refs[count + 6 :]
+    frames, pixels, channels = d_second.shape
+    own = frames // count
     last = (((1,), (1,)), ((), ()))
-    for start in range(0, w_project.shape[0], chunk):
-        part = slice(start, start + chunk)
-        d_hidden = lax.dot_general(grad_rows, w_project[part, :], last, preferred_element_type=F32)
-        d_pre[:, part] = (d_hidden * slope[:, part].astype(F32)).astype(BF16)
-    if with_grad:
-        keep, send, full = refs[count + 4 : count + 7]
-        full[...] = lax.dot_general(
-            d_pre[...], scaled[...], (((0,), (0,)), ((), ())), preferred_element_type=F32
-        ).reshape(full.shape)
-        core = lax.rem(lax.axis_index("dp"), 2)
-        for pair in range(full.shape[0] // 2):
-            keep[pair] = full[2 * pair + core]
-            send[pair] = full[2 * pair + 1 - core].astype(BF16)
-
-
-def token_bwd(count, *refs):
-    d_pre, normed, inv_std, taps, gain, w_expand, branch = refs[:7]
-    outs = refs[7 : count + 7]
-    d_second, d_first = refs[count + 7 :]
-    frames, pixels, channels = d_second.shape
-    last = (((1,), (1,)), ((), ()))
-    d_scaled = lax.dot_general(d_pre[...], w_expand[...], last, preferred_element_type=F32)
-    d_normed = d_scaled * gain[...].reshape(1, channels)
+    for steps, d_pre in zip(groups, parts):
+        d_scaled = lax.dot_general(d_pre[...], w_expand[...], last, preferred_element_type=F32)
+        d_scaled = d_scaled.reshape(len(steps), own, pixels, channels)
+        for index, step in enumerate(steps):
+            d_second[pl.ds(slot_from(step, count) * own, own)] = d_scaled[index]
+    d_normed = d_second[...].reshape(frames * pixels, channels) * gain[...].reshape(1, channels)
     norm = normed[...]
     d_tokens = inv_std[...] * (
         d_normed
@@ -295,7 +310,6 @@
     )
     d_second[...] = d_tokens.astype(BF16).astype(F32).reshape(frames, pixels, channels)
     mix_frames(d_second, d_first, taps, True)
-    own = frames // count
     for step in range(count):
         base = partner(step, count) * own
         outs[step][0] = branch[pl.ds(base, own)]
@@ -429,22 +443,33 @@
     sides = lax.axis_size("dp")
     staged = count == 4 and sides == 4
     half = (2 * count, hid // (sides * count), channels)
+    whole = (2 * half[0],) + half[1:]
+    groups = [[0, 1], [2, 3]] if staged else [list(range(count))]
+    parts, shares = [], []
+    for steps in groups:
+        rows = len(steps) * tokens // count
+        final = steps is groups[-1]
+        results = [struct((rows, hid), BF16)]
+        if staged and final:
+            results += [struct(half, F32), struct(half, BF16)]
+        elif staged:
+            results += [struct(whole, F32)]
+        part, *shares = call(
+            functools.partial(hidden_bwd, count, steps, staged, final),
+            results,
+            [pltpu.VMEM(whole, F32)] if staged and final else [],
+            *[cots[step] for step in steps],
+            slope,
+            w_project,
+            scaled,
+            *shares,
+        )
+        parts.append(part)
     outs = call(
-        functools.partial(hidden_bwd, count, chunk, staged),
-        [struct((tokens, hid), BF16)] + [struct(half, F32), struct(half, BF16)] * staged,
-        [pltpu.VMEM((2 * half[0],) + half[1:], F32)] * staged + [pltpu.VMEM(column, F32)],
-        *cots,
-        slope,
-        w_project,
-        scaled,
-    )
-    d_pre = outs[0]
-    shares = outs[1:]
-    outs = call(
-        functools.partial(token_bwd, count),
+        functools.partial(token_bwd, count, groups),
         [struct((2,) + back.shape, BF16)] * count,
         [pltpu.VMEM(column, F32), pltpu.VMEM(column, F32)],
-        d_pre,
+        *parts,
         normed,
         inv_std,
         temporal_kernel,
@@ -467,7 +492,7 @@
         grad_expand = scatter_grad(*shares, count, scale_factor, outs[0])
     else:
         whole = lax.dot_general(
-            d_pre, scaled, (((0,), (0,)), ((), ())), preferred_element_type=F32
+            parts[0], scaled, (((0,), (0,)), ((), ())), preferred_element_type=F32
         )
         whole = lax.psum_scatter(whole, ("tm", "dp"), scatter_dimension=0, tiled=True)
         grad_expand = whole * scale_factor

time: 56.4 us -> 55.9 us (level)
  waiting for transfers between devices: 20.1 us -> 18 us
  starting transfers between devices: 21.7 us -> 22.9 us
    ppermute x1, starting transfers between devices: 1.23 us -> 2.45 us  [scatter_grad(): got = lax.ppermute(send, 'tm', [(i, i ^ 2) for i in range(4)])]
    ppermute x6, waiting for transfers between devices: 6.69 us -> 5.74 us  [exchange(): got.append(lax.ppermute(pieces[step], 'tm', pairs))]
    ppermute x1, waiting for transfers between devices: 1.13 us -> 0.4 us  [scatter_grad(): got = lax.ppermute(send, 'tm', [(i, i ^ 2) for i in range(4)])]
    pallas_call x9 -> x10, Pallas kernels: 13.7 us -> 14.1 us  [call(): pl.pallas_call(kernel, out_shape=tuple(outs), in_specs=specs, out_specs=t...]
  transfers between devices with their start and end apart: 14 -> 14, of which waited for: 8 -> 8; matrix products, arithmetic and copies ran while one was open for 0% -> 0% of each run, Pallas kernels for 14% -> 16%
where the time goes in v4:
time: 55.9 us; the launch traced here: 55.7 us
  starting transfers between devices  22.9 us (41%)
  waiting for transfers between devices  18 us (32%)
  Pallas kernels  14.1 us (25%)
  between operations  0.74 us (1%)
    pallas_call x10, Pallas kernels, call(): pl.pallas_call(kernel, out_shape=tuple(outs), in_specs=specs, out_specs=t...  14.1 us
    ppermute x6, starting transfers between devices, exchange(): got.append(lax.ppermute(pieces[step], 'tm', pairs))  11.1 us
    ppermute x2, waiting for transfers between devices, scatter_grad(): lax.ppermute(send, 'tm', [(i, i ^ 1) for i in range(4)])  8.77 us
    ppermute x6, waiting for transfers between devices, exchange(): got.append(lax.ppermute(pieces[step], 'tm', pairs))  5.74 us
    ppermute x3, starting transfers between devices, swap(): got.append(lax.ppermute(pieces[step], 'tm', pairs))  4.94 us
    ppermute x1, waiting for transfers between devices, scatter_grad(): got = lax.ppermute(send, 'dp', [(i, i ^ 2) for i in range(4)])  2.93 us
    ppermute x2, starting transfers between devices, scatter_grad(): lax.ppermute(send, 'tm', [(i, i ^ 1) for i in range(4)])  2.71 us
    ppermute x1, starting transfers between devices, scatter_grad(): got = lax.ppermute(send, 'tm', [(i, i ^ 2) for i in range(4)])  2.45 us
  transfers between devices with their start and end apart: 14, of which 8 were waited for; matrix products, arithmetic and copies ran while one was open for 0% of the time, Pallas kernels for 16%

profile of v4, /device:TPU:0, one launch (start us, length us, event | category | flops | bytes accessed | tf_op | source)
XLA Modules:
  0.0 55.7 jit_solution(9808378706315711003)
XLA Ops:
  0.6 0.0 copy-start.3
  0.6 3.1 %shard_map.94 = (bf16[2,64,384]{2,1,0:T(8,128)(2,1)S(1)}, bf16[2,64,384]{2,1,0:T(8,128)(2,1)S(1)}, bf16[2,64,384]{2,1,0:T(8,128)(2,1)S(1)}, bf16[2,64,384]{2,1,0...) custom-call(bf16[1,2,8,32,384]{4,3,2,1,0:T(8,128)(2,1)} %refs_4_.3, ...), custom_call_target="tpu_custom_call" | custom-call | tf_op jit(solution)/shard_map/pallas_call | solution.py:31
  3.8 3.1 %collective-permute-start.1 = (bf16[2,64,384]{2,1,0:T(8,128)(2,1)S(1)}, bf16[2,64,384]{2,1,0:T(8,128)(2,1)S(1)}, u32[]{:S(2)}, u32[]{:S(2)}) collective-permute-start(bf16[2,64,384]{2,1,0:T(8,128)(2,1)S(1)} %get-tuple-element.40), channel_id=1, source_target_pairs={{0,4},{4,8},{8,12},{12,0},{1,5},{5,9},{9,13},{13,1},{2,6},{6,10},{... | collective-permute-start | bytes 294920 | tf_op jit(solution)/shard_map/ppermute | solution.py:77
  6.9 2.6 %collective-permute-start.2 = (bf16[2,64,384]{2,1,0:T(8,128)(2,1)S(1)}, bf16[2,64,384]{2,1,0:T(8,128)(2,1)S(1)}, u32[]{:S(2)}, u32[]{:S(2)}) collective-permute-start(bf16[2,64,384]{2,1,0:T(8,128)(2,1)S(1)} %get-tuple-element.41), channel_id=1, source_target_pairs={{0,8},{4,12},{8,0},{12,4},{1,9},{5,13},{9,1},{13,5},{2,10},{6,14},... | collective-permute-start | bytes 294920 | tf_op jit(solution)/shard_map/ppermute | solution.py:77
  9.5 1.3 %collective-permute-start.3 = (bf16[2,64,384]{2,1,0:T(8,128)(2,1)S(1)}, bf16[2,64,384]{2,1,0:T(8,128)(2,1)S(1)}, u32[]{:S(2)}, u32[]{:S(2)}) collective-permute-start(bf16[2,64,384]{2,1,0:T(8,128)(2,1)S(1)} %get-tuple-element.42), channel_id=1, source_target_pairs={{0,12},{4,0},{8,4},{12,8},{1,13},{5,1},{9,5},{13,9},{2,14},{6,2},{... | collective-permute-start | bytes 294920 | tf_op jit(solution)/shard_map/ppermute | solution.py:77
  10.8 0.7 %collective-permute-start = (bf16[2,2,32,384]{3,2,1,0:T(8,128)(2,1)S(1)}, bf16[2,2,32,384]{3,2,1,0:T(8,128)(2,1)S(1)}, u32[]{:S(2)}, u32[]{:S(2)}) collective-permute-start(bf16[2,2,32,384]{3,2,1,0:T(8,128)(2,1)S(1)} %get-tuple-element.38), channel_id=1, source_target_pairs={{0,4},{4,8},{8,12},{12,0},{1,5},{5,9},{9,13},{13,1},{2,6},{6,10},{... | collective-permute-start | bytes 294920 | tf_op jit(solution)/shard_map/ppermute | solution.py:77
  11.5 0.3 collective-permute-start.4
  11.8 0.7 %collective-permute-done.1.refs_1_ = bf16[2,64,384]{2,1,0:T(8,128)(2,1)S(1)} collective-permute-done((bf16[2,64,384]{2,1,0:T(8,128)(2,1)S(1)}, bf16[2,64,384]{2,1,0:T(8,128)(2,1)S(1)}, u32[]{:S(2)}, u32[]{:S(2)}) %collective-permute-start.1) | collective-permute-done | bytes 98336 | tf_op jit(solution)/shard_map/ppermute | solution.py:77
  12.5 3.1 %collective-permute-start.5 = (bf16[2,2,32,384]{3,2,1,0:T(8,128)(2,1)S(1)}, bf16[2,2,32,384]{3,2,1,0:T(8,128)(2,1)S(1)}, u32[]{:S(2)}, u32[]{:S(2)}) collective-permute-start(bf16[2,2,32,384]{3,2,1,0:T(8,128)(2,1)S(1)} %get-tuple-element.50), channel_id=1, source_target_pairs={{0,12},{4,0},{8,4},{12,8},{1,13},{5,1},{9,5},{13,9},{2,14},{6,2},{... | collective-permute-start | bytes 294920 | tf_op jit(solution)/shard_map/ppermute | solution.py:77
  15.7 3.9 %collective-permute-done.2.refs_2_ = bf16[2,64,384]{2,1,0:T(8,128)(2,1)S(1)} collective-permute-done((bf16[2,64,384]{2,1,0:T(8,128)(2,1)S(1)}, bf16[2,64,384]{2,1,0:T(8,128)(2,1)S(1)}, u32[]{:S(2)}, u32[]{:S(2)}) %collective-permute-start.2) | collective-permute-done | bytes 98336 | tf_op jit(solution)/shard_map/ppermute | solution.py:77
  19.6 0.0 collective-permute-done.3.refs_3_
  19.6 0.0 copy-done.3
  19.6 2.8 %shard_map.95 = (bf16[8,64,384]{2,1,0:T(8,128)(2,1)S(1)}, bf16[512,384]{1,0:T(8,128)(2,1)S(1)}, bf16[512,1536]{1,0:T(8,128)(2,1)S(1)}, f32[512,384]{1,0:T(8,128)S(1)}, f32[512,1]{1,0:T(8,128)S(1)}) custom-call(bf16[2,64,384]{2,1,0:T(8,128)(2,1)S(1)} %get-tuple-element.39.refs_0_, bf16[2,64,384]{2,1,0:T(8,128)(2,1)S(1)} %collective-permute-done.1.refs_1_, ...), custom_call_target="tpu_custom_call" | custom-call | tf_op jit(solution)/shard_map/pallas_call | solution.py:31
  22.3 0.0 collective-permute-done.refs_1_
  22.4 1.0 %shard_map.96 = (bf16[256,1536]{1,0:T(8,128)(2,1)S(1)}, f32[16,96,384]{2,1,0:T(8,128)S(1)}) custom-call(bf16[2,2,32,384]{3,2,1,0:T(8,128)(2,1)S(1)} %get-tuple-element.37.refs_0_, bf16[2,2,32,384]{3,2,1,0:T(8,128)(2,1)S(1)} %collective-permute-done.refs_1_, bf16[512,1536]{1,0:T(8,128)(2,1)S(1)} %get-tuple-element.46.refs_2_, ...), custom_call_target="tpu_custom_call" | custom-call | tf_op jit(solution)/shard_map/pallas_call | solution.py:31
  23.4 1.1 %collective-permute-done.4.refs_0_ = bf16[2,2,32,384]{3,2,1,0:T(8,128)(2,1)S(1)} collective-permute-done((bf16[2,2,32,384]{3,2,1,0:T(8,128)(2,1)S(1)}, bf16[2,2,32,384]{3,2,1,0:T(8,128)(2,1)S(1)}, u32[]{:S(2)}, u32[]{:S(2)}) %collective-permute-start.4) | collective-permute-done | bytes 98336 | tf_op jit(solution)/shard_map/ppermute | solution.py:77
  24.5 0.0 collective-permute-done.5.refs_1_
  24.5 1.5 %shard_map.97 = (bf16[256,1536]{1,0:T(8,128)(2,1)S(1)}, f32[8,96,384]{2,1,0:T(8,128)S(1)}, bf16[8,96,384]{2,1,0:T(8,128)(2,1)S(1)}) custom-call(bf16[2,2,32,384]{3,2,1,0:T(8,128)(2,1)S(1)} %collective-permute-done.4.refs_0_, bf16[2,2,32,384]{3,2,1,0:T(8,128)(2,1)S(1)} %collective-permute-done.5.refs_1_, bf16[512,1536]{1,0:T(8,128)(2,1)S(1)} %get-tuple-element.46.refs_2_, ...), custom_call_target="tpu_custom_call" | custom-call | tf_op jit(solution)/shard_map/pallas_call | solution.py:31
  26.0 0.1 collective-permute-start.9
  26.1 1.9 %shard_map.98 = (bf16[2,2,64,384]{3,2,1,0:T(8,128)(2,1)S(1)}, bf16[2,2,64,384]{3,2,1,0:T(8,128)(2,1)S(1)}, bf16[2,2,64,384]{3,2,1,0:T(8,128)(2,1)S(1)}, bf16[2,2,64,384]{3,2,1,0:T(8,128)(2,1)S(1)}) custom-call(bf16[256,1536]{1,0:T(8,128)(2,1)S(1)} %get-tuple-element.48.refs_0_, bf16[256,1536]{1,0:T(8,128)(2,1)S(1)} %get-tuple-element.52.refs_1_, ...), custom_call_target="tpu_custom_call" | custom-call | tf_op jit(solution)/shard_map/pallas_call | solution.py:31
  28.0 0.1 collective-permute-done.9.refs_1_
  28.1 0.0 copy-start
  28.1 0.0 copy-start.1
  28.1 0.0 copy-start.2
  28.1 0.1 shard_map.100
  28.2 1.5 %collective-permute-start.10 = (bf16[4,96,384]{2,1,0:T(8,128)(2,1)S(1)}, bf16[4,96,384]{2,1,0:T(8,128)(2,1)S(1)}, u32[]{:S(2)}, u32[]{:S(2)}) collective-permute-start(bf16[4,96,384]{2,1,0:T(8,128)(2,1)S(1)} %get-tuple-element.65), channel_id=1, source_target_pairs={{0,2},{1,3},{2,0},{3,1},{4,6},{5,7},{6,4},{7,5},{8,10},{9,11},{10,... | collective-permute-start | bytes 884744 | tf_op jit(solution)/shard_map/ppermute | solution.py:357
  29.7 2.6 %collective-permute-start.6 = (bf16[2,2,64,384]{3,2,1,0:T(8,128)(2,1)S(1)}, bf16[2,2,64,384]{3,2,1,0:T(8,128)(2,1)S(1)}, u32[]{:S(2)}, u32[]{:S(2)}) collective-permute-start(bf16[2,2,64,384]{3,2,1,0:T(8,128)(2,1)S(1)} %get-tuple-element.57), channel_id=1, source_target_pairs={{0,4},{4,0},{8,12},{12,8},{1,5},{5,1},{9,13},{13,9},{2,6},{6,2},{1... | collective-permute-start | bytes 589832 | tf_op jit(solution)/shard_map/ppermute | solution.py:68
  32.3 2.3 %collective-permute-start.7 = (bf16[2,2,64,384]{3,2,1,0:T(8,128)(2,1)S(1)}, bf16[2,2,64,384]{3,2,1,0:T(8,128)(2,1)S(1)}, u32[]{:S(2)}, u32[]{:S(2)}) collective-permute-start(bf16[2,2,64,384]{3,2,1,0:T(8,128)(2,1)S(1)} %get-tuple-element.58), channel_id=1, source_target_pairs={{0,8},{4,12},{8,0},{12,4},{1,9},{5,13},{9,1},{13,5},{2,10},{6,14},... | collective-permute-start | bytes 589832 | tf_op jit(solution)/shard_map/ppermute | solution.py:68
  34.6 0.0 collective-permute-start.8
  34.7 2.9 %collective-permute-done.10.refs_1_ = bf16[4,96,384]{2,1,0:T(8,128)(2,1)S(1)} collective-permute-done((bf16[4,96,384]{2,1,0:T(8,128)(2,1)S(1)}, bf16[4,96,384]{2,1,0:T(8,128)(2,1)S(1)}, u32[]{:S(2)}, u32[]{:S(2)}) %collective-permute-start.10) | collective-permute-done | bytes 294944 | tf_op jit(solution)/shard_map/ppermute | solution.py:357
  37.6 0.1 shard_map.101
  37.7 2.6 %collective-permute-start.11 = (bf16[96,384]{1,0:T(8,128)(2,1)S(1)}, bf16[96,384]{1,0:T(8,128)(2,1)S(1)}, u32[]{:S(2)}, u32[]{:S(2)}) collective-permute-start(bf16[96,384]{1,0:T(8,128)(2,1)S(1)} %get-tuple-element.67), channel_id=1, source_target_pairs={{0,4},{4,0},{8,12},{12,8},{1,5},{5,1},{9,13},{13,9},{2,6},{6,2},{1... | collective-permute-start | bytes 221192 | tf_op jit(solution)/shard_map/ppermute | solution.py:362
  40.3 0.1 collective-permute-start.12
  40.4 7.3 %collective-permute-done.11.refs_1_ = bf16[96,384]{1,0:T(8,128)(2,1)S(1)} collective-permute-done((bf16[96,384]{1,0:T(8,128)(2,1)S(1)}, bf16[96,384]{1,0:T(8,128)(2,1)S(1)}, u32[]{:S(2)}, u32[]{:S(2)}) %collective-permute-start.11) | collective-permute-done | bytes 73760 | tf_op jit(solution)/shard_map/ppermute | solution.py:362
  47.7 1.5 %collective-permute-done.12.refs_2_ = bf16[96,384]{1,0:T(8,128)(2,1)S(1)} collective-permute-done((bf16[96,384]{1,0:T(8,128)(2,1)S(1)}, bf16[96,384]{1,0:T(8,128)(2,1)S(1)}, u32[]{:S(2)}, u32[]{:S(2)}) %collective-permute-start.12) | collective-permute-done | bytes 73760 | tf_op jit(solution)/shard_map/ppermute | solution.py:362
  49.2 2.4 %collective-permute-start.13 = (bf16[96,384]{1,0:T(8,128)(2,1)S(1)}, bf16[96,384]{1,0:T(8,128)(2,1)S(1)}, u32[]{:S(2)}, u32[]{:S(2)}) collective-permute-start(bf16[96,384]{1,0:T(8,128)(2,1)S(1)} %get-tuple-element.70), channel_id=1, source_target_pairs={{0,8},{4,12},{8,0},{12,4},{1,9},{5,13},{9,1},{13,5},{2,10},{6,14},... | collective-permute-start | bytes 221192 | tf_op jit(solution)/shard_map/ppermute | solution.py:366
  51.6 0.0 collective-permute-done.6.refs_1_
  51.6 0.0 collective-permute-done.7.refs_2_
  51.6 0.0 collective-permute-done.8.refs_3_
  51.7 0.0 copy-done
  51.7 0.0 copy-done.1
  51.7 0.0 copy-done.2
  51.7 2.9 %shard_map.99 = (bf16[1,2,8,32,384]{4,3,2,1,0:T(8,128)(2,1)}, bf16[1,2,8,32,384]{4,3,2,1,0:T(8,128)(2,1)}) custom-call(bf16[2,2,64,384]{3,2,1,0:T(8,128)(2,1)S(1)} %get-tuple-element.56.refs_0_.refs_2_, bf16[2,2,64,384]{3,2,1,0:T(8,128)(2,1)S(1)} %collective-permute-done.6.refs_1_, bf16[2,2,64,384]{3,2,1,0:T(8,128)(2,1)S(1)} %collective-permute-done.7.refs_2_, ...), custom_call_target="tpu_custom_call" | custom-call | tf_op jit(solution)/shard_map/pallas_call | solution.py:31
  54.6 0.4 collective-permute-done.13.refs_1_
  55.0 0.7 %shard_map.103 = f32[96,384]{1,0:T(8,128)} custom-call(f32[96,384]{1,0:T(8,128)S(1)} %get-tuple-element.69.refs_0_, bf16[96,384]{1,0:T(8,128)(2,1)S(1)} %collective-permute-done.13.refs_1_), custom_call_target="tpu_custom_call" | custom-call | tf_op jit(solution)/shard_map/pallas_call | solution.py:31
  (1 shorter events, 0.0 us)
Async XLA Ops:
  0.6 19.0 %copy-start.3 = (f32[384]{0:T(512)S(1)}, f32[384]{0:T(512)}, u32[]{:S(2)}) copy-start(f32[384]{0:T(512)} %refs_5_.6) | copy-start | bytes 4612
  3.8 8.8 %collective-permute-start.1 = (bf16[2,64,384]{2,1,0:T(8,128)(2,1)S(1)}, bf16[2,64,384]{2,1,0:T(8,128)(2,1)S(1)}, u32[]{:S(2)}, u32[]{:S(2)}) collective-permute-start(bf16[2,64,384]{2,1,0:T(8,128)(2,1)S(1)} %get-tuple-element.40), channel_id=1, source_target_pairs={{0,4},{4,8},{8,12},{12,0},{1,5},{5,9},{9,13},{13,1},{2,6},{6,10},{... | collective-permute-start | bytes 294920 | tf_op jit(solution)/shard_map/ppermute | solution.py:77
  6.9 12.7 %collective-permute-start.2 = (bf16[2,64,384]{2,1,0:T(8,128)(2,1)S(1)}, bf16[2,64,384]{2,1,0:T(8,128)(2,1)S(1)}, u32[]{:S(2)}, u32[]{:S(2)}) collective-permute-start(bf16[2,64,384]{2,1,0:T(8,128)(2,1)S(1)} %get-tuple-element.41), channel_id=1, source_target_pairs={{0,8},{4,12},{8,0},{12,4},{1,9},{5,13},{9,1},{13,5},{2,10},{6,14},... | collective-permute-start | bytes 294920 | tf_op jit(solution)/shard_map/ppermute | solution.py:77
  9.5 10.1 %collective-permute-start.3 = (bf16[2,64,384]{2,1,0:T(8,128)(2,1)S(1)}, bf16[2,64,384]{2,1,0:T(8,128)(2,1)S(1)}, u32[]{:S(2)}, u32[]{:S(2)}) collective-permute-start(bf16[2,64,384]{2,1,0:T(8,128)(2,1)S(1)} %get-tuple-element.42), channel_id=1, source_target_pairs={{0,12},{4,0},{8,4},{12,8},{1,13},{5,1},{9,5},{13,9},{2,14},{6,2},{... | collective-permute-start | bytes 294920 | tf_op jit(solution)/shard_map/ppermute | solution.py:77
  10.8 11.5 %collective-permute-start = (bf16[2,2,32,384]{3,2,1,0:T(8,128)(2,1)S(1)}, bf16[2,2,32,384]{3,2,1,0:T(8,128)(2,1)S(1)}, u32[]{:S(2)}, u32[]{:S(2)}) collective-permute-start(bf16[2,2,32,384]{3,2,1,0:T(8,128)(2,1)S(1)} %get-tuple-element.38), channel_id=1, source_target_pairs={{0,4},{4,8},{8,12},{12,0},{1,5},{5,9},{9,13},{13,1},{2,6},{6,10},{... | collective-permute-start | bytes 294920 | tf_op jit(solution)/shard_map/ppermute | solution.py:77
  11.5 13.0 %collective-permute-start.4 = (bf16[2,2,32,384]{3,2,1,0:T(8,128)(2,1)S(1)}, bf16[2,2,32,384]{3,2,1,0:T(8,128)(2,1)S(1)}, u32[]{:S(2)}, u32[]{:S(2)}) collective-permute-start(bf16[2,2,32,384]{3,2,1,0:T(8,128)(2,1)S(1)} %get-tuple-element.49), channel_id=1, source_target_pairs={{0,8},{4,12},{8,0},{12,4},{1,9},{5,13},{9,1},{13,5},{2,10},{6,14},... | collective-permute-start | bytes 294920 | tf_op jit(solution)/shard_map/ppermute | solution.py:77
  12.5 11.9 %collective-permute-start.5 = (bf16[2,2,32,384]{3,2,1,0:T(8,128)(2,1)S(1)}, bf16[2,2,32,384]{3,2,1,0:T(8,128)(2,1)S(1)}, u32[]{:S(2)}, u32[]{:S(2)}) collective-permute-start(bf16[2,2,32,384]{3,2,1,0:T(8,128)(2,1)S(1)} %get-tuple-element.50), channel_id=1, source_target_pairs={{0,12},{4,0},{8,4},{12,8},{1,13},{5,1},{9,5},{13,9},{2,14},{6,2},{... | collective-permute-start | bytes 294920 | tf_op jit(solution)/shard_map/ppermute | solution.py:77
  26.0 2.1 %collective-permute-start.9 = (bf16[8,96,384]{2,1,0:T(8,128)(2,1)S(1)}, bf16[8,96,384]{2,1,0:T(8,128)(2,1)S(1)}, u32[]{:S(2)}, u32[]{:S(2)}) collective-permute-start(bf16[8,96,384]{2,1,0:T(8,128)(2,1)S(1)} %get-tuple-element.63), channel_id=1, source_target_pairs={{0,1},{1,0},{2,3},{3,2},{4,5},{5,4},{6,7},{7,6},{8,9},{9,8},{10,11... | collective-permute-start | bytes 1769480 | tf_op jit(solution)/shard_map/ppermute | solution.py:353
  28.1 23.6 %copy-start = (bf16[1,2,8,32,384]{4,3,2,1,0:T(8,128)(2,1)S(1)}, bf16[1,2,8,32,384]{4,3,2,1,0:T(8,128)(2,1)}, u32[]{:S(2)}) copy-start(bf16[1,2,8,32,384]{4,3,2,1,0:T(8,128)(2,1)} %refs_4_.3) | copy-start | bytes 1179652
  28.1 23.6 %copy-start.1 = (bf16[1,2,8,32,384]{4,3,2,1,0:T(8,128)(2,1)S(1)}, bf16[1,2,8,32,384]{4,3,2,1,0:T(8,128)(2,1)}, u32[]{:S(2)}) copy-start(bf16[1,2,8,32,384]{4,3,2,1,0:T(8,128)(2,1)} %refs_5_.7) | copy-start | bytes 1179652
  28.1 23.6 %copy-start.2 = (f32[7,7,384]{2,1,0:T(8,128)S(1)}, f32[7,7,384]{2,1,0:T(8,128)}, u32[]{:S(2)}) copy-start(f32[7,7,384]{2,1,0:T(8,128)} %refs_6_.1) | copy-start | bytes 225796
  28.2 9.4 %collective-permute-start.10 = (bf16[4,96,384]{2,1,0:T(8,128)(2,1)S(1)}, bf16[4,96,384]{2,1,0:T(8,128)(2,1)S(1)}, u32[]{:S(2)}, u32[]{:S(2)}) collective-permute-start(bf16[4,96,384]{2,1,0:T(8,128)(2,1)S(1)} %get-tuple-element.65), channel_id=1, source_target_pairs={{0,2},{1,3},{2,0},{3,1},{4,6},{5,7},{6,4},{7,5},{8,10},{9,11},{10,... | collective-permute-start | bytes 884744 | tf_op jit(solution)/shard_map/ppermute | solution.py:357
  29.7 21.9 %collective-permute-start.6 = (bf16[2,2,64,384]{3,2,1,0:T(8,128)(2,1)S(1)}, bf16[2,2,64,384]{3,2,1,0:T(8,128)(2,1)S(1)}, u32[]{:S(2)}, u32[]{:S(2)}) collective-permute-start(bf16[2,2,64,384]{3,2,1,0:T(8,128)(2,1)S(1)} %get-tuple-element.57), channel_id=1, source_target_pairs={{0,4},{4,0},{8,12},{12,8},{1,5},{5,1},{9,13},{13,9},{2,6},{6,2},{1... | collective-permute-start | bytes 589832 | tf_op jit(solution)/shard_map/ppermute | solution.py:68
  32.3 19.3 %collective-permute-start.7 = (bf16[2,2,64,384]{3,2,1,0:T(8,128)(2,1)S(1)}, bf16[2,2,64,384]{3,2,1,0:T(8,128)(2,1)S(1)}, u32[]{:S(2)}, u32[]{:S(2)}) collective-permute-start(bf16[2,2,64,384]{3,2,1,0:T(8,128)(2,1)S(1)} %get-tuple-element.58), channel_id=1, source_target_pairs={{0,8},{4,12},{8,0},{12,4},{1,9},{5,13},{9,1},{13,5},{2,10},{6,14},... | collective-permute-start | bytes 589832 | tf_op jit(solution)/shard_map/ppermute | solution.py:68
  34.6 17.0 %collective-permute-start.8 = (bf16[2,2,64,384]{3,2,1,0:T(8,128)(2,1)S(1)}, bf16[2,2,64,384]{3,2,1,0:T(8,128)(2,1)S(1)}, u32[]{:S(2)}, u32[]{:S(2)}) collective-permute-start(bf16[2,2,64,384]{3,2,1,0:T(8,128)(2,1)S(1)} %get-tuple-element.59), channel_id=1, source_target_pairs={{0,12},{4,8},{8,4},{12,0},{1,13},{5,9},{9,5},{13,1},{2,14},{6,10},... | collective-permute-start | bytes 589832 | tf_op jit(solution)/shard_map/ppermute | solution.py:68
  37.7 10.0 %collective-permute-start.11 = (bf16[96,384]{1,0:T(8,128)(2,1)S(1)}, bf16[96,384]{1,0:T(8,128)(2,1)S(1)}, u32[]{:S(2)}, u32[]{:S(2)}) collective-permute-start(bf16[96,384]{1,0:T(8,128)(2,1)S(1)} %get-tuple-element.67), channel_id=1, source_target_pairs={{0,4},{4,0},{8,12},{12,8},{1,5},{5,1},{9,13},{13,9},{2,6},{6,2},{1... | collective-permute-start | bytes 221192 | tf_op jit(solution)/shard_map/ppermute | solution.py:362
  40.3 8.8 %collective-permute-start.12 = (bf16[96,384]{1,0:T(8,128)(2,1)S(1)}, bf16[96,384]{1,0:T(8,128)(2,1)S(1)}, u32[]{:S(2)}, u32[]{:S(2)}) collective-permute-start(bf16[96,384]{1,0:T(8,128)(2,1)S(1)} %get-tuple-element.68), channel_id=1, source_target_pairs={{0,4},{4,0},{8,12},{12,8},{1,5},{5,1},{9,13},{13,9},{2,6},{6,2},{1... | collective-permute-start | bytes 221192 | tf_op jit(solution)/shard_map/ppermute | solution.py:362
  49.2 5.8 %collective-permute-start.13 = (bf16[96,384]{1,0:T(8,128)(2,1)S(1)}, bf16[96,384]{1,0:T(8,128)(2,1)S(1)}, u32[]{:S(2)}, u32[]{:S(2)}) collective-permute-start(bf16[96,384]{1,0:T(8,128)(2,1)S(1)} %get-tuple-element.70), channel_id=1, source_target_pairs={{0,8},{4,12},{8,0},{12,4},{1,9},{5,13},{9,1},{13,5},{2,10},{6,14},... | collective-permute-start | bytes 221192 | tf_op jit(solution)/shard_map/ppermute | solution.py:366

commit v5 on v4

--- a/solution.py
+++ b/solution.py
@@ -78,24 +78,25 @@
     return got
 
 
-def conv_rows(pad_ref, kernel_ref, block, col, height, flip, emit):
+def conv_rows(pad_ref, kernel_ref, block, col, height, flip, emit, low=0, high=None):
     taps = kernel_ref.shape[0]
     lanes = slice(block * LANES, (block + 1) * LANES)
     radius = taps // 2
+    high = height if high is None else high
     acc = [None] * height
     for col_off in range(taps):
         shift = radius - col_off if flip else col_off - radius
         weights = [
             kernel_ref[row_off, pl.ds(col_off, 1), lanes] for row_off in range(taps)
         ]
-        for row in range(height):
+        for row in range(max(low - radius, 0), min(high + radius, height)):
             values = pad_ref[block, :, row, pl.ds(PAD + col + shift, 8), :]
             for row_off in range(taps):
                 out = row - radius + row_off if flip else row + radius - row_off
-                if 0 <= out < height:
+                if low <= out < high:
                     term = values * weights[row_off][None]
                     acc[out] = term if acc[out] is None else acc[out] + term
-    for row in range(height):
+    for row in range(low, high):
         emit(row, acc[row])
 
 
@@ -151,11 +152,78 @@
 
             conv_rows(pad_ref, kernel, block, col, height, False, emit)
     for step in range(count):
-        base = slot_to(step, count) * rows
+        base = partner(step, count) * rows
         firsts[step][...] = (
             flat[:, pl.ds(base, rows), :, :].reshape(frames, pixels, channels).astype(BF16)
         )
     for copy in copies[2:]:
+        copy.wait()
+
+
+def half_rows(pad_ref, kernel, flat, half):
+    blocks, _, height, padded, _ = pad_ref.shape
+    for value in range(2):
+        low = value * height // 2
+
+        @pl.when(half == value)
+        def _():
+            for block in range(blocks):
+                lanes = slice(block * LANES, (block + 1) * LANES)
+                for col in range(0, padded - 2 * PAD, 8):
+
+                    def emit(row, result):
+                        flat[:, row - low, pl.ds(col, 8), lanes] = result
+
+                    conv_rows(
+                        pad_ref, kernel, block, col, height, False, emit, low, low + height // 2
+                    )
+
+
+def spatial_far(clips_far, kernel_far, first_a, first_b, pad_ref, kernel, clips, flat, sems):
+    frames, height, width, channels = clips.shape
+    copies = [
+        pltpu.make_async_copy(clips_far.at[0], clips, sems.at[0]),
+        pltpu.make_async_copy(kernel_far, kernel, sems.at[1]),
+    ]
+    for copy in copies:
+        copy.start()
+    clear_pads(pad_ref, width)
+    copies[0].wait()
+    for block in range(channels // LANES):
+        lanes = slice(block * LANES, (block + 1) * LANES)
+        pad_ref[block, :, :, PAD : PAD + width, :] = clips[:, :, :, lanes].astype(F32)
+    copies[1].wait()
+    half = 1 - lax.div(lax.axis_index("tm"), 2)
+    half_rows(pad_ref, kernel, flat, half)
+    rows = height // 4
+    for step, out in ((2, first_a), (3, first_b)):
+        base = partner(step, 4) * rows - half * (height // 2)
+        out[...] = flat[:, pl.ds(base, rows)].reshape(out.shape).astype(BF16)
+
+
+def spatial_near(held, *refs):
+    cot_far, fars = refs[0], refs[1 : 1 + held]
+    pad_ref, kernel, first_own, first_near = refs[1 + held : 5 + held]
+    cots, nears = refs[5 + held : 9 + held], refs[9 + held : 9 + 2 * held]
+    flat, sems = refs[9 + 2 * held :]
+    height = pad_ref.shape[2]
+    rows = height // 4
+    copies = []
+    for step in range(4):
+        base = slot_to(step, 4) * rows
+        copies.append(
+            pltpu.make_async_copy(cot_far.at[0, :, pl.ds(base, rows)], cots[step], sems.at[step])
+        )
+    for index in range(held):
+        copies.append(pltpu.make_async_copy(fars[index], nears[index], sems.at[4 + index]))
+    for copy in copies:
+        copy.start()
+    half = lax.div(lax.axis_index("tm"), 2)
+    half_rows(pad_ref, kernel, flat, half)
+    for step, out in ((0, first_own), (1, first_near)):
+        base = partner(step, 4) * rows - half * (height // 2)
+        out[...] = flat[:, pl.ds(base, rows)].reshape(out.shape).astype(BF16)
+    for copy in copies:
         copy.wait()
 
 
@@ -224,7 +292,7 @@
 def place_frames(count, pieces, target):
     for step in range(count):
         frames = pieces[step].shape[0]
-        base = slot_from(step, count) * frames
+        base = partner(step, count) * frames
         piece = pieces[step][...].reshape((frames,) + target.shape[1:])
         target[pl.ds(base, frames)] = piece.astype(target.dtype)
 
@@ -396,23 +464,47 @@
     piece = struct((frames, pixels // count, channels), BF16)
     cot_piece = struct((frames, height // count, width, channels), BF16)
     held = [temporal_kernel, w_expand, w_project]
-    outs = call(
-        functools.partial(spatial_fwd, count),
-        [piece] * count + [cot_piece] * count + [struct(a.shape, a.dtype) for a in held],
-        [
-            pltpu.VMEM(clips.shape[1:], BF16),
-            pltpu.VMEM(spatial_kernel.shape, F32),
-            pad,
-            pltpu.VMEM((frames, height, width, channels), F32),
-            pltpu.SemaphoreType.DMA((2 + count + len(held),)),
-        ],
-        clips,
-        cotangent,
-        spatial_kernel,
-        *held,
-        far=3 + len(held),
-    )
-    firsts = to_columns(list(outs[:count]))
+    kept = [struct(a.shape, a.dtype) for a in held]
+    image = (frames, height, width, channels)
+    if count == 4:
+        half_image = pltpu.VMEM((frames, height // 2, width, channels), F32)
+        *far, padded, taps = call(
+            spatial_far,
+            [piece] * 2 + [struct(pad.shape, F32), struct(spatial_kernel.shape, F32)],
+            [pltpu.VMEM(image, BF16), half_image, pltpu.SemaphoreType.DMA((2,))],
+            clips,
+            spatial_kernel,
+            far=2,
+        )
+        outs = call(
+            functools.partial(spatial_near, len(held)),
+            [piece] * 2 + [cot_piece] * count + kept,
+            [half_image, pltpu.SemaphoreType.DMA((count + len(held),))],
+            cotangent,
+            *held,
+            padded,
+            taps,
+            far=1 + len(held),
+        )
+        outs = [outs[0], outs[1], *far, *outs[2:]]
+    else:
+        outs = call(
+            functools.partial(spatial_fwd, count),
+            [piece] * count + [cot_piece] * count + [struct(a.shape, a.dtype) for a in held],
+            [
+                pltpu.VMEM(clips.shape[1:], BF16),
+                pltpu.VMEM(spatial_kernel.shape, F32),
+                pad,
+                pltpu.VMEM((frames, height, width, channels), F32),
+                pltpu.SemaphoreType.DMA((2 + count + len(held),)),
+            ],
+            clips,
+            cotangent,
+            spatial_kernel,
+            *held,
+            far=3 + len(held),
+        )
+    firsts = swap(outs[:count]) if count > 1 else to_columns(list(outs[:count]))
     cots = to_columns(list(outs[count : 2 * count]))
     temporal_kernel, w_expand, w_project = outs[2 * count :]
 

time: 55.9 us -> 55.7 us (level)
  waiting for transfers between devices: 18 us -> 15.7 us
  Pallas kernels: 14.1 us -> 15.3 us
  starting transfers between devices: 22.9 us -> 23.7 us
    ppermute x6 -> x3, starting transfers between devices: 11.1 us -> 5.5 us  [exchange(): got.append(lax.ppermute(pieces[step], 'tm', pairs))]
    ppermute x3 -> x6, starting transfers between devices: 4.94 us -> 10.6 us  [swap(): got.append(lax.ppermute(pieces[step], 'tm', pairs))]
    ppermute x6 -> x3, waiting for transfers between devices: 5.74 us -> 0.62 us  [exchange(): got.append(lax.ppermute(pieces[step], 'tm', pairs))]
    ppermute x3 -> x6, waiting for transfers between devices: 0.01 us -> 2.68 us  [swap(): got.append(lax.ppermute(pieces[step], 'tm', pairs))]
    pallas_call x10 -> x11, Pallas kernels: 14.1 us -> 15.3 us  [call(): pl.pallas_call(kernel, out_shape=tuple(outs), in_specs=specs, out_specs=t...]
    ppermute x1, starting transfers between devices: 2.45 us -> 3.11 us  [scatter_grad(): got = lax.ppermute(send, 'tm', [(i, i ^ 2) for i in range(4)])]
  transfers between devices with their start and end apart: 14 -> 14, of which waited for: 8 -> 8; matrix products, arithmetic and copies ran while one was open for 0% -> 0% of each run, Pallas kernels for 16% -> 19%
where the time goes in v5:
time: 55.7 us; the launch traced here: 55.5 us
  starting transfers between devices  23.7 us (43%)
  waiting for transfers between devices  15.7 us (28%)
  Pallas kernels  15.3 us (27%)
  between operations  0.73 us (1%)
    pallas_call x11, Pallas kernels, call(): pl.pallas_call(kernel, out_shape=tuple(outs), in_specs=specs, out_specs=t...  15.3 us
    ppermute x6, starting transfers between devices, swap(): got.append(lax.ppermute(pieces[step], 'tm', pairs))  10.6 us
    ppermute x2, waiting for transfers between devices, scatter_grad(): lax.ppermute(send, 'tm', [(i, i ^ 1) for i in range(4)])  8.77 us
    ppermute x3, starting transfers between devices, exchange(): got.append(lax.ppermute(pieces[step], 'tm', pairs))  5.5 us
    ppermute x1, starting transfers between devices, scatter_grad(): got = lax.ppermute(send, 'tm', [(i, i ^ 2) for i in range(4)])  3.11 us
    ppermute x6, waiting for transfers between devices, swap(): got.append(lax.ppermute(pieces[step], 'tm', pairs))  2.68 us
    ppermute x1, waiting for transfers between devices, scatter_grad(): got = lax.ppermute(send, 'dp', [(i, i ^ 2) for i in range(4)])  2.59 us
    ppermute x2, starting transfers between devices, scatter_grad(): lax.ppermute(send, 'tm', [(i, i ^ 1) for i in range(4)])  2.43 us
  transfers between devices with their start and end apart: 14, of which 8 were waited for; matrix products, arithmetic and copies ran while one was open for 0% of the time, Pallas kernels for 19%

profile of v5, /device:TPU:0, one launch (start us, length us, event | category | flops | bytes accessed | tf_op | source)
XLA Modules:
  0.0 55.5 jit_solution(12224806281983292884)
XLA Ops:
  0.6 2.4 %shard_map.94 = (bf16[2,64,384]{2,1,0:T(8,128)(2,1)S(1)}, bf16[2,64,384]{2,1,0:T(8,128)(2,1)S(1)}, f32[3,2,8,48,128]{4,3,2,1,0:T(8,128)S(1)}, f32[7,7,384]{2,1,0:T(8,128)S(1)}) custom-call(bf16[1,2,8,32,384]{4,3,2,1,0:T(8,128)(2,1)} %refs_4_.1, f32[7,7,384]{2,1,0:T(8,128)} %refs_6_.1), custom_call_target="tpu_custom_call" | custom-call | tf_op jit(solution)/shard_map/pallas_call | solution.py:31
  3.0 3.9 %collective-permute-start.2 = (bf16[2,64,384]{2,1,0:T(8,128)(2,1)S(1)}, bf16[2,64,384]{2,1,0:T(8,128)(2,1)S(1)}, u32[]{:S(2)}, u32[]{:S(2)}) collective-permute-start(bf16[2,64,384]{2,1,0:T(8,128)(2,1)S(1)} %get-tuple-element.45), channel_id=1, source_target_pairs={{0,8},{4,12},{8,0},{12,4},{1,9},{5,13},{9,1},{13,5},{2,10},{6,14},... | collective-permute-start | bytes 294920 | tf_op jit(solution)/shard_map/ppermute | solution.py:68
  6.9 1.5 %collective-permute-start.3 = (bf16[2,64,384]{2,1,0:T(8,128)(2,1)S(1)}, bf16[2,64,384]{2,1,0:T(8,128)(2,1)S(1)}, u32[]{:S(2)}, u32[]{:S(2)}) collective-permute-start(bf16[2,64,384]{2,1,0:T(8,128)(2,1)S(1)} %get-tuple-element.46), channel_id=1, source_target_pairs={{0,12},{4,8},{8,4},{12,0},{1,13},{5,9},{9,5},{13,1},{2,14},{6,10},... | collective-permute-start | bytes 294920 | tf_op jit(solution)/shard_map/ppermute | solution.py:68
  8.5 0.0 copy-start.3
  8.5 1.9 %shard_map.95 = (bf16[2,64,384]{2,1,0:T(8,128)(2,1)S(1)}, bf16[2,64,384]{2,1,0:T(8,128)(2,1)S(1)}, bf16[2,2,32,384]{3,2,1,0:T(8,128)(2,1)S(1)}, bf16[2,2,32,384]...) custom-call(bf16[1,2,8,32,384]{4,3,2,1,0:T(8,128)(2,1)} %refs_5_.5, ...), custom_call_target="tpu_custom_call" | custom-call | tf_op jit(solution)/shard_map/pallas_call | solution.py:31
  10.4 0.1 collective-permute-start.1
  10.5 2.0 %collective-permute-start = (bf16[2,2,32,384]{3,2,1,0:T(8,128)(2,1)S(1)}, bf16[2,2,32,384]{3,2,1,0:T(8,128)(2,1)S(1)}, u32[]{:S(2)}, u32[]{:S(2)}) collective-permute-start(bf16[2,2,32,384]{3,2,1,0:T(8,128)(2,1)S(1)} %get-tuple-element.42), channel_id=1, source_target_pairs={{0,4},{4,8},{8,12},{12,0},{1,5},{5,9},{9,13},{13,1},{2,6},{6,10},{... | collective-permute-start | bytes 294920 | tf_op jit(solution)/shard_map/ppermute | solution.py:77
  12.5 1.5 %collective-permute-start.4 = (bf16[2,2,32,384]{3,2,1,0:T(8,128)(2,1)S(1)}, bf16[2,2,32,384]{3,2,1,0:T(8,128)(2,1)S(1)}, u32[]{:S(2)}, u32[]{:S(2)}) collective-permute-start(bf16[2,2,32,384]{3,2,1,0:T(8,128)(2,1)S(1)} %get-tuple-element.53), channel_id=1, source_target_pairs={{0,8},{4,12},{8,0},{12,4},{1,9},{5,13},{9,1},{13,5},{2,10},{6,14},... | collective-permute-start | bytes 294920 | tf_op jit(solution)/shard_map/ppermute | solution.py:77
  14.0 1.6 %collective-permute-done.2.refs_2_ = bf16[2,64,384]{2,1,0:T(8,128)(2,1)S(1)} collective-permute-done((bf16[2,64,384]{2,1,0:T(8,128)(2,1)S(1)}, bf16[2,64,384]{2,1,0:T(8,128)(2,1)S(1)}, u32[]{:S(2)}, u32[]{:S(2)}) %collective-permute-start.2) | collective-permute-done | bytes 98336 | tf_op jit(solution)/shard_map/ppermute | solution.py:68
  15.6 2.0 %collective-permute-start.5 = (bf16[2,2,32,384]{3,2,1,0:T(8,128)(2,1)S(1)}, bf16[2,2,32,384]{3,2,1,0:T(8,128)(2,1)S(1)}, u32[]{:S(2)}, u32[]{:S(2)}) collective-permute-start(bf16[2,2,32,384]{3,2,1,0:T(8,128)(2,1)S(1)} %get-tuple-element.54), channel_id=1, source_target_pairs={{0,12},{4,0},{8,4},{12,8},{1,13},{5,1},{9,5},{13,9},{2,14},{6,2},{... | collective-permute-start | bytes 294920 | tf_op jit(solution)/shard_map/ppermute | solution.py:77
  17.6 0.0 collective-permute-done.3.refs_3_
  17.6 1.1 %collective-permute-done.1.refs_1_ = bf16[2,64,384]{2,1,0:T(8,128)(2,1)S(1)} collective-permute-done((bf16[2,64,384]{2,1,0:T(8,128)(2,1)S(1)}, bf16[2,64,384]{2,1,0:T(8,128)(2,1)S(1)}, u32[]{:S(2)}, u32[]{:S(2)}) %collective-permute-start.1) | collective-permute-done | bytes 98336 | tf_op jit(solution)/shard_map/ppermute | solution.py:68
  18.7 0.0 copy-done.3
  18.7 2.8 %shard_map.96 = (bf16[8,64,384]{2,1,0:T(8,128)(2,1)S(1)}, bf16[512,384]{1,0:T(8,128)(2,1)S(1)}, bf16[512,1536]{1,0:T(8,128)(2,1)S(1)}, f32[512,384]{1,0:T(8,128)S(1)}, f32[512,1]{1,0:T(8,128)S(1)}) custom-call(bf16[2,64,384]{2,1,0:T(8,128)(2,1)S(1)} %get-tuple-element.43.refs_0_, bf16[2,64,384]{2,1,0:T(8,128)(2,1)S(1)} %collective-permute-done.1.refs_1_, ...), custom_call_target="tpu_custom_call" | custom-call | tf_op jit(solution)/shard_map/pallas_call | solution.py:31
  21.4 0.0 collective-permute-done.refs_1_
  21.4 1.0 %shard_map.97 = (bf16[256,1536]{1,0:T(8,128)(2,1)S(1)}, f32[16,96,384]{2,1,0:T(8,128)S(1)}) custom-call(bf16[2,2,32,384]{3,2,1,0:T(8,128)(2,1)S(1)} %get-tuple-element.41.refs_0_, bf16[2,2,32,384]{3,2,1,0:T(8,128)(2,1)S(1)} %collective-permute-done.refs_1_, bf16[512,1536]{1,0:T(8,128)(2,1)S(1)} %get-tuple-element.50.refs_2_, ...), custom_call_target="tpu_custom_call" | custom-call | tf_op jit(solution)/shard_map/pallas_call | solution.py:31
  22.5 0.6 %collective-permute-done.4.refs_0_ = bf16[2,2,32,384]{3,2,1,0:T(8,128)(2,1)S(1)} collective-permute-done((bf16[2,2,32,384]{3,2,1,0:T(8,128)(2,1)S(1)}, bf16[2,2,32,384]{3,2,1,0:T(8,128)(2,1)S(1)}, u32[]{:S(2)}, u32[]{:S(2)}) %collective-permute-start.4) | collective-permute-done | bytes 98336 | tf_op jit(solution)/shard_map/ppermute | solution.py:77
  23.1 0.0 collective-permute-done.5.refs_1_
  23.1 1.5 %shard_map.98 = (bf16[256,1536]{1,0:T(8,128)(2,1)S(1)}, f32[8,96,384]{2,1,0:T(8,128)S(1)}, bf16[8,96,384]{2,1,0:T(8,128)(2,1)S(1)}) custom-call(bf16[2,2,32,384]{3,2,1,0:T(8,128)(2,1)S(1)} %collective-permute-done.4.refs_0_, bf16[2,2,32,384]{3,2,1,0:T(8,128)(2,1)S(1)} %collective-permute-done.5.refs_1_, bf16[512,1536]{1,0:T(8,128)(2,1)S(1)} %get-tuple-element.50.refs_2_, ...), custom_call_target="tpu_custom_call" | custom-call | tf_op jit(solution)/shard_map/pallas_call | solution.py:31
  24.6 0.1 collective-permute-start.9
  24.7 1.9 %shard_map.99 = (bf16[2,2,64,384]{3,2,1,0:T(8,128)(2,1)S(1)}, bf16[2,2,64,384]{3,2,1,0:T(8,128)(2,1)S(1)}, bf16[2,2,64,384]{3,2,1,0:T(8,128)(2,1)S(1)}, bf16[2,2,64,384]{3,2,1,0:T(8,128)(2,1)S(1)}) custom-call(bf16[256,1536]{1,0:T(8,128)(2,1)S(1)} %get-tuple-element.52.refs_0_, bf16[256,1536]{1,0:T(8,128)(2,1)S(1)} %get-tuple-element.56.refs_1_, ...), custom_call_target="tpu_custom_call" | custom-call | tf_op jit(solution)/shard_map/pallas_call | solution.py:31
  26.6 0.1 collective-permute-done.9.refs_1_
  26.7 0.0 copy-start
  26.7 0.0 copy-start.1
  26.7 0.0 copy-start.2
  26.7 0.1 shard_map.101
  26.8 2.1 %collective-permute-start.10 = (bf16[4,96,384]{2,1,0:T(8,128)(2,1)S(1)}, bf16[4,96,384]{2,1,0:T(8,128)(2,1)S(1)}, u32[]{:S(2)}, u32[]{:S(2)}) collective-permute-start(bf16[4,96,384]{2,1,0:T(8,128)(2,1)S(1)} %get-tuple-element.69), channel_id=1, source_target_pairs={{0,2},{1,3},{2,0},{3,1},{4,6},{5,7},{6,4},{7,5},{8,10},{9,11},{10,... | collective-permute-start | bytes 884744 | tf_op jit(solution)/shard_map/ppermute | solution.py:425
  28.9 2.3 %collective-permute-start.6 = (bf16[2,2,64,384]{3,2,1,0:T(8,128)(2,1)S(1)}, bf16[2,2,64,384]{3,2,1,0:T(8,128)(2,1)S(1)}, u32[]{:S(2)}, u32[]{:S(2)}) collective-permute-start(bf16[2,2,64,384]{3,2,1,0:T(8,128)(2,1)S(1)} %get-tuple-element.61), channel_id=1, source_target_pairs={{0,4},{4,0},{8,12},{12,8},{1,5},{5,1},{9,13},{13,9},{2,6},{6,2},{1... | collective-permute-start | bytes 589832 | tf_op jit(solution)/shard_map/ppermute | solution.py:68
  31.2 2.7 %collective-permute-start.7 = (bf16[2,2,64,384]{3,2,1,0:T(8,128)(2,1)S(1)}, bf16[2,2,64,384]{3,2,1,0:T(8,128)(2,1)S(1)}, u32[]{:S(2)}, u32[]{:S(2)}) collective-permute-start(bf16[2,2,64,384]{3,2,1,0:T(8,128)(2,1)S(1)} %get-tuple-element.62), channel_id=1, source_target_pairs={{0,8},{4,12},{8,0},{12,4},{1,9},{5,13},{9,1},{13,5},{2,10},{6,14},... | collective-permute-start | bytes 589832 | tf_op jit(solution)/shard_map/ppermute | solution.py:68
  33.9 0.0 collective-permute-start.8
  33.9 2.6 %collective-permute-done.10.refs_1_ = bf16[4,96,384]{2,1,0:T(8,128)(2,1)S(1)} collective-permute-done((bf16[4,96,384]{2,1,0:T(8,128)(2,1)S(1)}, bf16[4,96,384]{2,1,0:T(8,128)(2,1)S(1)}, u32[]{:S(2)}, u32[]{:S(2)}) %collective-permute-start.10) | collective-permute-done | bytes 294944 | tf_op jit(solution)/shard_map/ppermute | solution.py:425
  36.5 0.1 shard_map.102
  36.5 2.4 %collective-permute-start.11 = (bf16[96,384]{1,0:T(8,128)(2,1)S(1)}, bf16[96,384]{1,0:T(8,128)(2,1)S(1)}, u32[]{:S(2)}, u32[]{:S(2)}) collective-permute-start(bf16[96,384]{1,0:T(8,128)(2,1)S(1)} %get-tuple-element.71), channel_id=1, source_target_pairs={{0,4},{4,0},{8,12},{12,8},{1,5},{5,1},{9,13},{13,9},{2,6},{6,2},{1... | collective-permute-start | bytes 221192 | tf_op jit(solution)/shard_map/ppermute | solution.py:430
  38.9 0.1 collective-permute-start.12
  39.0 7.6 %collective-permute-done.11.refs_1_ = bf16[96,384]{1,0:T(8,128)(2,1)S(1)} collective-permute-done((bf16[96,384]{1,0:T(8,128)(2,1)S(1)}, bf16[96,384]{1,0:T(8,128)(2,1)S(1)}, u32[]{:S(2)}, u32[]{:S(2)}) %collective-permute-start.11) | collective-permute-done | bytes 73760 | tf_op jit(solution)/shard_map/ppermute | solution.py:430
  46.5 1.2 %collective-permute-done.12.refs_2_ = bf16[96,384]{1,0:T(8,128)(2,1)S(1)} collective-permute-done((bf16[96,384]{1,0:T(8,128)(2,1)S(1)}, bf16[96,384]{1,0:T(8,128)(2,1)S(1)}, u32[]{:S(2)}, u32[]{:S(2)}) %collective-permute-start.12) | collective-permute-done | bytes 73760 | tf_op jit(solution)/shard_map/ppermute | solution.py:430
  47.8 3.1 %collective-permute-start.13 = (bf16[96,384]{1,0:T(8,128)(2,1)S(1)}, bf16[96,384]{1,0:T(8,128)(2,1)S(1)}, u32[]{:S(2)}, u32[]{:S(2)}) collective-permute-start(bf16[96,384]{1,0:T(8,128)(2,1)S(1)} %get-tuple-element.74), channel_id=1, source_target_pairs={{0,8},{4,12},{8,0},{12,4},{1,9},{5,13},{9,1},{13,5},{2,10},{6,14},... | collective-permute-start | bytes 221192 | tf_op jit(solution)/shard_map/ppermute | solution.py:434
  50.9 0.0 collective-permute-done.6.refs_1_
  50.9 0.0 collective-permute-done.7.refs_2_
  50.9 0.0 collective-permute-done.8.refs_3_
  50.9 0.0 copy-done
  50.9 0.0 copy-done.1
  50.9 0.0 copy-done.2
  50.9 2.9 %shard_map.100 = (bf16[1,2,8,32,384]{4,3,2,1,0:T(8,128)(2,1)}, bf16[1,2,8,32,384]{4,3,2,1,0:T(8,128)(2,1)}) custom-call(bf16[2,2,64,384]{3,2,1,0:T(8,128)(2,1)S(1)} %get-tuple-element.60.refs_0_.refs_2_, bf16[2,2,64,384]{3,2,1,0:T(8,128)(2,1)S(1)} %collective-permute-done.6.refs_1_, bf16[2,2,64,384]{3,2,1,0:T(8,128)(2,1)S(1)} %collective-permute-done.7.refs_2_, ...), custom_call_target="tpu_custom_call" | custom-call | tf_op jit(solution)/shard_map/pallas_call | solution.py:31
  53.9 0.9 %collective-permute-done.13.refs_1_ = bf16[96,384]{1,0:T(8,128)(2,1)S(1)} collective-permute-done((bf16[96,384]{1,0:T(8,128)(2,1)S(1)}, bf16[96,384]{1,0:T(8,128)(2,1)S(1)}, u32[]{:S(2)}, u32[]{:S(2)}) %collective-permute-start.13) | collective-permute-done | bytes 73760 | tf_op jit(solution)/shard_map/ppermute | solution.py:434
  54.8 0.7 %shard_map.104 = f32[96,384]{1,0:T(8,128)} custom-call(f32[96,384]{1,0:T(8,128)S(1)} %get-tuple-element.73.refs_0_, bf16[96,384]{1,0:T(8,128)(2,1)S(1)} %collective-permute-done.13.refs_1_), custom_call_target="tpu_custom_call" | custom-call | tf_op jit(solution)/shard_map/pallas_call | solution.py:31
  (1 shorter events, 0.0 us)
Async XLA Ops:
  3.0 12.6 %collective-permute-start.2 = (bf16[2,64,384]{2,1,0:T(8,128)(2,1)S(1)}, bf16[2,64,384]{2,1,0:T(8,128)(2,1)S(1)}, u32[]{:S(2)}, u32[]{:S(2)}) collective-permute-start(bf16[2,64,384]{2,1,0:T(8,128)(2,1)S(1)} %get-tuple-element.45), channel_id=1, source_target_pairs={{0,8},{4,12},{8,0},{12,4},{1,9},{5,13},{9,1},{13,5},{2,10},{6,14},... | collective-permute-start | bytes 294920 | tf_op jit(solution)/shard_map/ppermute | solution.py:68
  6.9 10.7 %collective-permute-start.3 = (bf16[2,64,384]{2,1,0:T(8,128)(2,1)S(1)}, bf16[2,64,384]{2,1,0:T(8,128)(2,1)S(1)}, u32[]{:S(2)}, u32[]{:S(2)}) collective-permute-start(bf16[2,64,384]{2,1,0:T(8,128)(2,1)S(1)} %get-tuple-element.46), channel_id=1, source_target_pairs={{0,12},{4,8},{8,4},{12,0},{1,13},{5,9},{9,5},{13,1},{2,14},{6,10},... | collective-permute-start | bytes 294920 | tf_op jit(solution)/shard_map/ppermute | solution.py:68
  8.5 10.2 %copy-start.3 = (f32[384]{0:T(512)S(1)}, f32[384]{0:T(512)}, u32[]{:S(2)}) copy-start(f32[384]{0:T(512)} %refs_5_.4) | copy-start | bytes 4612
  10.4 8.3 %collective-permute-start.1 = (bf16[2,64,384]{2,1,0:T(8,128)(2,1)S(1)}, bf16[2,64,384]{2,1,0:T(8,128)(2,1)S(1)}, u32[]{:S(2)}, u32[]{:S(2)}) collective-permute-start(bf16[2,64,384]{2,1,0:T(8,128)(2,1)S(1)} %get-tuple-element.44), channel_id=1, source_target_pairs={{0,4},{4,0},{8,12},{12,8},{1,5},{5,1},{9,13},{13,9},{2,6},{6,2},{1... | collective-permute-start | bytes 294920 | tf_op jit(solution)/shard_map/ppermute | solution.py:68
  10.5 10.9 %collective-permute-start = (bf16[2,2,32,384]{3,2,1,0:T(8,128)(2,1)S(1)}, bf16[2,2,32,384]{3,2,1,0:T(8,128)(2,1)S(1)}, u32[]{:S(2)}, u32[]{:S(2)}) collective-permute-start(bf16[2,2,32,384]{3,2,1,0:T(8,128)(2,1)S(1)} %get-tuple-element.42), channel_id=1, source_target_pairs={{0,4},{4,8},{8,12},{12,0},{1,5},{5,9},{9,13},{13,1},{2,6},{6,10},{... | collective-permute-start | bytes 294920 | tf_op jit(solution)/shard_map/ppermute | solution.py:77
  12.5 10.6 %collective-permute-start.4 = (bf16[2,2,32,384]{3,2,1,0:T(8,128)(2,1)S(1)}, bf16[2,2,32,384]{3,2,1,0:T(8,128)(2,1)S(1)}, u32[]{:S(2)}, u32[]{:S(2)}) collective-permute-start(bf16[2,2,32,384]{3,2,1,0:T(8,128)(2,1)S(1)} %get-tuple-element.53), channel_id=1, source_target_pairs={{0,8},{4,12},{8,0},{12,4},{1,9},{5,13},{9,1},{13,5},{2,10},{6,14},... | collective-permute-start | bytes 294920 | tf_op jit(solution)/shard_map/ppermute | solution.py:77
  15.6 7.5 %collective-permute-start.5 = (bf16[2,2,32,384]{3,2,1,0:T(8,128)(2,1)S(1)}, bf16[2,2,32,384]{3,2,1,0:T(8,128)(2,1)S(1)}, u32[]{:S(2)}, u32[]{:S(2)}) collective-permute-start(bf16[2,2,32,384]{3,2,1,0:T(8,128)(2,1)S(1)} %get-tuple-element.54), channel_id=1, source_target_pairs={{0,12},{4,0},{8,4},{12,8},{1,13},{5,1},{9,5},{13,9},{2,14},{6,2},{... | collective-permute-start | bytes 294920 | tf_op jit(solution)/shard_map/ppermute | solution.py:77
  24.6 2.1 %collective-permute-start.9 = (bf16[8,96,384]{2,1,0:T(8,128)(2,1)S(1)}, bf16[8,96,384]{2,1,0:T(8,128)(2,1)S(1)}, u32[]{:S(2)}, u32[]{:S(2)}) collective-permute-start(bf16[8,96,384]{2,1,0:T(8,128)(2,1)S(1)} %get-tuple-element.67), channel_id=1, source_target_pairs={{0,1},{1,0},{2,3},{3,2},{4,5},{5,4},{6,7},{7,6},{8,9},{9,8},{10,11... | collective-permute-start | bytes 1769480 | tf_op jit(solution)/shard_map/ppermute | solution.py:421
  26.7 24.2 %copy-start = (bf16[1,2,8,32,384]{4,3,2,1,0:T(8,128)(2,1)S(1)}, bf16[1,2,8,32,384]{4,3,2,1,0:T(8,128)(2,1)}, u32[]{:S(2)}) copy-start(bf16[1,2,8,32,384]{4,3,2,1,0:T(8,128)(2,1)} %refs_5_.5) | copy-start | bytes 1179652
  26.7 24.2 %copy-start.1 = (bf16[1,2,8,32,384]{4,3,2,1,0:T(8,128)(2,1)S(1)}, bf16[1,2,8,32,384]{4,3,2,1,0:T(8,128)(2,1)}, u32[]{:S(2)}) copy-start(bf16[1,2,8,32,384]{4,3,2,1,0:T(8,128)(2,1)} %refs_4_.1) | copy-start | bytes 1179652
  26.7 24.2 %copy-start.2 = (f32[7,7,384]{2,1,0:T(8,128)S(1)}, f32[7,7,384]{2,1,0:T(8,128)}, u32[]{:S(2)}) copy-start(f32[7,7,384]{2,1,0:T(8,128)} %refs_6_.1) | copy-start | bytes 225796
  26.8 9.7 %collective-permute-start.10 = (bf16[4,96,384]{2,1,0:T(8,128)(2,1)S(1)}, bf16[4,96,384]{2,1,0:T(8,128)(2,1)S(1)}, u32[]{:S(2)}, u32[]{:S(2)}) collective-permute-start(bf16[4,96,384]{2,1,0:T(8,128)(2,1)S(1)} %get-tuple-element.69), channel_id=1, source_target_pairs={{0,2},{1,3},{2,0},{3,1},{4,6},{5,7},{6,4},{7,5},{8,10},{9,11},{10,... | collective-permute-start | bytes 884744 | tf_op jit(solution)/shard_map/ppermute | solution.py:425
  28.9 22.0 %collective-permute-start.6 = (bf16[2,2,64,384]{3,2,1,0:T(8,128)(2,1)S(1)}, bf16[2,2,64,384]{3,2,1,0:T(8,128)(2,1)S(1)}, u32[]{:S(2)}, u32[]{:S(2)}) collective-permute-start(bf16[2,2,64,384]{3,2,1,0:T(8,128)(2,1)S(1)} %get-tuple-element.61), channel_id=1, source_target_pairs={{0,4},{4,0},{8,12},{12,8},{1,5},{5,1},{9,13},{13,9},{2,6},{6,2},{1... | collective-permute-start | bytes 589832 | tf_op jit(solution)/shard_map/ppermute | solution.py:68
  31.2 19.7 %collective-permute-start.7 = (bf16[2,2,64,384]{3,2,1,0:T(8,128)(2,1)S(1)}, bf16[2,2,64,384]{3,2,1,0:T(8,128)(2,1)S(1)}, u32[]{:S(2)}, u32[]{:S(2)}) collective-permute-start(bf16[2,2,64,384]{3,2,1,0:T(8,128)(2,1)S(1)} %get-tuple-element.62), channel_id=1, source_target_pairs={{0,8},{4,12},{8,0},{12,4},{1,9},{5,13},{9,1},{13,5},{2,10},{6,14},... | collective-permute-start | bytes 589832 | tf_op jit(solution)/shard_map/ppermute | solution.py:68
  33.9 17.0 %collective-permute-start.8 = (bf16[2,2,64,384]{3,2,1,0:T(8,128)(2,1)S(1)}, bf16[2,2,64,384]{3,2,1,0:T(8,128)(2,1)S(1)}, u32[]{:S(2)}, u32[]{:S(2)}) collective-permute-start(bf16[2,2,64,384]{3,2,1,0:T(8,128)(2,1)S(1)} %get-tuple-element.63), channel_id=1, source_target_pairs={{0,12},{4,8},{8,4},{12,0},{1,13},{5,9},{9,5},{13,1},{2,14},{6,10},... | collective-permute-start | bytes 589832 | tf_op jit(solution)/shard_map/ppermute | solution.py:68
  36.5 10.0 %collective-permute-start.11 = (bf16[96,384]{1,0:T(8,128)(2,1)S(1)}, bf16[96,384]{1,0:T(8,128)(2,1)S(1)}, u32[]{:S(2)}, u32[]{:S(2)}) collective-permute-start(bf16[96,384]{1,0:T(8,128)(2,1)S(1)} %get-tuple-element.71), channel_id=1, source_target_pairs={{0,4},{4,0},{8,12},{12,8},{1,5},{5,1},{9,13},{13,9},{2,6},{6,2},{1... | collective-permute-start | bytes 221192 | tf_op jit(solution)/shard_map/ppermute | solution.py:430
  38.9 8.9 %collective-permute-start.12 = (bf16[96,384]{1,0:T(8,128)(2,1)S(1)}, bf16[96,384]{1,0:T(8,128)(2,1)S(1)}, u32[]{:S(2)}, u32[]{:S(2)}) collective-permute-start(bf16[96,384]{1,0:T(8,128)(2,1)S(1)} %get-tuple-element.72), channel_id=1, source_target_pairs={{0,4},{4,0},{8,12},{12,8},{1,5},{5,1},{9,13},{13,9},{2,6},{6,2},{1... | collective-permute-start | bytes 221192 | tf_op jit(solution)/shard_map/ppermute | solution.py:430
  47.8 7.0 %collective-permute-start.13 = (bf16[96,384]{1,0:T(8,128)(2,1)S(1)}, bf16[96,384]{1,0:T(8,128)(2,1)S(1)}, u32[]{:S(2)}, u32[]{:S(2)}) collective-permute-start(bf16[96,384]{1,0:T(8,128)(2,1)S(1)} %get-tuple-element.74), channel_id=1, source_target_pairs={{0,8},{4,12},{8,0},{12,4},{1,9},{5,13},{9,1},{13,5},{2,10},{6,14},... | collective-permute-start | bytes 221192 | tf_op jit(solution)/shard_map/ppermute | solution.py:434

commit v6 on v5

--- a/solution.py
+++ b/solution.py
@@ -336,24 +336,21 @@
     )
     steep = jnp.concatenate([slope[pl.ds(source, rows), :] for source in sources], axis=0)
     result = (d_hidden * steep.astype(F32)).astype(BF16)
-    if not with_grad:
+    if not (with_grad and final):
         refs[-1][...] = result
-        return
-    inputs = jnp.concatenate([scaled[pl.ds(source, rows), :] for source in sources], axis=0)
-    share = lax.dot_general(result, inputs, (((0,), (0,)), ((), ())), preferred_element_type=F32)
-    if not final:
-        d_pre, full = refs
-        d_pre[...] = result
-        full[...] = share.reshape(full.shape)
         return
     before, d_pre, keep, send, full = refs
     d_pre[...] = result
+    order = [step for step in range(count) if step not in steps] + list(steps)
+    sources = [pl.multiple_of(slot_from(step, count) * rows, rows) for step in order]
+    inputs = jnp.concatenate([scaled[pl.ds(source, rows), :] for source in sources], axis=0)
+    both = jnp.concatenate([before[...], result], axis=0)
+    share = lax.dot_general(both, inputs, (((0,), (0,)), ((), ())), preferred_element_type=F32)
     full[...] = share.reshape(full.shape)
     core = lax.rem(lax.axis_index("dp"), 2)
     for pair in range(full.shape[0] // 2):
-        mine, other = 2 * pair + core, 2 * pair + 1 - core
-        keep[pair] = full[mine] + before[mine]
-        send[pair] = (full[other] + before[other]).astype(BF16)
+        keep[pair] = full[2 * pair + core]
+        send[pair] = full[2 * pair + 1 - core].astype(BF16)
 
 
 def token_bwd(count, groups, *refs):
@@ -544,8 +541,6 @@
         results = [struct((rows, hid), BF16)]
         if staged and final:
             results += [struct(half, F32), struct(half, BF16)]
-        elif staged:
-            results += [struct(whole, F32)]
         part, *shares = call(
             functools.partial(hidden_bwd, count, steps, staged, final),
             results,
@@ -554,7 +549,7 @@
             slope,
             w_project,
             scaled,
-            *shares,
+            *parts,
         )
         parts.append(part)
     outs = call(

time: 55.7 us -> 56 us (level)
  starting transfers between devices: 23.7 us -> 25.1 us
  waiting for transfers between devices: 15.7 us -> 14.5 us
    ppermute x6, waiting for transfers between devices: 2.68 us -> 0.79 us  [swap(): got.append(lax.ppermute(pieces[step], 'tm', pairs))]
    ppermute x3, starting transfers between devices: 5.5 us -> 6.49 us  [exchange(): got.append(lax.ppermute(pieces[step], 'tm', pairs))]
    ppermute x3, waiting for transfers between devices: 0.62 us -> 1.53 us  [exchange(): got.append(lax.ppermute(pieces[step], 'tm', pairs))]
where the time goes in v6:
time: 56 us; the launch traced here: 55.8 us
  starting transfers between devices  25.1 us (45%)
  Pallas kernels  15.5 us (28%)
  waiting for transfers between devices  14.5 us (26%)
  between operations  0.75 us (1%)
    pallas_call x11, Pallas kernels, call(): pl.pallas_call(kernel, out_shape=tuple(outs), in_specs=specs, out_specs=t...  15.5 us
    ppermute x6, starting transfers between devices, swap(): got.append(lax.ppermute(pieces[step], 'tm', pairs))  10.4 us
    ppermute x2, waiting for transfers between devices, scatter_grad(): lax.ppermute(send, 'tm', [(i, i ^ 1) for i in range(4)])  8.48 us
    ppermute x3, starting transfers between devices, exchange(): got.append(lax.ppermute(pieces[step], 'tm', pairs))  6.49 us
    ppermute x1, starting transfers between devices, scatter_grad(): got = lax.ppermute(send, 'tm', [(i, i ^ 2) for i in range(4)])  3.61 us
    ppermute x1, waiting for transfers between devices, scatter_grad(): got = lax.ppermute(send, 'dp', [(i, i ^ 2) for i in range(4)])  2.73 us
    ppermute x1, starting transfers between devices, scatter_grad(): got = lax.ppermute(send, 'dp', [(i, i ^ 2) for i in range(4)])  2.4 us
    ppermute x2, starting transfers between devices, scatter_grad(): lax.ppermute(send, 'tm', [(i, i ^ 1) for i in range(4)])  2.09 us
  transfers between devices with their start and end apart: 14, of which 8 were waited for; matrix products, arithmetic and copies ran while one was open for 0% of the time, Pallas kernels for 19%

profile of v6, /device:TPU:0, one launch (start us, length us, event | category | flops | bytes accessed | tf_op | source)
XLA Modules:
  0.0 55.8 jit_solution(14226203074921139954)
XLA Ops:
  0.6 2.6 %shard_map.94 = (bf16[2,64,384]{2,1,0:T(8,128)(2,1)S(1)}, bf16[2,64,384]{2,1,0:T(8,128)(2,1)S(1)}, f32[3,2,8,48,128]{4,3,2,1,0:T(8,128)S(1)}, f32[7,7,384]{2,1,0:T(8,128)S(1)}) custom-call(bf16[1,2,8,32,384]{4,3,2,1,0:T(8,128)(2,1)} %refs_4_.1, f32[7,7,384]{2,1,0:T(8,128)} %refs_6_.1), custom_call_target="tpu_custom_call" | custom-call | tf_op jit(solution)/shard_map/pallas_call | solution.py:31
  3.2 3.8 %collective-permute-start.2 = (bf16[2,64,384]{2,1,0:T(8,128)(2,1)S(1)}, bf16[2,64,384]{2,1,0:T(8,128)(2,1)S(1)}, u32[]{:S(2)}, u32[]{:S(2)}) collective-permute-start(bf16[2,64,384]{2,1,0:T(8,128)(2,1)S(1)} %get-tuple-element.43), channel_id=1, source_target_pairs={{0,8},{4,12},{8,0},{12,4},{1,9},{5,13},{9,1},{13,5},{2,10},{6,14},... | collective-permute-start | bytes 294920 | tf_op jit(solution)/shard_map/ppermute | solution.py:68
  7.0 1.7 %collective-permute-start.3 = (bf16[2,64,384]{2,1,0:T(8,128)(2,1)S(1)}, bf16[2,64,384]{2,1,0:T(8,128)(2,1)S(1)}, u32[]{:S(2)}, u32[]{:S(2)}) collective-permute-start(bf16[2,64,384]{2,1,0:T(8,128)(2,1)S(1)} %get-tuple-element.44), channel_id=1, source_target_pairs={{0,12},{4,8},{8,4},{12,0},{1,13},{5,9},{9,5},{13,1},{2,14},{6,10},... | collective-permute-start | bytes 294920 | tf_op jit(solution)/shard_map/ppermute | solution.py:68
  8.7 0.0 copy-start.3
  8.7 1.9 %shard_map.95 = (bf16[2,64,384]{2,1,0:T(8,128)(2,1)S(1)}, bf16[2,64,384]{2,1,0:T(8,128)(2,1)S(1)}, bf16[2,2,32,384]{3,2,1,0:T(8,128)(2,1)S(1)}, bf16[2,2,32,384]...) custom-call(bf16[1,2,8,32,384]{4,3,2,1,0:T(8,128)(2,1)} %refs_5_.5, ...), custom_call_target="tpu_custom_call" | custom-call | tf_op jit(solution)/shard_map/pallas_call | solution.py:31
  10.6 0.1 collective-permute-start.1
  10.7 2.0 %collective-permute-start = (bf16[2,2,32,384]{3,2,1,0:T(8,128)(2,1)S(1)}, bf16[2,2,32,384]{3,2,1,0:T(8,128)(2,1)S(1)}, u32[]{:S(2)}, u32[]{:S(2)}) collective-permute-start(bf16[2,2,32,384]{3,2,1,0:T(8,128)(2,1)S(1)} %get-tuple-element.40), channel_id=1, source_target_pairs={{0,4},{4,8},{8,12},{12,0},{1,5},{5,9},{9,13},{13,1},{2,6},{6,10},{... | collective-permute-start | bytes 294920 | tf_op jit(solution)/shard_map/ppermute | solution.py:77
  12.7 1.4 %collective-permute-start.4 = (bf16[2,2,32,384]{3,2,1,0:T(8,128)(2,1)S(1)}, bf16[2,2,32,384]{3,2,1,0:T(8,128)(2,1)S(1)}, u32[]{:S(2)}, u32[]{:S(2)}) collective-permute-start(bf16[2,2,32,384]{3,2,1,0:T(8,128)(2,1)S(1)} %get-tuple-element.50), channel_id=1, source_target_pairs={{0,8},{4,12},{8,0},{12,4},{1,9},{5,13},{9,1},{13,5},{2,10},{6,14},... | collective-permute-start | bytes 294920 | tf_op jit(solution)/shard_map/ppermute | solution.py:77
  14.0 0.5 collective-permute-done.2.refs_2_
  14.5 3.1 %collective-permute-start.5 = (bf16[2,2,32,384]{3,2,1,0:T(8,128)(2,1)S(1)}, bf16[2,2,32,384]{3,2,1,0:T(8,128)(2,1)S(1)}, u32[]{:S(2)}, u32[]{:S(2)}) collective-permute-start(bf16[2,2,32,384]{3,2,1,0:T(8,128)(2,1)S(1)} %get-tuple-element.51), channel_id=1, source_target_pairs={{0,12},{4,0},{8,4},{12,8},{1,13},{5,1},{9,5},{13,9},{2,14},{6,2},{... | collective-permute-start | bytes 294920 | tf_op jit(solution)/shard_map/ppermute | solution.py:77
  17.7 0.0 collective-permute-done.3.refs_3_
  17.7 0.3 collective-permute-done.1.refs_1_
  18.0 0.0 copy-done.3
  18.0 2.8 %shard_map.96 = (bf16[8,64,384]{2,1,0:T(8,128)(2,1)S(1)}, bf16[512,384]{1,0:T(8,128)(2,1)S(1)}, bf16[512,1536]{1,0:T(8,128)(2,1)S(1)}, f32[512,384]{1,0:T(8,128)S(1)}, f32[512,1]{1,0:T(8,128)S(1)}) custom-call(bf16[2,64,384]{2,1,0:T(8,128)(2,1)S(1)} %get-tuple-element.41.refs_0_, bf16[2,64,384]{2,1,0:T(8,128)(2,1)S(1)} %collective-permute-done.1.refs_1_, ...), custom_call_target="tpu_custom_call" | custom-call | tf_op jit(solution)/shard_map/pallas_call | solution.py:31
  20.8 0.0 collective-permute-done.refs_1_
  20.8 0.6 %shard_map.97.refs_5_.refs_0_ = bf16[256,1536]{1,0:T(8,128)(2,1)S(1)} custom-call(bf16[2,2,32,384]{3,2,1,0:T(8,128)(2,1)S(1)} %get-tuple-element.39.refs_0_, bf16[2,2,32,384]{3,2,1,0:T(8,128)(2,1)S(1)} %collective-permute-done.refs_1_, bf16[512,1536]{1,0:T(8,128)(2,1)S(1)} %get-tuple-element.48.refs_2_, ...), custom_call_target="tpu_custom_call" | custom-call | tf_op jit(solution)/shard_map/pallas_call | solution.py:31
  21.4 1.5 %collective-permute-done.4.refs_0_ = bf16[2,2,32,384]{3,2,1,0:T(8,128)(2,1)S(1)} collective-permute-done((bf16[2,2,32,384]{3,2,1,0:T(8,128)(2,1)S(1)}, bf16[2,2,32,384]{3,2,1,0:T(8,128)(2,1)S(1)}, u32[]{:S(2)}, u32[]{:S(2)}) %collective-permute-start.4) | collective-permute-done | bytes 98336 | tf_op jit(solution)/shard_map/ppermute | solution.py:77
  22.9 0.0 collective-permute-done.5.refs_1_
  22.9 1.8 %shard_map.98 = (bf16[256,1536]{1,0:T(8,128)(2,1)S(1)}, f32[8,96,384]{2,1,0:T(8,128)S(1)}, bf16[8,96,384]{2,1,0:T(8,128)(2,1)S(1)}) custom-call(bf16[2,2,32,384]{3,2,1,0:T(8,128)(2,1)S(1)} %collective-permute-done.4.refs_0_, bf16[2,2,32,384]{3,2,1,0:T(8,128)(2,1)S(1)} %collective-permute-done.5.refs_1_, bf16[512,1536]{1,0:T(8,128)(2,1)S(1)} %get-tuple-element.48.refs_2_, ...), custom_call_target="tpu_custom_call" | custom-call | tf_op jit(solution)/shard_map/pallas_call | solution.py:31
  24.7 0.1 collective-permute-start.9
  24.8 1.9 %shard_map.99 = (bf16[2,2,64,384]{3,2,1,0:T(8,128)(2,1)S(1)}, bf16[2,2,64,384]{3,2,1,0:T(8,128)(2,1)S(1)}, bf16[2,2,64,384]{3,2,1,0:T(8,128)(2,1)S(1)}, bf16[2,2,64,384]{3,2,1,0:T(8,128)(2,1)S(1)}) custom-call(bf16[256,1536]{1,0:T(8,128)(2,1)S(1)} %shard_map.97.refs_5_.refs_0_, bf16[256,1536]{1,0:T(8,128)(2,1)S(1)} %get-tuple-element.52.refs_1_, ...), custom_call_target="tpu_custom_call" | custom-call | tf_op jit(solution)/shard_map/pallas_call | solution.py:31
  26.7 0.1 collective-permute-done.9.refs_1_
  26.8 0.0 copy-start
  26.8 0.0 copy-start.1
  26.8 0.0 copy-start.2
  26.8 0.1 shard_map.101
  26.9 2.4 %collective-permute-start.10 = (bf16[4,96,384]{2,1,0:T(8,128)(2,1)S(1)}, bf16[4,96,384]{2,1,0:T(8,128)(2,1)S(1)}, u32[]{:S(2)}, u32[]{:S(2)}) collective-permute-start(bf16[4,96,384]{2,1,0:T(8,128)(2,1)S(1)} %get-tuple-element.65), channel_id=1, source_target_pairs={{0,2},{1,3},{2,0},{3,1},{4,6},{5,7},{6,4},{7,5},{8,10},{9,11},{10,... | collective-permute-start | bytes 884744 | tf_op jit(solution)/shard_map/ppermute | solution.py:422
  29.3 1.9 %collective-permute-start.6 = (bf16[2,2,64,384]{3,2,1,0:T(8,128)(2,1)S(1)}, bf16[2,2,64,384]{3,2,1,0:T(8,128)(2,1)S(1)}, u32[]{:S(2)}, u32[]{:S(2)}) collective-permute-start(bf16[2,2,64,384]{3,2,1,0:T(8,128)(2,1)S(1)} %get-tuple-element.57), channel_id=1, source_target_pairs={{0,4},{4,0},{8,12},{12,8},{1,5},{5,1},{9,13},{13,9},{2,6},{6,2},{1... | collective-permute-start | bytes 589832 | tf_op jit(solution)/shard_map/ppermute | solution.py:68
  31.3 3.0 %collective-permute-start.7 = (bf16[2,2,64,384]{3,2,1,0:T(8,128)(2,1)S(1)}, bf16[2,2,64,384]{3,2,1,0:T(8,128)(2,1)S(1)}, u32[]{:S(2)}, u32[]{:S(2)}) collective-permute-start(bf16[2,2,64,384]{3,2,1,0:T(8,128)(2,1)S(1)} %get-tuple-element.58), channel_id=1, source_target_pairs={{0,8},{4,12},{8,0},{12,4},{1,9},{5,13},{9,1},{13,5},{2,10},{6,14},... | collective-permute-start | bytes 589832 | tf_op jit(solution)/shard_map/ppermute | solution.py:68
  34.2 0.0 collective-permute-start.8
  34.2 2.7 %collective-permute-done.10.refs_1_ = bf16[4,96,384]{2,1,0:T(8,128)(2,1)S(1)} collective-permute-done((bf16[4,96,384]{2,1,0:T(8,128)(2,1)S(1)}, bf16[4,96,384]{2,1,0:T(8,128)(2,1)S(1)}, u32[]{:S(2)}, u32[]{:S(2)}) %collective-permute-start.10) | collective-permute-done | bytes 294944 | tf_op jit(solution)/shard_map/ppermute | solution.py:422
  37.0 0.1 shard_map.102
  37.0 2.0 %collective-permute-start.11 = (bf16[96,384]{1,0:T(8,128)(2,1)S(1)}, bf16[96,384]{1,0:T(8,128)(2,1)S(1)}, u32[]{:S(2)}, u32[]{:S(2)}) collective-permute-start(bf16[96,384]{1,0:T(8,128)(2,1)S(1)} %get-tuple-element.67), channel_id=1, source_target_pairs={{0,4},{4,0},{8,12},{12,8},{1,5},{5,1},{9,13},{13,9},{2,6},{6,2},{1... | collective-permute-start | bytes 221192 | tf_op jit(solution)/shard_map/ppermute | solution.py:427
  39.0 0.1 collective-permute-start.12
  39.1 7.5 %collective-permute-done.11.refs_1_ = bf16[96,384]{1,0:T(8,128)(2,1)S(1)} collective-permute-done((bf16[96,384]{1,0:T(8,128)(2,1)S(1)}, bf16[96,384]{1,0:T(8,128)(2,1)S(1)}, u32[]{:S(2)}, u32[]{:S(2)}) %collective-permute-start.11) | collective-permute-done | bytes 73760 | tf_op jit(solution)/shard_map/ppermute | solution.py:427
  46.6 1.0 %collective-permute-done.12.refs_2_ = bf16[96,384]{1,0:T(8,128)(2,1)S(1)} collective-permute-done((bf16[96,384]{1,0:T(8,128)(2,1)S(1)}, bf16[96,384]{1,0:T(8,128)(2,1)S(1)}, u32[]{:S(2)}, u32[]{:S(2)}) %collective-permute-start.12) | collective-permute-done | bytes 73760 | tf_op jit(solution)/shard_map/ppermute | solution.py:427
  47.6 3.6 %collective-permute-start.13 = (bf16[96,384]{1,0:T(8,128)(2,1)S(1)}, bf16[96,384]{1,0:T(8,128)(2,1)S(1)}, u32[]{:S(2)}, u32[]{:S(2)}) collective-permute-start(bf16[96,384]{1,0:T(8,128)(2,1)S(1)} %get-tuple-element.70), channel_id=1, source_target_pairs={{0,8},{4,12},{8,0},{12,4},{1,9},{5,13},{9,1},{13,5},{2,10},{6,14},... | collective-permute-start | bytes 221192 | tf_op jit(solution)/shard_map/ppermute | solution.py:431
  51.2 0.0 collective-permute-done.6.refs_1_
  51.2 0.0 collective-permute-done.7.refs_2_
  51.3 0.0 collective-permute-done.8.refs_3_
  51.3 0.0 copy-done
  51.3 0.0 copy-done.1
  51.3 0.0 copy-done.2
  51.3 3.0 %shard_map.100 = (bf16[1,2,8,32,384]{4,3,2,1,0:T(8,128)(2,1)}, bf16[1,2,8,32,384]{4,3,2,1,0:T(8,128)(2,1)}) custom-call(bf16[2,2,64,384]{3,2,1,0:T(8,128)(2,1)S(1)} %get-tuple-element.56.refs_0_.refs_2_, bf16[2,2,64,384]{3,2,1,0:T(8,128)(2,1)S(1)} %collective-permute-done.6.refs_1_, bf16[2,2,64,384]{3,2,1,0:T(8,128)(2,1)S(1)} %collective-permute-done.7.refs_2_, ...), custom_call_target="tpu_custom_call" | custom-call | tf_op jit(solution)/shard_map/pallas_call | solution.py:31
  54.3 0.9 %collective-permute-done.13.refs_1_ = bf16[96,384]{1,0:T(8,128)(2,1)S(1)} collective-permute-done((bf16[96,384]{1,0:T(8,128)(2,1)S(1)}, bf16[96,384]{1,0:T(8,128)(2,1)S(1)}, u32[]{:S(2)}, u32[]{:S(2)}) %collective-permute-start.13) | collective-permute-done | bytes 73760 | tf_op jit(solution)/shard_map/ppermute | solution.py:431
  55.2 0.7 %shard_map.104 = f32[96,384]{1,0:T(8,128)} custom-call(f32[96,384]{1,0:T(8,128)S(1)} %get-tuple-element.69.refs_0_, bf16[96,384]{1,0:T(8,128)(2,1)S(1)} %collective-permute-done.13.refs_1_), custom_call_target="tpu_custom_call" | custom-call | tf_op jit(solution)/shard_map/pallas_call | solution.py:31
  (1 shorter events, 0.0 us)
Async XLA Ops:
  3.2 11.3 %collective-permute-start.2 = (bf16[2,64,384]{2,1,0:T(8,128)(2,1)S(1)}, bf16[2,64,384]{2,1,0:T(8,128)(2,1)S(1)}, u32[]{:S(2)}, u32[]{:S(2)}) collective-permute-start(bf16[2,64,384]{2,1,0:T(8,128)(2,1)S(1)} %get-tuple-element.43), channel_id=1, source_target_pairs={{0,8},{4,12},{8,0},{12,4},{1,9},{5,13},{9,1},{13,5},{2,10},{6,14},... | collective-permute-start | bytes 294920 | tf_op jit(solution)/shard_map/ppermute | solution.py:68
  7.0 10.7 %collective-permute-start.3 = (bf16[2,64,384]{2,1,0:T(8,128)(2,1)S(1)}, bf16[2,64,384]{2,1,0:T(8,128)(2,1)S(1)}, u32[]{:S(2)}, u32[]{:S(2)}) collective-permute-start(bf16[2,64,384]{2,1,0:T(8,128)(2,1)S(1)} %get-tuple-element.44), channel_id=1, source_target_pairs={{0,12},{4,8},{8,4},{12,0},{1,13},{5,9},{9,5},{13,1},{2,14},{6,10},... | collective-permute-start | bytes 294920 | tf_op jit(solution)/shard_map/ppermute | solution.py:68
  8.7 9.3 %copy-start.3 = (f32[384]{0:T(512)S(1)}, f32[384]{0:T(512)}, u32[]{:S(2)}) copy-start(f32[384]{0:T(512)} %refs_5_.4) | copy-start | bytes 4612
  10.6 7.4 %collective-permute-start.1 = (bf16[2,64,384]{2,1,0:T(8,128)(2,1)S(1)}, bf16[2,64,384]{2,1,0:T(8,128)(2,1)S(1)}, u32[]{:S(2)}, u32[]{:S(2)}) collective-permute-start(bf16[2,64,384]{2,1,0:T(8,128)(2,1)S(1)} %get-tuple-element.42), channel_id=1, source_target_pairs={{0,4},{4,0},{8,12},{12,8},{1,5},{5,1},{9,13},{13,9},{2,6},{6,2},{1... | collective-permute-start | bytes 294920 | tf_op jit(solution)/shard_map/ppermute | solution.py:68
  10.7 10.1 %collective-permute-start = (bf16[2,2,32,384]{3,2,1,0:T(8,128)(2,1)S(1)}, bf16[2,2,32,384]{3,2,1,0:T(8,128)(2,1)S(1)}, u32[]{:S(2)}, u32[]{:S(2)}) collective-permute-start(bf16[2,2,32,384]{3,2,1,0:T(8,128)(2,1)S(1)} %get-tuple-element.40), channel_id=1, source_target_pairs={{0,4},{4,8},{8,12},{12,0},{1,5},{5,9},{9,13},{13,1},{2,6},{6,10},{... | collective-permute-start | bytes 294920 | tf_op jit(solution)/shard_map/ppermute | solution.py:77
  12.7 10.3 %collective-permute-start.4 = (bf16[2,2,32,384]{3,2,1,0:T(8,128)(2,1)S(1)}, bf16[2,2,32,384]{3,2,1,0:T(8,128)(2,1)S(1)}, u32[]{:S(2)}, u32[]{:S(2)}) collective-permute-start(bf16[2,2,32,384]{3,2,1,0:T(8,128)(2,1)S(1)} %get-tuple-element.50), channel_id=1, source_target_pairs={{0,8},{4,12},{8,0},{12,4},{1,9},{5,13},{9,1},{13,5},{2,10},{6,14},... | collective-permute-start | bytes 294920 | tf_op jit(solution)/shard_map/ppermute | solution.py:77
  14.5 8.4 %collective-permute-start.5 = (bf16[2,2,32,384]{3,2,1,0:T(8,128)(2,1)S(1)}, bf16[2,2,32,384]{3,2,1,0:T(8,128)(2,1)S(1)}, u32[]{:S(2)}, u32[]{:S(2)}) collective-permute-start(bf16[2,2,32,384]{3,2,1,0:T(8,128)(2,1)S(1)} %get-tuple-element.51), channel_id=1, source_target_pairs={{0,12},{4,0},{8,4},{12,8},{1,13},{5,1},{9,5},{13,9},{2,14},{6,2},{... | collective-permute-start | bytes 294920 | tf_op jit(solution)/shard_map/ppermute | solution.py:77
  24.7 2.1 %collective-permute-start.9 = (bf16[8,96,384]{2,1,0:T(8,128)(2,1)S(1)}, bf16[8,96,384]{2,1,0:T(8,128)(2,1)S(1)}, u32[]{:S(2)}, u32[]{:S(2)}) collective-permute-start(bf16[8,96,384]{2,1,0:T(8,128)(2,1)S(1)} %get-tuple-element.63), channel_id=1, source_target_pairs={{0,1},{1,0},{2,3},{3,2},{4,5},{5,4},{6,7},{7,6},{8,9},{9,8},{10,11... | collective-permute-start | bytes 1769480 | tf_op jit(solution)/shard_map/ppermute | solution.py:418
  26.8 24.5 %copy-start = (bf16[1,2,8,32,384]{4,3,2,1,0:T(8,128)(2,1)S(1)}, bf16[1,2,8,32,384]{4,3,2,1,0:T(8,128)(2,1)}, u32[]{:S(2)}) copy-start(bf16[1,2,8,32,384]{4,3,2,1,0:T(8,128)(2,1)} %refs_5_.5) | copy-start | bytes 1179652
  26.8 24.5 %copy-start.1 = (bf16[1,2,8,32,384]{4,3,2,1,0:T(8,128)(2,1)S(1)}, bf16[1,2,8,32,384]{4,3,2,1,0:T(8,128)(2,1)}, u32[]{:S(2)}) copy-start(bf16[1,2,8,32,384]{4,3,2,1,0:T(8,128)(2,1)} %refs_4_.1) | copy-start | bytes 1179652
  26.8 24.5 %copy-start.2 = (f32[7,7,384]{2,1,0:T(8,128)S(1)}, f32[7,7,384]{2,1,0:T(8,128)}, u32[]{:S(2)}) copy-start(f32[7,7,384]{2,1,0:T(8,128)} %refs_6_.1) | copy-start | bytes 225796
  26.9 10.1 %collective-permute-start.10 = (bf16[4,96,384]{2,1,0:T(8,128)(2,1)S(1)}, bf16[4,96,384]{2,1,0:T(8,128)(2,1)S(1)}, u32[]{:S(2)}, u32[]{:S(2)}) collective-permute-start(bf16[4,96,384]{2,1,0:T(8,128)(2,1)S(1)} %get-tuple-element.65), channel_id=1, source_target_pairs={{0,2},{1,3},{2,0},{3,1},{4,6},{5,7},{6,4},{7,5},{8,10},{9,11},{10,... | collective-permute-start | bytes 884744 | tf_op jit(solution)/shard_map/ppermute | solution.py:422
  29.3 21.9 %collective-permute-start.6 = (bf16[2,2,64,384]{3,2,1,0:T(8,128)(2,1)S(1)}, bf16[2,2,64,384]{3,2,1,0:T(8,128)(2,1)S(1)}, u32[]{:S(2)}, u32[]{:S(2)}) collective-permute-start(bf16[2,2,64,384]{3,2,1,0:T(8,128)(2,1)S(1)} %get-tuple-element.57), channel_id=1, source_target_pairs={{0,4},{4,0},{8,12},{12,8},{1,5},{5,1},{9,13},{13,9},{2,6},{6,2},{1... | collective-permute-start | bytes 589832 | tf_op jit(solution)/shard_map/ppermute | solution.py:68
  31.3 20.0 %collective-permute-start.7 = (bf16[2,2,64,384]{3,2,1,0:T(8,128)(2,1)S(1)}, bf16[2,2,64,384]{3,2,1,0:T(8,128)(2,1)S(1)}, u32[]{:S(2)}, u32[]{:S(2)}) collective-permute-start(bf16[2,2,64,384]{3,2,1,0:T(8,128)(2,1)S(1)} %get-tuple-element.58), channel_id=1, source_target_pairs={{0,8},{4,12},{8,0},{12,4},{1,9},{5,13},{9,1},{13,5},{2,10},{6,14},... | collective-permute-start | bytes 589832 | tf_op jit(solution)/shard_map/ppermute | solution.py:68
  34.2 17.0 %collective-permute-start.8 = (bf16[2,2,64,384]{3,2,1,0:T(8,128)(2,1)S(1)}, bf16[2,2,64,384]{3,2,1,0:T(8,128)(2,1)S(1)}, u32[]{:S(2)}, u32[]{:S(2)}) collective-permute-start(bf16[2,2,64,384]{3,2,1,0:T(8,128)(2,1)S(1)} %get-tuple-element.59), channel_id=1, source_target_pairs={{0,12},{4,8},{8,4},{12,0},{1,13},{5,9},{9,5},{13,1},{2,14},{6,10},... | collective-permute-start | bytes 589832 | tf_op jit(solution)/shard_map/ppermute | solution.py:68
  37.0 9.6 %collective-permute-start.11 = (bf16[96,384]{1,0:T(8,128)(2,1)S(1)}, bf16[96,384]{1,0:T(8,128)(2,1)S(1)}, u32[]{:S(2)}, u32[]{:S(2)}) collective-permute-start(bf16[96,384]{1,0:T(8,128)(2,1)S(1)} %get-tuple-element.67), channel_id=1, source_target_pairs={{0,4},{4,0},{8,12},{12,8},{1,5},{5,1},{9,13},{13,9},{2,6},{6,2},{1... | collective-permute-start | bytes 221192 | tf_op jit(solution)/shard_map/ppermute | solution.py:427
  39.0 8.6 %collective-permute-start.12 = (bf16[96,384]{1,0:T(8,128)(2,1)S(1)}, bf16[96,384]{1,0:T(8,128)(2,1)S(1)}, u32[]{:S(2)}, u32[]{:S(2)}) collective-permute-start(bf16[96,384]{1,0:T(8,128)(2,1)S(1)} %get-tuple-element.68), channel_id=1, source_target_pairs={{0,4},{4,0},{8,12},{12,8},{1,5},{5,1},{9,13},{13,9},{2,6},{6,2},{1... | collective-permute-start | bytes 221192 | tf_op jit(solution)/shard_map/ppermute | solution.py:427
  47.6 7.5 %collective-permute-start.13 = (bf16[96,384]{1,0:T(8,128)(2,1)S(1)}, bf16[96,384]{1,0:T(8,128)(2,1)S(1)}, u32[]{:S(2)}, u32[]{:S(2)}) collective-permute-start(bf16[96,384]{1,0:T(8,128)(2,1)S(1)} %get-tuple-element.70), channel_id=1, source_target_pairs={{0,8},{4,12},{8,0},{12,4},{1,9},{5,13},{9,1},{13,5},{2,10},{6,14},... | collective-permute-start | bytes 221192 | tf_op jit(solution)/shard_map/ppermute | solution.py:431

commit v7 on v5

--- a/solution.py
+++ b/solution.py
@@ -442,7 +442,7 @@
     pixels = height * width
     scale_factor = float(clips.shape[0] * frames * pixels * device_count) ** (-0.5)
     hid = w_expand.shape[1]
-    chunk = 256
+    chunk = 768
     blocks = channels // LANES
     count = members if members in (2, 4, 8) and height % members == 0 else 1
     all_frames = frames * members

time: 55.7 us -> 55.7 us (level)
  no operation moved by 1% of the time
where the time goes in v7:
time: 55.7 us; the launch traced here: 55.5 us
  starting transfers between devices  23.7 us (43%)
  waiting for transfers between devices  15.7 us (28%)
  Pallas kernels  15.3 us (27%)
  between operations  0.73 us (1%)
    pallas_call x11, Pallas kernels, call(): pl.pallas_call(kernel, out_shape=tuple(outs), in_specs=specs, out_specs=t...  15.3 us
    ppermute x6, starting transfers between devices, swap(): got.append(lax.ppermute(pieces[step], 'tm', pairs))  10.6 us
    ppermute x2, waiting for transfers between devices, scatter_grad(): lax.ppermute(send, 'tm', [(i, i ^ 1) for i in range(4)])  8.77 us
    ppermute x3, starting transfers between devices, exchange(): got.append(lax.ppermute(pieces[step], 'tm', pairs))  5.5 us
    ppermute x1, starting transfers between devices, scatter_grad(): got = lax.ppermute(send, 'tm', [(i, i ^ 2) for i in range(4)])  3.11 us
    ppermute x6, waiting for transfers between devices, swap(): got.append(lax.ppermute(pieces[step], 'tm', pairs))  2.68 us
    ppermute x1, waiting for transfers between devices, scatter_grad(): got = lax.ppermute(send, 'dp', [(i, i ^ 2) for i in range(4)])  2.59 us
    ppermute x2, starting transfers between devices, scatter_grad(): lax.ppermute(send, 'tm', [(i, i ^ 1) for i in range(4)])  2.44 us
  transfers between devices with their start and end apart: 14, of which 8 were waited for; matrix products, arithmetic and copies ran while one was open for 0% of the time, Pallas kernels for 19%

profile of v7, /device:TPU:0, one launch (start us, length us, event | category | flops | bytes accessed | tf_op | source)
XLA Modules:
  0.0 55.5 jit_solution(11054953297479768579)
XLA Ops:
  0.6 2.4 %shard_map.94 = (bf16[2,64,384]{2,1,0:T(8,128)(2,1)S(1)}, bf16[2,64,384]{2,1,0:T(8,128)(2,1)S(1)}, f32[3,2,8,48,128]{4,3,2,1,0:T(8,128)S(1)}, f32[7,7,384]{2,1,0:T(8,128)S(1)}) custom-call(bf16[1,2,8,32,384]{4,3,2,1,0:T(8,128)(2,1)} %refs_4_.1, f32[7,7,384]{2,1,0:T(8,128)} %refs_6_.1), custom_call_target="tpu_custom_call" | custom-call | tf_op jit(solution)/shard_map/pallas_call | solution.py:31
  3.0 3.9 %collective-permute-start.2 = (bf16[2,64,384]{2,1,0:T(8,128)(2,1)S(1)}, bf16[2,64,384]{2,1,0:T(8,128)(2,1)S(1)}, u32[]{:S(2)}, u32[]{:S(2)}) collective-permute-start(bf16[2,64,384]{2,1,0:T(8,128)(2,1)S(1)} %get-tuple-element.45), channel_id=1, source_target_pairs={{0,8},{4,12},{8,0},{12,4},{1,9},{5,13},{9,1},{13,5},{2,10},{6,14},... | collective-permute-start | bytes 294920 | tf_op jit(solution)/shard_map/ppermute | solution.py:68
  6.9 1.5 %collective-permute-start.3 = (bf16[2,64,384]{2,1,0:T(8,128)(2,1)S(1)}, bf16[2,64,384]{2,1,0:T(8,128)(2,1)S(1)}, u32[]{:S(2)}, u32[]{:S(2)}) collective-permute-start(bf16[2,64,384]{2,1,0:T(8,128)(2,1)S(1)} %get-tuple-element.46), channel_id=1, source_target_pairs={{0,12},{4,8},{8,4},{12,0},{1,13},{5,9},{9,5},{13,1},{2,14},{6,10},... | collective-permute-start | bytes 294920 | tf_op jit(solution)/shard_map/ppermute | solution.py:68
  8.5 0.0 copy-start.3
  8.5 1.9 %shard_map.95 = (bf16[2,64,384]{2,1,0:T(8,128)(2,1)S(1)}, bf16[2,64,384]{2,1,0:T(8,128)(2,1)S(1)}, bf16[2,2,32,384]{3,2,1,0:T(8,128)(2,1)S(1)}, bf16[2,2,32,384]...) custom-call(bf16[1,2,8,32,384]{4,3,2,1,0:T(8,128)(2,1)} %refs_5_.5, ...), custom_call_target="tpu_custom_call" | custom-call | tf_op jit(solution)/shard_map/pallas_call | solution.py:31
  10.4 0.1 collective-permute-start.1
  10.5 2.0 %collective-permute-start = (bf16[2,2,32,384]{3,2,1,0:T(8,128)(2,1)S(1)}, bf16[2,2,32,384]{3,2,1,0:T(8,128)(2,1)S(1)}, u32[]{:S(2)}, u32[]{:S(2)}) collective-permute-start(bf16[2,2,32,384]{3,2,1,0:T(8,128)(2,1)S(1)} %get-tuple-element.42), channel_id=1, source_target_pairs={{0,4},{4,8},{8,12},{12,0},{1,5},{5,9},{9,13},{13,1},{2,6},{6,10},{... | collective-permute-start | bytes 294920 | tf_op jit(solution)/shard_map/ppermute | solution.py:77
  12.5 1.5 %collective-permute-start.4 = (bf16[2,2,32,384]{3,2,1,0:T(8,128)(2,1)S(1)}, bf16[2,2,32,384]{3,2,1,0:T(8,128)(2,1)S(1)}, u32[]{:S(2)}, u32[]{:S(2)}) collective-permute-start(bf16[2,2,32,384]{3,2,1,0:T(8,128)(2,1)S(1)} %get-tuple-element.53), channel_id=1, source_target_pairs={{0,8},{4,12},{8,0},{12,4},{1,9},{5,13},{9,1},{13,5},{2,10},{6,14},... | collective-permute-start | bytes 294920 | tf_op jit(solution)/shard_map/ppermute | solution.py:77
  14.0 1.6 %collective-permute-done.2.refs_2_ = bf16[2,64,384]{2,1,0:T(8,128)(2,1)S(1)} collective-permute-done((bf16[2,64,384]{2,1,0:T(8,128)(2,1)S(1)}, bf16[2,64,384]{2,1,0:T(8,128)(2,1)S(1)}, u32[]{:S(2)}, u32[]{:S(2)}) %collective-permute-start.2) | collective-permute-done | bytes 98336 | tf_op jit(solution)/shard_map/ppermute | solution.py:68
  15.6 2.0 %collective-permute-start.5 = (bf16[2,2,32,384]{3,2,1,0:T(8,128)(2,1)S(1)}, bf16[2,2,32,384]{3,2,1,0:T(8,128)(2,1)S(1)}, u32[]{:S(2)}, u32[]{:S(2)}) collective-permute-start(bf16[2,2,32,384]{3,2,1,0:T(8,128)(2,1)S(1)} %get-tuple-element.54), channel_id=1, source_target_pairs={{0,12},{4,0},{8,4},{12,8},{1,13},{5,1},{9,5},{13,9},{2,14},{6,2},{... | collective-permute-start | bytes 294920 | tf_op jit(solution)/shard_map/ppermute | solution.py:77
  17.6 0.0 collective-permute-done.3.refs_3_
  17.6 1.1 %collective-permute-done.1.refs_1_ = bf16[2,64,384]{2,1,0:T(8,128)(2,1)S(1)} collective-permute-done((bf16[2,64,384]{2,1,0:T(8,128)(2,1)S(1)}, bf16[2,64,384]{2,1,0:T(8,128)(2,1)S(1)}, u32[]{:S(2)}, u32[]{:S(2)}) %collective-permute-start.1) | collective-permute-done | bytes 98336 | tf_op jit(solution)/shard_map/ppermute | solution.py:68
  18.7 0.0 copy-done.3
  18.7 2.8 %shard_map.96 = (bf16[8,64,384]{2,1,0:T(8,128)(2,1)S(1)}, bf16[512,384]{1,0:T(8,128)(2,1)S(1)}, bf16[512,1536]{1,0:T(8,128)(2,1)S(1)}, f32[512,384]{1,0:T(8,128)S(1)}, f32[512,1]{1,0:T(8,128)S(1)}) custom-call(bf16[2,64,384]{2,1,0:T(8,128)(2,1)S(1)} %get-tuple-element.43.refs_0_, bf16[2,64,384]{2,1,0:T(8,128)(2,1)S(1)} %collective-permute-done.1.refs_1_, ...), custom_call_target="tpu_custom_call" | custom-call | tf_op jit(solution)/shard_map/pallas_call | solution.py:31
  21.4 0.0 collective-permute-done.refs_1_
  21.5 1.0 %shard_map.97 = (bf16[256,1536]{1,0:T(8,128)(2,1)S(1)}, f32[16,96,384]{2,1,0:T(8,128)S(1)}) custom-call(bf16[2,2,32,384]{3,2,1,0:T(8,128)(2,1)S(1)} %get-tuple-element.41.refs_0_, bf16[2,2,32,384]{3,2,1,0:T(8,128)(2,1)S(1)} %collective-permute-done.refs_1_, bf16[512,1536]{1,0:T(8,128)(2,1)S(1)} %get-tuple-element.50.refs_2_, ...), custom_call_target="tpu_custom_call" | custom-call | tf_op jit(solution)/shard_map/pallas_call | solution.py:31
  22.5 0.6 %collective-permute-done.4.refs_0_ = bf16[2,2,32,384]{3,2,1,0:T(8,128)(2,1)S(1)} collective-permute-done((bf16[2,2,32,384]{3,2,1,0:T(8,128)(2,1)S(1)}, bf16[2,2,32,384]{3,2,1,0:T(8,128)(2,1)S(1)}, u32[]{:S(2)}, u32[]{:S(2)}) %collective-permute-start.4) | collective-permute-done | bytes 98336 | tf_op jit(solution)/shard_map/ppermute | solution.py:77
  23.1 0.0 collective-permute-done.5.refs_1_
  23.1 1.5 %shard_map.98 = (bf16[256,1536]{1,0:T(8,128)(2,1)S(1)}, f32[8,96,384]{2,1,0:T(8,128)S(1)}, bf16[8,96,384]{2,1,0:T(8,128)(2,1)S(1)}) custom-call(bf16[2,2,32,384]{3,2,1,0:T(8,128)(2,1)S(1)} %collective-permute-done.4.refs_0_, bf16[2,2,32,384]{3,2,1,0:T(8,128)(2,1)S(1)} %collective-permute-done.5.refs_1_, bf16[512,1536]{1,0:T(8,128)(2,1)S(1)} %get-tuple-element.50.refs_2_, ...), custom_call_target="tpu_custom_call" | custom-call | tf_op jit(solution)/shard_map/pallas_call | solution.py:31
  24.6 0.1 collective-permute-start.9
  24.7 1.9 %shard_map.99 = (bf16[2,2,64,384]{3,2,1,0:T(8,128)(2,1)S(1)}, bf16[2,2,64,384]{3,2,1,0:T(8,128)(2,1)S(1)}, bf16[2,2,64,384]{3,2,1,0:T(8,128)(2,1)S(1)}, bf16[2,2,64,384]{3,2,1,0:T(8,128)(2,1)S(1)}) custom-call(bf16[256,1536]{1,0:T(8,128)(2,1)S(1)} %get-tuple-element.52.refs_0_, bf16[256,1536]{1,0:T(8,128)(2,1)S(1)} %get-tuple-element.56.refs_1_, ...), custom_call_target="tpu_custom_call" | custom-call | tf_op jit(solution)/shard_map/pallas_call | solution.py:31
  26.6 0.1 collective-permute-done.9.refs_1_
  26.7 0.0 copy-start
  26.7 0.0 copy-start.1
  26.7 0.0 copy-start.2
  26.7 0.1 shard_map.101
  26.8 2.1 %collective-permute-start.10 = (bf16[4,96,384]{2,1,0:T(8,128)(2,1)S(1)}, bf16[4,96,384]{2,1,0:T(8,128)(2,1)S(1)}, u32[]{:S(2)}, u32[]{:S(2)}) collective-permute-start(bf16[4,96,384]{2,1,0:T(8,128)(2,1)S(1)} %get-tuple-element.69), channel_id=1, source_target_pairs={{0,2},{1,3},{2,0},{3,1},{4,6},{5,7},{6,4},{7,5},{8,10},{9,11},{10,... | collective-permute-start | bytes 884744 | tf_op jit(solution)/shard_map/ppermute | solution.py:425
  28.9 2.3 %collective-permute-start.6 = (bf16[2,2,64,384]{3,2,1,0:T(8,128)(2,1)S(1)}, bf16[2,2,64,384]{3,2,1,0:T(8,128)(2,1)S(1)}, u32[]{:S(2)}, u32[]{:S(2)}) collective-permute-start(bf16[2,2,64,384]{3,2,1,0:T(8,128)(2,1)S(1)} %get-tuple-element.61), channel_id=1, source_target_pairs={{0,4},{4,0},{8,12},{12,8},{1,5},{5,1},{9,13},{13,9},{2,6},{6,2},{1... | collective-permute-start | bytes 589832 | tf_op jit(solution)/shard_map/ppermute | solution.py:68
  31.2 2.7 %collective-permute-start.7 = (bf16[2,2,64,384]{3,2,1,0:T(8,128)(2,1)S(1)}, bf16[2,2,64,384]{3,2,1,0:T(8,128)(2,1)S(1)}, u32[]{:S(2)}, u32[]{:S(2)}) collective-permute-start(bf16[2,2,64,384]{3,2,1,0:T(8,128)(2,1)S(1)} %get-tuple-element.62), channel_id=1, source_target_pairs={{0,8},{4,12},{8,0},{12,4},{1,9},{5,13},{9,1},{13,5},{2,10},{6,14},... | collective-permute-start | bytes 589832 | tf_op jit(solution)/shard_map/ppermute | solution.py:68
  33.9 0.0 collective-permute-start.8
  33.9 2.6 %collective-permute-done.10.refs_1_ = bf16[4,96,384]{2,1,0:T(8,128)(2,1)S(1)} collective-permute-done((bf16[4,96,384]{2,1,0:T(8,128)(2,1)S(1)}, bf16[4,96,384]{2,1,0:T(8,128)(2,1)S(1)}, u32[]{:S(2)}, u32[]{:S(2)}) %collective-permute-start.10) | collective-permute-done | bytes 294944 | tf_op jit(solution)/shard_map/ppermute | solution.py:425
  36.5 0.1 shard_map.102
  36.5 2.4 %collective-permute-start.11 = (bf16[96,384]{1,0:T(8,128)(2,1)S(1)}, bf16[96,384]{1,0:T(8,128)(2,1)S(1)}, u32[]{:S(2)}, u32[]{:S(2)}) collective-permute-start(bf16[96,384]{1,0:T(8,128)(2,1)S(1)} %get-tuple-element.71), channel_id=1, source_target_pairs={{0,4},{4,0},{8,12},{12,8},{1,5},{5,1},{9,13},{13,9},{2,6},{6,2},{1... | collective-permute-start | bytes 221192 | tf_op jit(solution)/shard_map/ppermute | solution.py:430
  38.9 0.1 collective-permute-start.12
  39.0 7.6 %collective-permute-done.11.refs_1_ = bf16[96,384]{1,0:T(8,128)(2,1)S(1)} collective-permute-done((bf16[96,384]{1,0:T(8,128)(2,1)S(1)}, bf16[96,384]{1,0:T(8,128)(2,1)S(1)}, u32[]{:S(2)}, u32[]{:S(2)}) %collective-permute-start.11) | collective-permute-done | bytes 73760 | tf_op jit(solution)/shard_map/ppermute | solution.py:430
  46.5 1.2 %collective-permute-done.12.refs_2_ = bf16[96,384]{1,0:T(8,128)(2,1)S(1)} collective-permute-done((bf16[96,384]{1,0:T(8,128)(2,1)S(1)}, bf16[96,384]{1,0:T(8,128)(2,1)S(1)}, u32[]{:S(2)}, u32[]{:S(2)}) %collective-permute-start.12) | collective-permute-done | bytes 73760 | tf_op jit(solution)/shard_map/ppermute | solution.py:430
  47.8 3.1 %collective-permute-start.13 = (bf16[96,384]{1,0:T(8,128)(2,1)S(1)}, bf16[96,384]{1,0:T(8,128)(2,1)S(1)}, u32[]{:S(2)}, u32[]{:S(2)}) collective-permute-start(bf16[96,384]{1,0:T(8,128)(2,1)S(1)} %get-tuple-element.74), channel_id=1, source_target_pairs={{0,8},{4,12},{8,0},{12,4},{1,9},{5,13},{9,1},{13,5},{2,10},{6,14},... | collective-permute-start | bytes 221192 | tf_op jit(solution)/shard_map/ppermute | solution.py:434
  50.9 0.0 collective-permute-done.6.refs_1_
  50.9 0.0 collective-permute-done.7.refs_2_
  50.9 0.0 collective-permute-done.8.refs_3_
  50.9 0.0 copy-done
  50.9 0.0 copy-done.1
  50.9 0.0 copy-done.2
  50.9 2.9 %shard_map.100 = (bf16[1,2,8,32,384]{4,3,2,1,0:T(8,128)(2,1)}, bf16[1,2,8,32,384]{4,3,2,1,0:T(8,128)(2,1)}) custom-call(bf16[2,2,64,384]{3,2,1,0:T(8,128)(2,1)S(1)} %get-tuple-element.60.refs_0_.refs_2_, bf16[2,2,64,384]{3,2,1,0:T(8,128)(2,1)S(1)} %collective-permute-done.6.refs_1_, bf16[2,2,64,384]{3,2,1,0:T(8,128)(2,1)S(1)} %collective-permute-done.7.refs_2_, ...), custom_call_target="tpu_custom_call" | custom-call | tf_op jit(solution)/shard_map/pallas_call | solution.py:31
  53.9 0.9 %collective-permute-done.13.refs_1_ = bf16[96,384]{1,0:T(8,128)(2,1)S(1)} collective-permute-done((bf16[96,384]{1,0:T(8,128)(2,1)S(1)}, bf16[96,384]{1,0:T(8,128)(2,1)S(1)}, u32[]{:S(2)}, u32[]{:S(2)}) %collective-permute-start.13) | collective-permute-done | bytes 73760 | tf_op jit(solution)/shard_map/ppermute | solution.py:434
  54.8 0.7 %shard_map.104 = f32[96,384]{1,0:T(8,128)} custom-call(f32[96,384]{1,0:T(8,128)S(1)} %get-tuple-element.73.refs_0_, bf16[96,384]{1,0:T(8,128)(2,1)S(1)} %collective-permute-done.13.refs_1_), custom_call_target="tpu_custom_call" | custom-call | tf_op jit(solution)/shard_map/pallas_call | solution.py:31
  (1 shorter events, 0.0 us)
Async XLA Ops:
  3.0 12.6 %collective-permute-start.2 = (bf16[2,64,384]{2,1,0:T(8,128)(2,1)S(1)}, bf16[2,64,384]{2,1,0:T(8,128)(2,1)S(1)}, u32[]{:S(2)}, u32[]{:S(2)}) collective-permute-start(bf16[2,64,384]{2,1,0:T(8,128)(2,1)S(1)} %get-tuple-element.45), channel_id=1, source_target_pairs={{0,8},{4,12},{8,0},{12,4},{1,9},{5,13},{9,1},{13,5},{2,10},{6,14},... | collective-permute-start | bytes 294920 | tf_op jit(solution)/shard_map/ppermute | solution.py:68
  6.9 10.7 %collective-permute-start.3 = (bf16[2,64,384]{2,1,0:T(8,128)(2,1)S(1)}, bf16[2,64,384]{2,1,0:T(8,128)(2,1)S(1)}, u32[]{:S(2)}, u32[]{:S(2)}) collective-permute-start(bf16[2,64,384]{2,1,0:T(8,128)(2,1)S(1)} %get-tuple-element.46), channel_id=1, source_target_pairs={{0,12},{4,8},{8,4},{12,0},{1,13},{5,9},{9,5},{13,1},{2,14},{6,10},... | collective-permute-start | bytes 294920 | tf_op jit(solution)/shard_map/ppermute | solution.py:68
  8.5 10.2 %copy-start.3 = (f32[384]{0:T(512)S(1)}, f32[384]{0:T(512)}, u32[]{:S(2)}) copy-start(f32[384]{0:T(512)} %refs_5_.4) | copy-start | bytes 4612
  10.4 8.3 %collective-permute-start.1 = (bf16[2,64,384]{2,1,0:T(8,128)(2,1)S(1)}, bf16[2,64,384]{2,1,0:T(8,128)(2,1)S(1)}, u32[]{:S(2)}, u32[]{:S(2)}) collective-permute-start(bf16[2,64,384]{2,1,0:T(8,128)(2,1)S(1)} %get-tuple-element.44), channel_id=1, source_target_pairs={{0,4},{4,0},{8,12},{12,8},{1,5},{5,1},{9,13},{13,9},{2,6},{6,2},{1... | collective-permute-start | bytes 294920 | tf_op jit(solution)/shard_map/ppermute | solution.py:68
  10.5 11.0 %collective-permute-start = (bf16[2,2,32,384]{3,2,1,0:T(8,128)(2,1)S(1)}, bf16[2,2,32,384]{3,2,1,0:T(8,128)(2,1)S(1)}, u32[]{:S(2)}, u32[]{:S(2)}) collective-permute-start(bf16[2,2,32,384]{3,2,1,0:T(8,128)(2,1)S(1)} %get-tuple-element.42), channel_id=1, source_target_pairs={{0,4},{4,8},{8,12},{12,0},{1,5},{5,9},{9,13},{13,1},{2,6},{6,10},{... | collective-permute-start | bytes 294920 | tf_op jit(solution)/shard_map/ppermute | solution.py:77
  12.5 10.6 %collective-permute-start.4 = (bf16[2,2,32,384]{3,2,1,0:T(8,128)(2,1)S(1)}, bf16[2,2,32,384]{3,2,1,0:T(8,128)(2,1)S(1)}, u32[]{:S(2)}, u32[]{:S(2)}) collective-permute-start(bf16[2,2,32,384]{3,2,1,0:T(8,128)(2,1)S(1)} %get-tuple-element.53), channel_id=1, source_target_pairs={{0,8},{4,12},{8,0},{12,4},{1,9},{5,13},{9,1},{13,5},{2,10},{6,14},... | collective-permute-start | bytes 294920 | tf_op jit(solution)/shard_map/ppermute | solution.py:77
  15.6 7.5 %collective-permute-start.5 = (bf16[2,2,32,384]{3,2,1,0:T(8,128)(2,1)S(1)}, bf16[2,2,32,384]{3,2,1,0:T(8,128)(2,1)S(1)}, u32[]{:S(2)}, u32[]{:S(2)}) collective-permute-start(bf16[2,2,32,384]{3,2,1,0:T(8,128)(2,1)S(1)} %get-tuple-element.54), channel_id=1, source_target_pairs={{0,12},{4,0},{8,4},{12,8},{1,13},{5,1},{9,5},{13,9},{2,14},{6,2},{... | collective-permute-start | bytes 294920 | tf_op jit(solution)/shard_map/ppermute | solution.py:77
  24.6 2.1 %collective-permute-start.9 = (bf16[8,96,384]{2,1,0:T(8,128)(2,1)S(1)}, bf16[8,96,384]{2,1,0:T(8,128)(2,1)S(1)}, u32[]{:S(2)}, u32[]{:S(2)}) collective-permute-start(bf16[8,96,384]{2,1,0:T(8,128)(2,1)S(1)} %get-tuple-element.67), channel_id=1, source_target_pairs={{0,1},{1,0},{2,3},{3,2},{4,5},{5,4},{6,7},{7,6},{8,9},{9,8},{10,11... | collective-permute-start | bytes 1769480 | tf_op jit(solution)/shard_map/ppermute | solution.py:421
  26.7 24.2 %copy-start = (bf16[1,2,8,32,384]{4,3,2,1,0:T(8,128)(2,1)S(1)}, bf16[1,2,8,32,384]{4,3,2,1,0:T(8,128)(2,1)}, u32[]{:S(2)}) copy-start(bf16[1,2,8,32,384]{4,3,2,1,0:T(8,128)(2,1)} %refs_5_.5) | copy-start | bytes 1179652
  26.7 24.2 %copy-start.1 = (bf16[1,2,8,32,384]{4,3,2,1,0:T(8,128)(2,1)S(1)}, bf16[1,2,8,32,384]{4,3,2,1,0:T(8,128)(2,1)}, u32[]{:S(2)}) copy-start(bf16[1,2,8,32,384]{4,3,2,1,0:T(8,128)(2,1)} %refs_4_.1) | copy-start | bytes 1179652
  26.7 24.2 %copy-start.2 = (f32[7,7,384]{2,1,0:T(8,128)S(1)}, f32[7,7,384]{2,1,0:T(8,128)}, u32[]{:S(2)}) copy-start(f32[7,7,384]{2,1,0:T(8,128)} %refs_6_.1) | copy-start | bytes 225796
  26.8 9.7 %collective-permute-start.10 = (bf16[4,96,384]{2,1,0:T(8,128)(2,1)S(1)}, bf16[4,96,384]{2,1,0:T(8,128)(2,1)S(1)}, u32[]{:S(2)}, u32[]{:S(2)}) collective-permute-start(bf16[4,96,384]{2,1,0:T(8,128)(2,1)S(1)} %get-tuple-element.69), channel_id=1, source_target_pairs={{0,2},{1,3},{2,0},{3,1},{4,6},{5,7},{6,4},{7,5},{8,10},{9,11},{10,... | collective-permute-start | bytes 884744 | tf_op jit(solution)/shard_map/ppermute | solution.py:425
  28.9 22.0 %collective-permute-start.6 = (bf16[2,2,64,384]{3,2,1,0:T(8,128)(2,1)S(1)}, bf16[2,2,64,384]{3,2,1,0:T(8,128)(2,1)S(1)}, u32[]{:S(2)}, u32[]{:S(2)}) collective-permute-start(bf16[2,2,64,384]{3,2,1,0:T(8,128)(2,1)S(1)} %get-tuple-element.61), channel_id=1, source_target_pairs={{0,4},{4,0},{8,12},{12,8},{1,5},{5,1},{9,13},{13,9},{2,6},{6,2},{1... | collective-permute-start | bytes 589832 | tf_op jit(solution)/shard_map/ppermute | solution.py:68
  31.2 19.7 %collective-permute-start.7 = (bf16[2,2,64,384]{3,2,1,0:T(8,128)(2,1)S(1)}, bf16[2,2,64,384]{3,2,1,0:T(8,128)(2,1)S(1)}, u32[]{:S(2)}, u32[]{:S(2)}) collective-permute-start(bf16[2,2,64,384]{3,2,1,0:T(8,128)(2,1)S(1)} %get-tuple-element.62), channel_id=1, source_target_pairs={{0,8},{4,12},{8,0},{12,4},{1,9},{5,13},{9,1},{13,5},{2,10},{6,14},... | collective-permute-start | bytes 589832 | tf_op jit(solution)/shard_map/ppermute | solution.py:68
  33.9 17.0 %collective-permute-start.8 = (bf16[2,2,64,384]{3,2,1,0:T(8,128)(2,1)S(1)}, bf16[2,2,64,384]{3,2,1,0:T(8,128)(2,1)S(1)}, u32[]{:S(2)}, u32[]{:S(2)}) collective-permute-start(bf16[2,2,64,384]{3,2,1,0:T(8,128)(2,1)S(1)} %get-tuple-element.63), channel_id=1, source_target_pairs={{0,12},{4,8},{8,4},{12,0},{1,13},{5,9},{9,5},{13,1},{2,14},{6,10},... | collective-permute-start | bytes 589832 | tf_op jit(solution)/shard_map/ppermute | solution.py:68
  36.5 10.0 %collective-permute-start.11 = (bf16[96,384]{1,0:T(8,128)(2,1)S(1)}, bf16[96,384]{1,0:T(8,128)(2,1)S(1)}, u32[]{:S(2)}, u32[]{:S(2)}) collective-permute-start(bf16[96,384]{1,0:T(8,128)(2,1)S(1)} %get-tuple-element.71), channel_id=1, source_target_pairs={{0,4},{4,0},{8,12},{12,8},{1,5},{5,1},{9,13},{13,9},{2,6},{6,2},{1... | collective-permute-start | bytes 221192 | tf_op jit(solution)/shard_map/ppermute | solution.py:430
  38.9 8.8 %collective-permute-start.12 = (bf16[96,384]{1,0:T(8,128)(2,1)S(1)}, bf16[96,384]{1,0:T(8,128)(2,1)S(1)}, u32[]{:S(2)}, u32[]{:S(2)}) collective-permute-start(bf16[96,384]{1,0:T(8,128)(2,1)S(1)} %get-tuple-element.72), channel_id=1, source_target_pairs={{0,4},{4,0},{8,12},{12,8},{1,5},{5,1},{9,13},{13,9},{2,6},{6,2},{1... | collective-permute-start | bytes 221192 | tf_op jit(solution)/shard_map/ppermute | solution.py:430
  47.8 7.0 %collective-permute-start.13 = (bf16[96,384]{1,0:T(8,128)(2,1)S(1)}, bf16[96,384]{1,0:T(8,128)(2,1)S(1)}, u32[]{:S(2)}, u32[]{:S(2)}) collective-permute-start(bf16[96,384]{1,0:T(8,128)(2,1)S(1)} %get-tuple-element.74), channel_id=1, source_target_pairs={{0,8},{4,12},{8,0},{12,4},{1,9},{5,13},{9,1},{13,5},{2,10},{6,14},... | collective-permute-start | bytes 221192 | tf_op jit(solution)/shard_map/ppermute | solution.py:434
